TPU v7x, 256 devices: a whole 4x4x8 slice. The times are simulated.
256 devices in a mesh: row: 8 (over z), col: 32 (over x, y, core).
Axes of the slice: x: 4, y: 4, z: 8, core: 2. Of those that a mesh axis runs over, the one named last changes fastest.
Arguments:
- a_values: bfloat16 [12288, 4096], P('row', 'col'), may hold values from 0 to 0.029907227
- b_values: bfloat16 [4096, 32768], P('col'), may hold values from 0 to 0.029907227
- a_pattern: int32 [96, 32], P('row', 'col'), may hold values 0 or 1
- b_pattern: int32 [32, 256], P('col'), may hold values 0 or 1
- c_pattern: int32 [96, 256], P('row', 'col'), may hold values 0 or 1
Outputs:
- rescaled: bfloat16 [12288, 32768], P('row', 'col')
All inputs are finite; a program needn't handle non-finite values. No bound on the sum of `a_pattern` or of `b_pattern` or of `c_pattern` on one device may be relied on, other than what follows from the above.
Results may differ from a plain program's by a relative error of at most 0.001.
Values may be sent and summed in bfloat16 or wider, within the bound.
No kernel may reach another device: no remote copies, remote signals or barrier semaphores. Data moves between devices by JAX's collectives and lax.ppermute only.
A program may use at most 128 MiB of HBM per device.

v0:
```python
import jax
import jax.numpy as jnp
from jax import lax
from jax.sharding import PartitionSpec as P

BLOCK = 128


def expand_mask(values, pattern):
    row_count, col_count = pattern.shape
    shaped = values.reshape(row_count, BLOCK, col_count, BLOCK)
    masked = shaped * pattern.astype(values.dtype)[:, None, :, None]
    return masked.reshape(row_count * BLOCK, col_count * BLOCK)


def shards(a_values, b_values, a_pattern, b_pattern, c_pattern):
    left = expand_mask(a_values, a_pattern)
    right = expand_mask(b_values, b_pattern)
    row_total = left.shape[0]
    gathered = lax.all_to_all(right, "col", split_axis=1, concat_axis=0, tiled=True)
    expanded = jnp.dot(
        lax.all_gather(left, "col", axis=1, tiled=True),
        gathered,
        preferred_element_type=jnp.float32,
    )
    expanded = expand_mask(expanded, c_pattern)
    inflated = expanded * expanded
    column_total = lax.psum(jnp.sum(inflated, axis=0), "row")
    total_rows = row_total * lax.axis_size("row")
    return (inflated * (total_rows / (column_total + 1e-06))[None, :]).astype(jnp.bfloat16)


def solution(mesh):
    return jax.shard_map(
        shards,
        mesh=mesh,
        in_specs=(
            P("row", "col"),
            P("col", None),
            P("row", "col"),
            P("col", None),
            P("row", "col"),
        ),
        out_specs=P("row", "col"),
        check_vma=False,
    )
```

profile of v0, /device:TPU:8, one launch (start us, length us, event | category | flops | bytes accessed | tf_op | source)
XLA Modules:
  0.0 252.0 jit_solution(18236468836315410632)
XLA Ops:
  6.5 0.0 all-gather.2.cloned.1.call-start
  6.5 0.7 convert_bitcast_fusion
  7.2 0.1 broadcast_bitcast_fusion.1
  7.3 2.0 broadcast_multiply_fusion.1
  9.3 0.0 all-gather.2.cloned.1.call-update
  9.3 0.0 copy-start.1
  9.3 11.9 %copy.14 = bf16[128,32768]{0,1:T(8,128)(2,1)} copy(bf16[128,32768]{1,0:T(8,128)(2,1)} %param.6) | data formatting | bytes 16777216 | tf_op args[1]
  21.2 0.0 copy-done.1
  21.3 0.1 broadcast_bitcast_fusion
  21.4 8.7 %broadcast_multiply_fusion = bf16[128,32768]{0,1:T(8,128)(2,1)} fusion(bf16[128,32768]{0,1:T(8,128)(2,1)} %copy.14, bf16[32768]{0:T(1024)(128)(2,1)S(1)} %broadcast_bitcast_fusion), kind=kLoop, calls=%fused_computation.3 | loop fusion | flops 4194304 | bytes 16842752 | tf_op jit(solution)/shard_map/mul | solution.py:12
  30.0 11.9 %copy.15 = bf16[128,32,1024]{2,0,1:T(8,128)(2,1)} copy(bf16[128,32,1024]{0,2,1:T(8,128)(2,1)} %bitcast.29) | data formatting | bytes 16777216 | tf_op jit(solution)/shard_map/all_to_all | solution.py:20
  42.0 0.0 copy-start
  42.0 7.7 %all-to-all-start = ((bf16[128,32,1024]{2,0,1:T(8,128)(2,1)}), bf16[128,32,1024]{2,0,1:T(8,128)(2,1)}, u32[]{:S(2)}, u32[]{:S(2)}) async-start(bf16[128,32,1024]{2,0,1:T(8,128)(2,1)} %copy.15), calls=%async_computation | async-start | bytes 16777216 | tf_op jit(solution)/shard_map/all_to_all | solution.py:20
  49.7 0.0 copy-done
  49.7 0.1 copy.17
  49.8 130.5 %all-to-all-done = bf16[128,32,1024]{2,0,1:T(8,128)(2,1)} async-done(((bf16[128,32,1024]{2,0,1:T(8,128)(2,1)}), bf16[128,32,1024]{2,0,1:T(8,128)(2,1)}, u32[]{:S(2)}, u32[]{:S(2)}) %all-to-all-start) | async-done | bytes 8388640 | tf_op jit(solution)/shard_map/all_to_all | solution.py:20
  180.3 11.3 %copy.16 = bf16[4096,1024]{0,1:T(8,128)(2,1)} copy(bf16[4096,1024]{1,0:T(8,128)(2,1)} %bitcast.8) | data formatting | bytes 16777216 | tf_op jit(solution)/shard_map/all_to_all | solution.py:20
  191.6 0.0 all-gather.2.cloned.1.call-done
  191.6 18.5 %fusion.1 = (f32[8,128]{1,0:T(8,128)S(1)}, f32[12,128,8,128]{3,1,2,0:T(8,128)S(1)}) fusion(f32[12,8]{1,0:T(8,128)S(1)} %copy.17, bf16[12,128,4096,1]{2,1,3,0:T(8,128)(2,1)} %bitcast.33, bf16[8,128,4096,1]{2,1,0,3:T(8,128)(2,1)} %bitcast.31), kind=kOutput, calls=%fused_computation.10 | convolution fusion | flops 12889619456 | bytes 27267456 | tf_op jit(solution)/shard_map/dot_general | solution.py:21
  210.1 7.0 %copy.18 = f32[12,128,8,128]{3,2,1,0:T(8,128)} copy(f32[12,128,8,128]{3,1,2,0:T(8,128)S(1)} %get-tuple-element.6) | data formatting | bytes 12582912 | tf_op jit(solution)/shard_map/mul | solution.py:27
  217.1 22.4 %psum.7 = f32[1024]{0:T(1024)S(1)} all-reduce(f32[1024]{0:T(1024)S(1)} %bitcast.32), channel_id=1, replica_groups=mesh['row'=8,'col'=32] {'row'}, use_global_device_ids=true, to_apply=%region_1.0 | all-reduce | flops 1024 | bytes 8192 | tf_op jit(solution)/shard_map/psum | solution.py:28
  239.5 5.7 %fusion = bf16[1536,1024]{1,0:T(8,128)(2,1)} fusion(f32[192,8,8,128]{3,2,1,0:T(8,128)} %bitcast.30, f32[1024]{0:T(1024)S(1)} %add_divide_fusion), kind=kLoop, calls=%fused_computation.1 | loop fusion | flops 3145728 | bytes 9441280 | tf_op jit(solution)/shard_map/convert_element_type | solution.py:30
  (3 shorter events, 0.0 us)
Async XLA Ops:
  6.5 185.1 %all-gather.2.cloned.1.call-start = ((), (), s32[]{:S(2)}) async-start(), calls=%async_computation.1 | async-start | bytes 12976128 | tf_op jit(solution)/shard_map/all_gather | solution.py:22
  9.3 11.9 %copy-start.1 = (s32[1,256]{1,0:T(1,128)S(1)}, s32[1,256]{1,0:T(1,128)}, u32[]{:S(2)}) copy-start(s32[1,256]{1,0:T(1,128)} %param.8) | copy-start | bytes 3076
  42.0 7.7 %copy-start = (s32[12,8]{0,1:T(8,128)S(1)}, s32[12,8]{0,1:T(8,128)}, u32[]{:S(2)}) copy-start(s32[12,8]{0,1:T(8,128)} %param.9) | copy-start | bytes 1156
  42.0 138.3 %all-to-all-start = ((bf16[128,32,1024]{2,0,1:T(8,128)(2,1)}), bf16[128,32,1024]{2,0,1:T(8,128)(2,1)}, u32[]{:S(2)}, u32[]{:S(2)}) async-start(bf16[128,32,1024]{2,0,1:T(8,128)(2,1)} %copy.15), calls=%async_computation | async-start | bytes 16777216 | tf_op jit(solution)/shard_map/all_to_all | solution.py:20
Sparse Core Ops, SparseCore 0:
  9.8 166.9 all-gather.1
where the time goes:
time: 253 us; the launch traced here: 252 us
  waiting for transfers between devices  131 us (52%)
  local copies, waits for them, and re-layouts  42.4 us (17%)
  blocking collectives  22.4 us (9%)
  matrix products  18.5 us (7%)
  other arithmetic  17.1 us (7%)
  between operations  13.4 us (5%)
  starting transfers between devices  7.69 us (3%)
    all_to_all x1, waiting for transfers between devices, shards(): lax.all_to_all(right, 'col', split_axis=1, concat_axis=0, tiled=True)  131 us
    all_to_all x2, local copies, waits for them, and re-layouts, shards(): lax.all_to_all(right, 'col', split_axis=1, concat_axis=0, tiled=True)  23.2 us
    psum x1, blocking collectives, shards(): column_total = lax.psum(jnp.sum(inflated, axis=0), 'row')  22.4 us
    dot_general x1, matrix products, shards(): jnp.dot(lax.all_gather(left, 'col', axis=1, tiled=True), gathered, prefer...  18.5 us
    unnamed x5, local copies, waits for them, and re-layouts  11.9 us
    mul x3, other arithmetic, expand_mask(): masked = shaped * pattern.astype(values.dtype)[:, None, :, None]  11.3 us
    all_to_all x1, starting transfers between devices, shards(): lax.all_to_all(right, 'col', split_axis=1, concat_axis=0, tiled=True)  7.69 us
    mul x1, local copies, waits for them, and re-layouts, shards(): inflated = expanded * expanded  7.01 us
  transfers between devices with their start and end apart: 2, of which 1 were waited for; matrix products, arithmetic and copies ran while one was open for 17% of the time, Pallas kernels for 0%

commit v1 on v0

v1 whole, which is shorter than its diff:
```python
import functools

import jax
import jax.numpy as jnp
from jax import lax
from jax.experimental import pallas as pl
from jax.experimental.pallas import tpu as pltpu
from jax.sharding import PartitionSpec as P

BLOCK = 128
XS, YS, CORES = 4, 4, 2
COLS = XS * YS * CORES
ROWS = 8
EPS = 1e-06
F32 = jnp.float32
BF16 = jnp.bfloat16

OFFSETS = (0, -1, 1, 2)
NEAR = ((0, 0), (0, 1), (0, 2), (1, 0), (2, 0))
FAR = tuple((d, e) for d in range(4) for e in range(4) if (d, e) not in NEAR)
PAIRS = ((-1, 1), (-2, 2), (-3, 3), (0, 4))
TILE = 512


def flat(x, y, c):
    return ((x % XS) * YS + y % YS) * CORES + c


def place(x, y, c, first, second):
    if isinstance(c, int):
        return flat(x + first, y + second, c) if c == 0 else flat(x + second, y + first, c)
    dx = jnp.where(c == 0, first, second)
    dy = jnp.where(c == 0, second, first)
    return flat(x + dx + XS, y + dy + YS, c)


def shift(value, first, second):
    pairs = []
    for x in range(XS):
        for y in range(YS):
            for c in range(CORES):
                pairs.append((flat(x, y, c), place(x, y, c, first, second)))
    return lax.ppermute(value, "col", pairs)


def swap(value):
    return lax.ppermute(value, "col", [(i, i ^ 1) for i in range(COLS)])


def along(value, step):
    return lax.ppermute(value, "row", [(i, (i + step) % ROWS) for i in range(ROWS)])


def after(values, others):
    held, _ = lax.optimization_barrier((values, others))
    return held


def smem():
    return pl.BlockSpec(memory_space=pltpu.SMEM)


def vmem():
    return pl.BlockSpec(memory_space=pltpu.VMEM)


def any_space():
    return pl.BlockSpec(memory_space=pl.ANY)


def params():
    return pltpu.CompilerParams(vmem_limit_bytes=56 * 1024 * 1024)


def mask_left_kernel(pattern_ref, a_ref, o_ref):
    for i in range(a_ref.shape[0] // BLOCK):
        rows = slice(i * BLOCK, (i + 1) * BLOCK)
        block = a_ref[rows, :]
        o_ref[rows, :] = jnp.where(pattern_ref[i, 0] != 0, block, jnp.zeros_like(block))


def mask_left(a, pattern):
    return pl.pallas_call(
        mask_left_kernel,
        out_shape=jax.ShapeDtypeStruct(a.shape, a.dtype),
        in_specs=[smem(), vmem()],
        out_specs=vmem(),
        compiler_params=params(),
        cost_estimate=pl.CostEstimate(flops=a.size, bytes_accessed=4 * a.size, transcendentals=0),
    )(pattern, a)


def spread_kernel(row_ref, pattern_ref, b_ref, o_ref, held, sems):
    row = row_ref[0]
    count = o_ref.shape[0]

    def copy(j):
        columns = pl.ds(pl.multiple_of((j * ROWS + row) * BLOCK, BLOCK), BLOCK)
        return pltpu.make_async_copy(b_ref.at[:, columns], held.at[j], sems.at[j])

    for j in range(count):
        copy(j).start()
    for j in range(count):
        copy(j).wait()
        block = held[j]
        o_ref[j] = jnp.where(pattern_ref[0, j * ROWS + row] != 0, block, jnp.zeros_like(block))


def spread(b, pattern, row):
    shape = (COLS, b.shape[0], BLOCK)
    return pl.pallas_call(
        spread_kernel,
        out_shape=jax.ShapeDtypeStruct(shape, b.dtype),
        in_specs=[smem(), smem(), any_space()],
        out_specs=vmem(),
        scratch_shapes=[pltpu.VMEM(shape, b.dtype), pltpu.SemaphoreType.DMA((COLS,))],
        compiler_params=params(),
        cost_estimate=pl.CostEstimate(flops=1 << 20, bytes_accessed=1 << 21, transcendentals=0),
    )(row, pattern, b)


def pieces_kernel(where_ref, pattern_ref, b_ref, *rest):
    outs, held, sems = rest[:5], rest[5], rest[6]
    width = outs[0].shape[2]
    blocks = width // BLOCK

    def copy(k):
        columns = pl.ds(pl.multiple_of(where_ref[k] * width, width), width)
        return pltpu.make_async_copy(b_ref.at[:, columns], held.at[k], sems.at[k])

    for k in range(10):
        copy(k).start()
    for k in range(10):
        copy(k).wait()
        for i in range(blocks):
            columns = slice(i * BLOCK, (i + 1) * BLOCK)
            block = held[k, :, columns]
            keep = pattern_ref[0, where_ref[k] * blocks + i] != 0
            outs[k // 2][k % 2, :, columns] = jnp.where(keep, block, jnp.zeros_like(block))


def pieces(b, pattern, where):
    width = b.shape[1] // COLS
    shape = (2, b.shape[0], width)
    return pl.pallas_call(
        pieces_kernel,
        out_shape=[jax.ShapeDtypeStruct(shape, b.dtype)] * 5,
        in_specs=[smem(), smem(), any_space()],
        out_specs=[vmem()] * 5,
        scratch_shapes=[pltpu.VMEM((10, b.shape[0], width), b.dtype), pltpu.SemaphoreType.DMA((10,))],
        compiler_params=params(),
        cost_estimate=pl.CostEstimate(flops=3 << 20, bytes_accessed=6 << 20, transcendentals=0),
    )(where, pattern, b)


def select_kernel(index_ref, r_ref, o_ref, sem):
    for j in range(o_ref.shape[0]):
        pltpu.make_async_copy(r_ref.at[index_ref[j]], o_ref.at[j], sem.at[j]).start()
    for j in range(o_ref.shape[0]):
        pltpu.make_async_copy(r_ref.at[index_ref[j]], o_ref.at[j], sem.at[j]).wait()


def select(received, index):
    count = index.shape[0]
    return pl.pallas_call(
        select_kernel,
        out_shape=jax.ShapeDtypeStruct((count,) + received.shape[1:], received.dtype),
        in_specs=[smem(), any_space()],
        out_specs=any_space(),
        scratch_shapes=[pltpu.SemaphoreType.DMA((count,))],
        compiler_params=params(),
        cost_estimate=pl.CostEstimate(flops=0, bytes_accessed=2 << 20, transcendentals=0),
    )(index, received)


def product_kernel(far_counts, last, blk_ref, cpat_ref, *refs):
    refs = list(refs)
    lefts = [refs.pop(0) for _ in range(8)]
    nears = [[refs.pop(0) for _ in range(6)] for _ in range(2)]
    fars = [[refs.pop(0) for _ in range(n)] for n in far_counts]
    earlier = [refs.pop(0) for _ in range(3)] if last else []
    o_ref, t_ref = refs.pop(0), refs.pop(0)
    right = refs.pop(0)
    step = pl.program_id(0)

    @pl.when(step == 0)
    def _():
        for n in range(2):
            lanes = slice(n * BLOCK, (n + 1) * BLOCK)
            for o in range(2):
                for k, (d, e) in enumerate(NEAR):
                    slot = (o * 4 + d) * 4 + e
                    block = nears[n][k][...] if o == 0 else nears[n][5][k]
                    right[slot * BLOCK:(slot + 1) * BLOCK, lanes] = block
                for k, (d, e) in enumerate(FAR):
                    slot = (o * 4 + d) * 4 + e
                    if len(fars[n]) == 1:
                        block = fars[n][0][o * len(FAR) + k]
                    else:
                        block = fars[n][o][k]
                    right[slot * BLOCK:(slot + 1) * BLOCK, lanes] = block

    left = jnp.concatenate([ref[e] for ref in lefts for e in range(4)], axis=1)
    product = jnp.dot(left, right[...], preferred_element_type=F32)
    blocks = TILE // BLOCK
    sums = [jnp.zeros((1, BLOCK), F32) for _ in range(2)]
    for n in range(2):
        lanes = slice(n * BLOCK, (n + 1) * BLOCK)
        for i in range(blocks):
            rows = slice(i * BLOCK, (i + 1) * BLOCK)
            keep = cpat_ref[step * blocks + i, blk_ref[n]] != 0
            block = product[rows, lanes]
            block = jnp.where(keep, block * block, jnp.zeros_like(block))
            o_ref[rows, lanes] = block
            sums[n] = sums[n] + jnp.sum(block, axis=0, keepdims=True)

    if not last:
        @pl.when(step == 0)
        def _():
            t_ref[...] = jnp.zeros_like(t_ref)

        for n in range(2):
            t_ref[n:n + 1, :] += sums[n]
    else:
        total = refs.pop(0)

        @pl.when(step == 0)
        def _():
            total[...] = jnp.zeros_like(total)

        for n in range(2):
            total[n:n + 1, :] += sums[n]

        @pl.when(step == pl.num_programs(0) - 1)
        def _():
            for k in range(ROWS):
                source = earlier[k // 2] if k < 6 else total
                n = k % 2
                where = blk_ref[2 + k]
                for r in range(ROWS):
                    t_ref[r, pl.ds(where, 1), :] = source[n:n + 1, :]


def product(blk, cpat, lefts, near, nears, fars, earlier=None, everywhere=None):
    last = earlier is not None
    rows = lefts[0].shape[1]
    scalars = blk if not last else jnp.concatenate([blk, everywhere])
    in_specs = [pl.BlockSpec((4, TILE, BLOCK), lambda i, *_: (0, i, 0)) for _ in lefts]
    operands = list(lefts)
    for n in range(2):
        for array in nears:
            in_specs.append(pl.BlockSpec((None, BLOCK, BLOCK), lambda i, s, _, n=n: (0, 0, s[n])))
            operands.append(array)
        in_specs.append(pl.BlockSpec((5, BLOCK, BLOCK), lambda i, s, _, n=n: (0, 0, s[n])))
        operands.append(near)
    for group in fars:
        for array in group:
            in_specs.append(pl.BlockSpec(array.shape, lambda i, *_: (0, 0, 0)))
            operands.append(array)
    out_shape = [jax.ShapeDtypeStruct((rows, 2 * BLOCK), F32)]
    out_specs = [pl.BlockSpec((TILE, 2 * BLOCK), lambda i, *_: (i, 0))]
    scratch = [pltpu.VMEM((COLS * BLOCK, 2 * BLOCK), BF16)]
    if last:
        for array in earlier:
            in_specs.append(pl.BlockSpec(array.shape, lambda i, *_: (0, 0)))
            operands.append(array)
        out_shape.append(jax.ShapeDtypeStruct((ROWS, ROWS, BLOCK), F32))
        out_specs.append(pl.BlockSpec((ROWS, ROWS, BLOCK), lambda i, *_: (0, 0, 0)))
        scratch.append(pltpu.VMEM((2, BLOCK), F32))
    else:
        out_shape.append(jax.ShapeDtypeStruct((2, BLOCK), F32))
        out_specs.append(pl.BlockSpec((2, BLOCK), lambda i, *_: (0, 0)))
    return pl.pallas_call(
        functools.partial(product_kernel, tuple(len(g) for g in fars), last),
        out_shape=out_shape,
        grid_spec=pltpu.PrefetchScalarGridSpec(
            num_scalar_prefetch=2,
            grid=(rows // TILE,),
            in_specs=in_specs,
            out_specs=out_specs,
            scratch_shapes=scratch,
        ),
        compiler_params=params(),
        cost_estimate=pl.CostEstimate(
            flops=2 * rows * COLS * BLOCK * 2 * BLOCK, bytes_accessed=16 << 20, transcendentals=0
        ),
    )(scalars, cpat, *operands)


def rescale_kernel(count, blk_ref, t_ref, i0, i1, i2, i3, o_ref, scale):
    total = t_ref[0]
    for r in range(1, ROWS):
        total = total + t_ref[r]
    scale[...] = count / (total + EPS)
    for k, ref in enumerate((i0, i1, i2, i3)):
        for n in range(2):
            where = blk_ref[2 * k + n]
            lanes = pl.ds(pl.multiple_of(where * BLOCK, BLOCK), BLOCK)
            factor = scale[pl.ds(where, 1), :]
            o_ref[:, lanes] = (ref[:, n * BLOCK:(n + 1) * BLOCK] * factor).astype(BF16)


def rescale(everywhere, totals, inflated):
    rows = inflated[0].shape[0]
    return pl.pallas_call(
        functools.partial(rescale_kernel, float(rows * ROWS)),
        out_shape=jax.ShapeDtypeStruct((rows, ROWS * BLOCK), BF16),
        grid_spec=pltpu.PrefetchScalarGridSpec(
            num_scalar_prefetch=1,
            grid=(rows // TILE,),
            in_specs=[pl.BlockSpec(totals.shape, lambda i, *_: (0, 0, 0))]
            + [pl.BlockSpec((TILE, 2 * BLOCK), lambda i, *_: (i, 0))] * 4,
            out_specs=pl.BlockSpec((TILE, ROWS * BLOCK), lambda i, *_: (i, 0)),
            scratch_shapes=[pltpu.VMEM((ROWS, BLOCK), F32)],
        ),
        compiler_params=params(),
        cost_estimate=pl.CostEstimate(flops=rows * 2048, bytes_accessed=10 << 20, transcendentals=0),
    )(everywhere, totals, *inflated)


def shards(a_values, b_values, a_pattern, b_pattern, c_pattern):
    col = lax.axis_index("col").astype(jnp.int32)
    row = lax.axis_index("row").astype(jnp.int32)
    x, y, c = col // (YS * CORES), (col // CORES) % YS, col % CORES

    sent = spread(b_values, b_pattern, row[None])
    received = lax.all_to_all(sent, "col", split_axis=0, concat_axis=0, tiled=True)

    left = mask_left(a_values, a_pattern)[None]
    line = [left] + [shift(left, s, 0) for s in (1, -1, 2)]

    index = []
    for core in (c, 1 - c):
        for d, e in FAR:
            index.append(place(x, y, core, OFFSETS[e], OFFSETS[d]))
    own = select(received, jnp.stack(index))

    up, down = [own], [own]
    for _ in range(3):
        up.append(along(up[-1], 1))
        down.append(along(down[-1], -1))
    half = len(FAR)
    opposite = [along(up[-1][:half], 1), along(down[-1][half:], -1)]

    line = jnp.concatenate(line, axis=0)
    lefts = [line] + [shift(line, 0, s) for s in (1, -1, 2)]
    lefts = lefts + [swap(g) for g in lefts]

    where = []
    for first, second in ((0, 0), (1, 0), (-1, 0), (0, 1), (0, -1)):
        there = place(x, y, c, first, second)
        where += [there, there ^ 1]
    near = pieces(after(b_values, own), b_pattern, jnp.stack(where))
    nears = [near[0], shift(near[1], 1, 0), shift(near[2], -1, 0), shift(near[3], 0, 1), shift(near[4], 0, -1)]
    other = swap(jnp.stack([piece[1] for piece in nears]))

    blocks = [[(row + ROWS + k) % ROWS for k in pair] for pair in PAIRS]
    everywhere = jnp.stack([b for pair in blocks for b in pair])
    inflated, totals = [], []
    for k in range(3):
        out, total = product(jnp.stack(blocks[k]), c_pattern, lefts, other, nears, [[up[k + 1]], [down[k + 1]]])
        inflated.append(out)
        totals.append(total)
    out, total = product(
        jnp.stack(blocks[3]), c_pattern, lefts, other, nears, [[own], opposite], totals, everywhere
    )
    inflated.append(out)
    gathered = lax.all_to_all(total, "row", split_axis=0, concat_axis=0, tiled=True)
    return rescale(everywhere, gathered, inflated)


def solution(mesh):
    return jax.shard_map(
        shards,
        mesh=mesh,
        in_specs=(
            P("row", "col"),
            P("col", None),
            P("row", "col"),
            P("col", None),
            P("row", "col"),
        ),
        out_specs=P("row", "col"),
        check_vma=False,
    )
```

time: 253 us -> 211 us (0.83)
  the two profiles are of different devices: /device:TPU:8 before, /device:TPU:2 now
where the time goes in v1:
time: 211 us; the launch traced here: 210 us
  Pallas kernels  78.7 us (37%)
  waiting for transfers between devices  65.4 us (31%)
  starting transfers between devices  51.3 us (24%)
  local copies, waits for them, and re-layouts  12 us (6%)
    ppermute x10, waiting for transfers between devices, shift(): return lax.ppermute(value, 'col', pairs)  39.8 us
    pallas_call x4, Pallas kernels, product(): pl.pallas_call(functools.partial(product_kernel, tuple((len(g) for g in f...  39.4 us
    pallas_call x1, Pallas kernels, select(): pl.pallas_call(select_kernel, out_shape=jax.ShapeDtypeStruct((count,) + r...  23.8 us
    ppermute x8, starting transfers between devices, along(): lax.ppermute(value, 'row', [(i, (i + step) % ROWS) for i in range(ROWS)])  18.8 us
    ppermute x10, starting transfers between devices, shift(): return lax.ppermute(value, 'col', pairs)  13.6 us
    ppermute x8, waiting for transfers between devices, along(): lax.ppermute(value, 'row', [(i, (i + step) % ROWS) for i in range(ROWS)])  11.5 us
    all_to_all x1, starting transfers between devices, shards(): lax.all_to_all(total, 'row', split_axis=0, concat_axis=0, tiled=True)  10.1 us
    all_to_all x1, starting transfers between devices, shards(): lax.all_to_all(sent, 'col', split_axis=0, concat_axis=0, tiled=True)  7.64 us
  transfers between devices with their start and end apart: 25, of which 6 were waited for; matrix products, arithmetic and copies ran while one was open for 6% of the time, Pallas kernels for 28%

profile of v1, /device:TPU:2, one launch (start us, length us, event | category | flops | bytes accessed | tf_op | source)
XLA Modules:
  0.0 209.8 jit_solution(10959035314717105857)
XLA Ops:
  0.0 3.1 %shard_map.56 = bf16[32,128,128]{2,1,0:T(8,128)(2,1)} custom-call(s32[1]{0:T(128)} %bitcast.41.row_ref, s32[1,256]{1,0:T(1,128)} %pattern_ref.4, bf16[128,32768]{1,0:T(8,128)(2,1)} %b_ref.2), custom_call_target="tpu_custom_call" | custom-call | flops 1048576 | bytes 2097152 | tf_op jit(solution)/shard_map/pallas_call | solution.py:111
  3.2 7.6 %all-to-all-start = ((bf16[32,128,128]{2,1,0:T(8,128)(2,1)}), bf16[32,128,128]{2,1,0:T(8,128)(2,1)S(1)}, u32[]{:S(2)}, u32[]{:S(2)}) async-start(bf16[32,128,128]{2,1,0:T(8,128)(2,1)} %shard_map.56), calls=%async_computation | async-start | bytes 2097152 | tf_op jit(solution)/shard_map/all_to_all | solution.py:327
  10.8 0.7 copy.6.pattern_ref
  11.5 1.9 shard_map.55
  13.4 2.1 %collective-permute-start.2 = (bf16[1,1536,128]{2,1,0:T(8,128)(2,1)}, bf16[1,1536,128]{2,1,0:T(8,128)(2,1)S(1)}, u32[]{:S(2)}, u32[]{:S(2)}) collective-permute-start(bf16[1,1536,128]{2,1,0:T(8,128)(2,1)} %bitcast.42), channel_id=1, source_target_pairs={{0,16},{1,5},{2,18},{3,7},{4,20},{5,1},{6,22},{7,3},{8,24},{9,13},... | collective-permute-start | bytes 1179656 | tf_op jit(solution)/shard_map/ppermute | solution.py:43
  15.5 1.4 collective-permute-start.1
  16.9 0.6 collective-permute-start
  17.5 0.6 stack.168.where_ref
  18.1 0.6 stack.191.index_ref
  18.8 6.6 %all-to-all-done.r_ref = bf16[32,128,128]{2,1,0:T(8,128)(2,1)S(1)} async-done(((bf16[32,128,128]{2,1,0:T(8,128)(2,1)}), bf16[32,128,128]{2,1,0:T(8,128)(2,1)S(1)}, u32[]{:S(2)}, u32[]{:S(2)}) %all-to-all-start) | async-done | bytes 1048608 | tf_op jit(solution)/shard_map/all_to_all | solution.py:327
  25.4 1.0 copy-done.7
  26.3 23.8 %shard_map.57.refs_20_ = bf16[22,128,128]{2,1,0:T(8,128)(2,1)} custom-call(s32[22]{0:T(128)} %stack.191.index_ref, bf16[32,128,128]{2,1,0:T(8,128)(2,1)} %copy-done.7), custom_call_target="tpu_custom_call" | custom-call | bytes 2097152 | tf_op jit(solution)/shard_map/pallas_call | solution.py:165
  50.2 4.1 %shard_map.58 = (bf16[2,128,1024]{2,1,0:T(8,128)(2,1)}, bf16[2,128,1024]{2,1,0:T(8,128)(2,1)}, bf16[2,128,1024]{2,1,0:T(8,128)(2,1)}, bf16[2,128,1024]{2,1,0:T(8,128)(2,1)}, bf16[2,128,1024]{2,1,0:T(8,128)(2,1)}) custom-call(s32[10]{0:T(128)} %stack.168.where_ref, s32[1,256]{1,0:T(1,128)} %pattern_ref.4, bf16[128,32768]{1,0:T(8,128)(2,1)} %b_ref.2), custom_call_target="tpu_custom_call" | custom-call | flops 3145728 | bytes 6291456 | tf_op jit(solution)/shard_map/pallas_call | solution.py:145
  54.2 4.1 %collective-permute-start.10 = (bf16[2,128,1024]{2,1,0:T(8,128)(2,1)}, bf16[2,128,1024]{2,1,0:T(8,128)(2,1)S(1)}, u32[]{:S(2)}, u32[]{:S(2)}) collective-permute-start(bf16[2,128,1024]{2,1,0:T(8,128)(2,1)} %get-tuple-element.21), channel_id=1, source_target_pairs={{0,8},{1,3},{2,10},{3,5},{4,12},{5,7},{6,14},{7,1},{8,16},{9,11},{... | collective-permute-start | bytes 1572872 | tf_op jit(solution)/shard_map/ppermute | solution.py:43
  58.3 5.9 %collective-permute-start.19 = (bf16[22,128,128]{2,1,0:T(8,128)(2,1)S(1)}, bf16[22,128,128]{2,1,0:T(8,128)(2,1)S(1)}, u32[]{:S(2)}, u32[]{:S(2)}) collective-permute-start(bf16[22,128,128]{2,1,0:T(8,128)(2,1)S(1)} %copy-done.8), channel_id=1, source_target_pairs={{0,224},{32,0},{64,32},{96,64},{128,96},{160,128},{192,160},{224,1... | collective-permute-start | bytes 2162696 | tf_op jit(solution)/shard_map/ppermute | solution.py:51
  64.3 3.2 %collective-permute-start.13 = (bf16[2,128,1024]{2,1,0:T(8,128)(2,1)}, bf16[2,128,1024]{2,1,0:T(8,128)(2,1)S(1)}, u32[]{:S(2)}, u32[]{:S(2)}) collective-permute-start(bf16[2,128,1024]{2,1,0:T(8,128)(2,1)} %get-tuple-element.24), channel_id=1, source_target_pairs={{0,6},{1,25},{2,0},{3,27},{4,2},{5,29},{6,4},{7,31},{8,14},{9,1},{... | collective-permute-start | bytes 1572872 | tf_op jit(solution)/shard_map/ppermute | solution.py:43
  67.5 5.2 %collective-permute-start.15 = (bf16[22,128,128]{2,1,0:T(8,128)(2,1)S(1)}, bf16[22,128,128]{2,1,0:T(8,128)(2,1)S(1)}, u32[]{:S(2)}, u32[]{:S(2)}) collective-permute-start(bf16[22,128,128]{2,1,0:T(8,128)(2,1)S(1)} %copy-done.8), channel_id=1, source_target_pairs={{0,32},{32,64},{64,96},{96,128},{128,160},{160,192},{192,224},{224... | collective-permute-start | bytes 2162696 | tf_op jit(solution)/shard_map/ppermute | solution.py:51
  72.9 23.0 %collective-permute-done.11.refs_10_.refs_16_ = bf16[2,128,1024]{2,1,0:T(8,128)(2,1)S(1)} collective-permute-done((bf16[2,128,1024]{2,1,0:T(8,128)(2,1)}, bf16[2,128,1024]{2,1,0:T(8,128)(2,1)S(1)}, u32[]{:S(2)}, u32[]{:S(2)}) %collective-permute-start.11) | collective-permute-done | bytes 524320 | tf_op jit(solution)/shard_map/ppermute | solution.py:43
  96.1 2.0 collective-permute-start.3
  98.2 2.0 collective-permute-start.16
  100.2 11.5 %collective-permute-done.20.refs_21_ = bf16[22,128,128]{2,1,0:T(8,128)(2,1)S(1)} collective-permute-done((bf16[22,128,128]{2,1,0:T(8,128)(2,1)S(1)}, bf16[22,128,128]{2,1,0:T(8,128)(2,1)S(1)}, u32[]{:S(2)}, u32[]{:S(2)}) %collective-permute-start.20) | collective-permute-done | bytes 720928 | tf_op jit(solution)/shard_map/ppermute | solution.py:51
  111.7 3.7 %collective-permute-start.21 = (bf16[22,128,128]{2,1,0:T(8,128)(2,1)S(1)}, bf16[22,128,128]{2,1,0:T(8,128)(2,1)}, u32[]{:S(2)}, u32[]{:S(2)}) collective-permute-start(bf16[22,128,128]{2,1,0:T(8,128)(2,1)S(1)} %collective-permute-done.20.refs_21_), channel_id=1, source_target_pairs={{0,224},{32,0},{64,32},{96,64},{128,96},{160,128},{192,160},{224,1... | collective-permute-start | bytes 2162696 | tf_op jit(solution)/shard_map/ppermute | solution.py:51
  115.4 0.7 slice_dynamic-update-slice_fusion.4
  116.1 0.8 slice_dynamic-update-slice_fusion.3
  116.9 0.7 slice_dynamic-update-slice_fusion.2
  118.1 0.5 collective-permute-start.9
  118.6 16.2 %collective-permute-done.3.refs_1_ = bf16[4,1536,128]{2,1,0:T(8,128)(2,1)} collective-permute-done((bf16[4,1536,128]{2,1,0:T(8,128)(2,1)S(1)}, bf16[4,1536,128]{2,1,0:T(8,128)(2,1)}, u32[]{:S(2)}, u32[]{:S(2)}) %collective-permute-start.3) | collective-permute-done | bytes 1572896 | tf_op jit(solution)/shard_map/ppermute | solution.py:43
  134.9 0.5 collective-permute-start.7
  135.4 0.7 slice_dynamic-update-slice_fusion.1
  136.1 0.7 slice_dynamic-update-slice_fusion
  137.1 0.7 copy.10.cpat_ref
  137.7 0.6 concatenate.7.blk_ref
  138.4 0.6 pad_add_fusion.blk_ref
  139.0 0.6 pad_add_fusion.2.blk_ref
  139.7 0.6 pad_add_fusion.1.blk_ref
  140.2 1.0 slice.33
  141.3 1.0 slice.32
  142.4 2.0 collective-permute-start.18
  144.4 9.9 %shard_map.61 = (f32[1536,256]{1,0:T(8,128)}, f32[2,128]{1,0:T(2,128)}) custom-call(s32[2]{0:T(128)} %pad_add_fusion.2.blk_ref, s32[12,8]{1,0:T(8,128)} %copy.10.cpat_ref, bf16[4,1536,128]{2,1,0:T(8,128)(2,1)} %copy-done.1, bf16[4,1536,128]{2,1,0:T(8,128)(2,1)} %collective-permute-done.3.refs_1_, bf16[4,1536,128]{2,1,0:T(8,128)(2,1)} %collective-permute-done.4.refs_2_, ...), custom_call_target="tpu_custom_call" | custom-call | flops 3221225472 | bytes 16777216 | tf_op jit(solution)/shard_map/pallas_call | solution.py:273
  154.3 9.9 %shard_map.60 = (f32[1536,256]{1,0:T(8,128)}, f32[2,128]{1,0:T(2,128)}) custom-call(s32[2]{0:T(128)} %pad_add_fusion.1.blk_ref, s32[12,8]{1,0:T(8,128)} %copy.10.cpat_ref, bf16[4,1536,128]{2,1,0:T(8,128)(2,1)} %copy-done.1, bf16[4,1536,128]{2,1,0:T(8,128)(2,1)} %collective-permute-done.3.refs_1_, bf16[4,1536,128]{2,1,0:T(8,128)(2,1)} %collective-permute-done.4.refs_2_, ...), custom_call_target="tpu_custom_call" | custom-call | flops 3221225472 | bytes 16777216 | tf_op jit(solution)/shard_map/pallas_call | solution.py:273
  164.2 9.9 %shard_map.59 = (f32[1536,256]{1,0:T(8,128)}, f32[2,128]{1,0:T(2,128)}) custom-call(s32[2]{0:T(128)} %pad_add_fusion.blk_ref, s32[12,8]{1,0:T(8,128)} %copy.10.cpat_ref, bf16[4,1536,128]{2,1,0:T(8,128)(2,1)} %copy-done.1, bf16[4,1536,128]{2,1,0:T(8,128)(2,1)} %collective-permute-done.3.refs_1_, bf16[4,1536,128]{2,1,0:T(8,128)(2,1)} %collective-permute-done.4.refs_2_, ...), custom_call_target="tpu_custom_call" | custom-call | flops 3221225472 | bytes 16777216 | tf_op jit(solution)/shard_map/pallas_call | solution.py:273
  174.1 0.7 copy-done.14
  174.9 9.8 %shard_map.62 = (f32[1536,256]{1,0:T(8,128)}, f32[8,8,128]{2,1,0:T(8,128)}) custom-call(s32[10]{0:T(128)} %concatenate.7.blk_ref, s32[12,8]{1,0:T(8,128)} %copy.10.cpat_ref, bf16[4,1536,128]{2,1,0:T(8,128)(2,1)} %copy-done.1, bf16[4,1536,128]{2,1,0:T(8,128)(2,1)} %collective-permute-done.3.refs_1_, bf16[4,1536,128]{2,1,0:T(8,128)(2,1)} %collective-permute-done.4.refs_2_, ...), custom_call_target="tpu_custom_call" | custom-call | flops 3221225472 | bytes 16777216 | tf_op jit(solution)/shard_map/pallas_call | solution.py:273
  184.7 10.1 %all-to-all-start.1 = ((f32[8,8,128]{2,1,0:T(8,128)}), f32[8,8,128]{2,1,0:T(8,128)S(1)}, u32[]{:S(2)}, u32[]{:S(2)}) async-start(f32[8,8,128]{2,1,0:T(8,128)} %get-tuple-element.28), calls=%async_computation.1 | async-start | bytes 65536 | tf_op jit(solution)/shard_map/all_to_all | solution.py:368
  194.8 0.6 stack.157.blk_ref
  195.4 7.4 %all-to-all-done.1.t_ref = f32[8,8,128]{2,1,0:T(8,128)S(1)} async-done(((f32[8,8,128]{2,1,0:T(8,128)}), f32[8,8,128]{2,1,0:T(8,128)S(1)}, u32[]{:S(2)}, u32[]{:S(2)}) %all-to-all-start.1) | async-done | bytes 32800 | tf_op jit(solution)/shard_map/all_to_all | solution.py:368
  202.8 0.6 copy-done.16
  203.4 6.4 %shard_map.63 = bf16[1536,1024]{1,0:T(8,128)(2,1)} custom-call(s32[8]{0:T(128)} %stack.157.blk_ref, f32[8,8,128]{2,1,0:T(8,128)} %copy-done.16, f32[1536,256]{1,0:T(8,128)} %get-tuple-element.29.i0, f32[1536,256]{1,0:T(8,128)} %get-tuple-element.30.i1, f32[1536,256]{1,0:T(8,128)} %get-tuple-element.31.i2, f32[1536,256]{1,0:T(8,128)} %get-tuple-element.32.i3), custom_call_target="tpu_custom_call" | custom-call | flops 3145728 | bytes 10485760 | tf_op jit(solution)/shard_map/pallas_call | solution.py:305
  (66 shorter events, 1.3 us)
Async XLA Ops:
  3.2 7.7 %copy-start.18 = (s32[12,1]{0,1:T(1,128)S(1)}, s32[12,1]{0,1:T(1,128)}, u32[]{:S(2)}) copy-start(s32[12,1]{0,1:T(1,128)} %param.7) | copy-start | bytes 148
  3.2 22.2 %all-to-all-start = ((bf16[32,128,128]{2,1,0:T(8,128)(2,1)}), bf16[32,128,128]{2,1,0:T(8,128)(2,1)S(1)}, u32[]{:S(2)}, u32[]{:S(2)}) async-start(bf16[32,128,128]{2,1,0:T(8,128)(2,1)} %shard_map.56), calls=%async_computation | async-start | bytes 2097152 | tf_op jit(solution)/shard_map/all_to_all | solution.py:327
  13.4 50.8 %collective-permute-start.2 = (bf16[1,1536,128]{2,1,0:T(8,128)(2,1)}, bf16[1,1536,128]{2,1,0:T(8,128)(2,1)S(1)}, u32[]{:S(2)}, u32[]{:S(2)}) collective-permute-start(bf16[1,1536,128]{2,1,0:T(8,128)(2,1)} %bitcast.42), channel_id=1, source_target_pairs={{0,16},{1,5},{2,18},{3,7},{4,20},{5,1},{6,22},{7,3},{8,24},{9,13},... | collective-permute-start | bytes 1179656 | tf_op jit(solution)/shard_map/ppermute | solution.py:43
  15.5 48.7 %collective-permute-start.1 = (bf16[1,1536,128]{2,1,0:T(8,128)(2,1)}, bf16[1,1536,128]{2,1,0:T(8,128)(2,1)S(1)}, u32[]{:S(2)}, u32[]{:S(2)}) collective-permute-start(bf16[1,1536,128]{2,1,0:T(8,128)(2,1)} %bitcast.43), channel_id=1, source_target_pairs={{0,24},{1,7},{2,26},{3,1},{4,28},{5,3},{6,30},{7,5},{8,0},{9,15},{... | collective-permute-start | bytes 1179656 | tf_op jit(solution)/shard_map/ppermute | solution.py:43
  16.9 47.4 %collective-permute-start = (bf16[1,1536,128]{2,1,0:T(8,128)(2,1)}, bf16[1,1536,128]{2,1,0:T(8,128)(2,1)S(1)}, u32[]{:S(2)}, u32[]{:S(2)}) collective-permute-start(bf16[1,1536,128]{2,1,0:T(8,128)(2,1)} %bitcast.44), channel_id=1, source_target_pairs={{0,8},{1,3},{2,10},{3,5},{4,12},{5,7},{6,14},{7,1},{8,16},{9,11},{... | collective-permute-start | bytes 1179656 | tf_op jit(solution)/shard_map/ppermute | solution.py:43
  25.4 1.0 copy-start.7
  50.1 8.2 %copy-start.8 = (bf16[22,128,128]{2,1,0:T(8,128)(2,1)S(1)}, bf16[22,128,128]{2,1,0:T(8,128)(2,1)}, u32[]{:S(2)}) copy-start(bf16[22,128,128]{2,1,0:T(8,128)(2,1)} %shard_map.57.refs_20_) | copy-start | bytes 2162692
  50.1 22.6 %copy-start.9 = (bf16[1536,128]{1,0:T(8,128)(2,1)S(1)}, bf16[1536,128]{1,0:T(8,128)(2,1)}, u32[]{:S(2)}) copy-start(bf16[1536,128]{1,0:T(8,128)(2,1)} %shard_map.55) | copy-start | bytes 1179652
  54.2 13.3 %collective-permute-start.10 = (bf16[2,128,1024]{2,1,0:T(8,128)(2,1)}, bf16[2,128,1024]{2,1,0:T(8,128)(2,1)S(1)}, u32[]{:S(2)}, u32[]{:S(2)}) collective-permute-start(bf16[2,128,1024]{2,1,0:T(8,128)(2,1)} %get-tuple-element.21), channel_id=1, source_target_pairs={{0,8},{1,3},{2,10},{3,5},{4,12},{5,7},{6,14},{7,1},{8,16},{9,11},{... | collective-permute-start | bytes 1572872 | tf_op jit(solution)/shard_map/ppermute | solution.py:43
  58.3 39.8 %collective-permute-start.19 = (bf16[22,128,128]{2,1,0:T(8,128)(2,1)S(1)}, bf16[22,128,128]{2,1,0:T(8,128)(2,1)S(1)}, u32[]{:S(2)}, u32[]{:S(2)}) collective-permute-start(bf16[22,128,128]{2,1,0:T(8,128)(2,1)S(1)} %copy-done.8), channel_id=1, source_target_pairs={{0,224},{32,0},{64,32},{96,64},{128,96},{160,128},{192,160},{224,1... | collective-permute-start | bytes 2162696 | tf_op jit(solution)/shard_map/ppermute | solution.py:51
  64.2 31.8 %collective-permute-start.11 = (bf16[2,128,1024]{2,1,0:T(8,128)(2,1)}, bf16[2,128,1024]{2,1,0:T(8,128)(2,1)S(1)}, u32[]{:S(2)}, u32[]{:S(2)}) collective-permute-start(bf16[2,128,1024]{2,1,0:T(8,128)(2,1)} %get-tuple-element.22), channel_id=1, source_target_pairs={{0,24},{1,7},{2,26},{3,1},{4,28},{5,3},{6,30},{7,5},{8,0},{9,15},{... | collective-permute-start | bytes 1572872 | tf_op jit(solution)/shard_map/ppermute | solution.py:43
  64.2 31.8 %collective-permute-start.12 = (bf16[2,128,1024]{2,1,0:T(8,128)(2,1)}, bf16[2,128,1024]{2,1,0:T(8,128)(2,1)S(1)}, u32[]{:S(2)}, u32[]{:S(2)}) collective-permute-start(bf16[2,128,1024]{2,1,0:T(8,128)(2,1)} %get-tuple-element.23), channel_id=1, source_target_pairs={{0,2},{1,9},{2,4},{3,11},{4,6},{5,13},{6,0},{7,15},{8,10},{9,17},{... | collective-permute-start | bytes 1572872 | tf_op jit(solution)/shard_map/ppermute | solution.py:43
  64.3 51.0 %copy-start.2 = (bf16[2,128,1024]{2,1,0:T(8,128)(2,1)S(1)}, bf16[2,128,1024]{2,1,0:T(8,128)(2,1)}, u32[]{:S(2)}) copy-start(bf16[2,128,1024]{2,1,0:T(8,128)(2,1)} %get-tuple-element.20.refs_8_.refs_14_) | copy-start | bytes 1572868
  64.3 31.8 %collective-permute-start.13 = (bf16[2,128,1024]{2,1,0:T(8,128)(2,1)}, bf16[2,128,1024]{2,1,0:T(8,128)(2,1)S(1)}, u32[]{:S(2)}, u32[]{:S(2)}) collective-permute-start(bf16[2,128,1024]{2,1,0:T(8,128)(2,1)} %get-tuple-element.24), channel_id=1, source_target_pairs={{0,6},{1,25},{2,0},{3,27},{4,2},{5,29},{6,4},{7,31},{8,14},{9,1},{... | collective-permute-start | bytes 1572872 | tf_op jit(solution)/shard_map/ppermute | solution.py:43
  67.5 48.6 %copy-start.3 = (bf16[2,128,1024]{2,1,0:T(8,128)(2,1)}, bf16[2,128,1024]{2,1,0:T(8,128)(2,1)S(1)}, u32[]{:S(2)}) copy-start(bf16[2,128,1024]{2,1,0:T(8,128)(2,1)S(1)} %collective-permute-done.10.refs_9_.refs_15_) | copy-start | bytes 1572868
  67.5 30.6 %collective-permute-start.15 = (bf16[22,128,128]{2,1,0:T(8,128)(2,1)S(1)}, bf16[22,128,128]{2,1,0:T(8,128)(2,1)S(1)}, u32[]{:S(2)}, u32[]{:S(2)}) collective-permute-start(bf16[22,128,128]{2,1,0:T(8,128)(2,1)S(1)} %copy-done.8), channel_id=1, source_target_pairs={{0,32},{32,64},{64,96},{96,128},{128,160},{160,192},{192,224},{224... | collective-permute-start | bytes 2162696 | tf_op jit(solution)/shard_map/ppermute | solution.py:51
  72.9 68.3 %copy-start.1 = (bf16[4,1536,128]{2,1,0:T(8,128)(2,1)}, bf16[4,1536,128]{2,1,0:T(8,128)(2,1)S(1)}, u32[]{:S(2)}) copy-start(bf16[4,1536,128]{2,1,0:T(8,128)(2,1)S(1)} %pad_maximum_fusion.refs_0_) | copy-start | bytes 4718596
  72.9 64.1 %copy-start.17 = (s32[12,8]{0,1:T(8,128)S(1)}, s32[12,8]{0,1:T(8,128)}, u32[]{:S(2)}) copy-start(s32[12,8]{0,1:T(8,128)} %param.9) | copy-start | bytes 1156
  96.0 40.9 %copy-start.4 = (bf16[2,128,1024]{2,1,0:T(8,128)(2,1)}, bf16[2,128,1024]{2,1,0:T(8,128)(2,1)S(1)}, u32[]{:S(2)}) copy-start(bf16[2,128,1024]{2,1,0:T(8,128)(2,1)S(1)} %collective-permute-done.11.refs_10_.refs_16_) | copy-start | bytes 1572868
  96.0 22.1 %collective-permute-start.5 = (bf16[4,1536,128]{2,1,0:T(8,128)(2,1)S(1)}, bf16[4,1536,128]{2,1,0:T(8,128)(2,1)}, u32[]{:S(2)}, u32[]{:S(2)}) collective-permute-start(bf16[4,1536,128]{2,1,0:T(8,128)(2,1)S(1)} %pad_maximum_fusion.refs_0_), channel_id=1, source_target_pairs={{0,4},{1,17},{2,6},{3,19},{4,0},{5,21},{6,2},{7,23},{8,12},{9,25},... | collective-permute-start | bytes 4718600 | tf_op jit(solution)/shard_map/ppermute | solution.py:43
  96.0 40.9 %copy-start.5 = (bf16[2,128,1024]{2,1,0:T(8,128)(2,1)}, bf16[2,128,1024]{2,1,0:T(8,128)(2,1)S(1)}, u32[]{:S(2)}) copy-start(bf16[2,128,1024]{2,1,0:T(8,128)(2,1)S(1)} %collective-permute-done.12.refs_11_.refs_17_) | copy-start | bytes 1572868
  96.0 22.1 %collective-permute-start.4 = (bf16[4,1536,128]{2,1,0:T(8,128)(2,1)S(1)}, bf16[4,1536,128]{2,1,0:T(8,128)(2,1)}, u32[]{:S(2)}, u32[]{:S(2)}) collective-permute-start(bf16[4,1536,128]{2,1,0:T(8,128)(2,1)S(1)} %pad_maximum_fusion.refs_0_), channel_id=1, source_target_pairs={{0,6},{1,25},{2,0},{3,27},{4,2},{5,29},{6,4},{7,31},{8,14},{9,1},{... | collective-permute-start | bytes 4718600 | tf_op jit(solution)/shard_map/ppermute | solution.py:43
  96.1 40.7 %copy-start.6 = (bf16[2,128,1024]{2,1,0:T(8,128)(2,1)}, bf16[2,128,1024]{2,1,0:T(8,128)(2,1)S(1)}, u32[]{:S(2)}) copy-start(bf16[2,128,1024]{2,1,0:T(8,128)(2,1)S(1)} %collective-permute-done.13.refs_12_.refs_18_) | copy-start | bytes 1572868
  96.1 38.7 %collective-permute-start.3 = (bf16[4,1536,128]{2,1,0:T(8,128)(2,1)S(1)}, bf16[4,1536,128]{2,1,0:T(8,128)(2,1)}, u32[]{:S(2)}, u32[]{:S(2)}) collective-permute-start(bf16[4,1536,128]{2,1,0:T(8,128)(2,1)S(1)} %pad_maximum_fusion.refs_0_), channel_id=1, source_target_pairs={{0,2},{1,9},{2,4},{3,11},{4,6},{5,13},{6,0},{7,15},{8,10},{9,17},{... | collective-permute-start | bytes 4718600 | tf_op jit(solution)/shard_map/ppermute | solution.py:43
  98.1 38.7 %copy-start.10 = (bf16[22,128,128]{2,1,0:T(8,128)(2,1)}, bf16[22,128,128]{2,1,0:T(8,128)(2,1)S(1)}, u32[]{:S(2)}) copy-start(bf16[22,128,128]{2,1,0:T(8,128)(2,1)S(1)} %collective-permute-done.19.refs_21_) | copy-start | bytes 2162692
  98.1 13.5 %collective-permute-start.20 = (bf16[22,128,128]{2,1,0:T(8,128)(2,1)S(1)}, bf16[22,128,128]{2,1,0:T(8,128)(2,1)S(1)}, u32[]{:S(2)}, u32[]{:S(2)}) collective-permute-start(bf16[22,128,128]{2,1,0:T(8,128)(2,1)S(1)} %collective-permute-done.19.refs_21_), channel_id=1, source_target_pairs={{0,224},{32,0},{64,32},{96,64},{128,96},{160,128},{192,160},{224,1... | collective-permute-start | bytes 2162696 | tf_op jit(solution)/shard_map/ppermute | solution.py:51
  98.1 38.7 %copy-start.11 = (bf16[22,128,128]{2,1,0:T(8,128)(2,1)}, bf16[22,128,128]{2,1,0:T(8,128)(2,1)S(1)}, u32[]{:S(2)}) copy-start(bf16[22,128,128]{2,1,0:T(8,128)(2,1)S(1)} %collective-permute-done.15.refs_20_) | copy-start | bytes 2162692
  98.2 17.9 %collective-permute-start.16 = (bf16[22,128,128]{2,1,0:T(8,128)(2,1)S(1)}, bf16[22,128,128]{2,1,0:T(8,128)(2,1)S(1)}, u32[]{:S(2)}, u32[]{:S(2)}) collective-permute-start(bf16[22,128,128]{2,1,0:T(8,128)(2,1)S(1)} %collective-permute-done.15.refs_20_), channel_id=1, source_target_pairs={{0,32},{32,64},{64,96},{96,128},{128,160},{160,192},{192,224},{224... | collective-permute-start | bytes 2162696 | tf_op jit(solution)/shard_map/ppermute | solution.py:51
  111.7 25.2 %copy-start.12 = (bf16[22,128,128]{2,1,0:T(8,128)(2,1)}, bf16[22,128,128]{2,1,0:T(8,128)(2,1)S(1)}, u32[]{:S(2)}) copy-start(bf16[22,128,128]{2,1,0:T(8,128)(2,1)S(1)} %collective-permute-done.20.refs_21_) | copy-start | bytes 2162692
  111.7 23.2 %collective-permute-start.21 = (bf16[22,128,128]{2,1,0:T(8,128)(2,1)S(1)}, bf16[22,128,128]{2,1,0:T(8,128)(2,1)}, u32[]{:S(2)}, u32[]{:S(2)}) collective-permute-start(bf16[22,128,128]{2,1,0:T(8,128)(2,1)S(1)} %collective-permute-done.20.refs_21_), channel_id=1, source_target_pairs={{0,224},{32,0},{64,32},{96,64},{128,96},{160,128},{192,160},{224,1... | collective-permute-start | bytes 2162696 | tf_op jit(solution)/shard_map/ppermute | solution.py:51
  116.1 20.8 %copy-start.13 = (bf16[22,128,128]{2,1,0:T(8,128)(2,1)}, bf16[22,128,128]{2,1,0:T(8,128)(2,1)S(1)}, u32[]{:S(2)}) copy-start(bf16[22,128,128]{2,1,0:T(8,128)(2,1)S(1)} %collective-permute-done.16.refs_20_) | copy-start | bytes 2162692
  116.1 20.8 %collective-permute-start.17 = (bf16[22,128,128]{2,1,0:T(8,128)(2,1)S(1)}, bf16[22,128,128]{2,1,0:T(8,128)(2,1)}, u32[]{:S(2)}, u32[]{:S(2)}) collective-permute-start(bf16[22,128,128]{2,1,0:T(8,128)(2,1)S(1)} %collective-permute-done.16.refs_20_), channel_id=1, source_target_pairs={{0,32},{32,64},{64,96},{96,128},{128,160},{160,192},{192,224},{224... | collective-permute-start | bytes 2162696 | tf_op jit(solution)/shard_map/ppermute | solution.py:51
  118.1 24.2 %collective-permute-start.6 = (bf16[4,1536,128]{2,1,0:T(8,128)(2,1)S(1)}, bf16[4,1536,128]{2,1,0:T(8,128)(2,1)}, u32[]{:S(2)}, u32[]{:S(2)}) collective-permute-start(bf16[4,1536,128]{2,1,0:T(8,128)(2,1)S(1)} %pad_maximum_fusion.refs_0_), channel_id=1, source_target_pairs={{0,1},{1,0},{2,3},{3,2},{4,5},{5,4},{6,7},{7,6},{8,9},{9,8},{10,11... | collective-permute-start | bytes 4718600 | tf_op jit(solution)/shard_map/ppermute | solution.py:47
  118.1 26.3 %collective-permute-start.9 = (bf16[4,1536,128]{2,1,0:T(8,128)(2,1)}, bf16[4,1536,128]{2,1,0:T(8,128)(2,1)}, u32[]{:S(2)}, u32[]{:S(2)}) collective-permute-start(bf16[4,1536,128]{2,1,0:T(8,128)(2,1)} %collective-permute-done.5.refs_3_), channel_id=1, source_target_pairs={{0,1},{1,0},{2,3},{3,2},{4,5},{5,4},{6,7},{7,6},{8,9},{9,8},{10,11... | collective-permute-start | bytes 4718600 | tf_op jit(solution)/shard_map/ppermute | solution.py:47
  134.9 9.5 %collective-permute-start.8 = (bf16[4,1536,128]{2,1,0:T(8,128)(2,1)}, bf16[4,1536,128]{2,1,0:T(8,128)(2,1)}, u32[]{:S(2)}, u32[]{:S(2)}) collective-permute-start(bf16[4,1536,128]{2,1,0:T(8,128)(2,1)} %collective-permute-done.4.refs_2_), channel_id=1, source_target_pairs={{0,1},{1,0},{2,3},{3,2},{4,5},{5,4},{6,7},{7,6},{8,9},{9,8},{10,11... | collective-permute-start | bytes 4718600 | tf_op jit(solution)/shard_map/ppermute | solution.py:47
  134.9 9.5 %collective-permute-start.7 = (bf16[4,1536,128]{2,1,0:T(8,128)(2,1)}, bf16[4,1536,128]{2,1,0:T(8,128)(2,1)}, u32[]{:S(2)}, u32[]{:S(2)}) collective-permute-start(bf16[4,1536,128]{2,1,0:T(8,128)(2,1)} %collective-permute-done.3.refs_1_), channel_id=1, source_target_pairs={{0,1},{1,0},{2,3},{3,2},{4,5},{5,4},{6,7},{7,6},{8,9},{9,8},{10,11... | collective-permute-start | bytes 4718600 | tf_op jit(solution)/shard_map/ppermute | solution.py:47
  136.9 5.5 %collective-permute-start.14 = (bf16[5,128,1024]{2,1,0:T(8,128)(2,1)}, bf16[5,128,1024]{2,1,0:T(8,128)(2,1)S(1)}, u32[]{:S(2)}, u32[]{:S(2)}) collective-permute-start(bf16[5,128,1024]{2,1,0:T(8,128)(2,1)} %slice_dynamic-update-slice_fusion), channel_id=1, source_target_pairs={{0,1},{1,0},{2,3},{3,2},{4,5},{5,4},{6,7},{7,6},{8,9},{9,8},{10,11... | collective-permute-start | bytes 3932168 | tf_op jit(solution)/shard_map/ppermute | solution.py:47
  142.3 31.8 %collective-permute-start.22 = (bf16[11,128,128]{2,1,0:T(8,128)(2,1)S(1)}, bf16[11,128,128]{2,1,0:T(8,128)(2,1)S(1)}, u32[]{:S(2)}, u32[]{:S(2)}) collective-permute-start(bf16[11,128,128]{2,1,0:T(8,128)(2,1)S(1)} %slice.33), channel_id=1, source_target_pairs={{0,224},{32,0},{64,32},{96,64},{128,96},{160,128},{192,160},{224,1... | collective-permute-start | bytes 1081352 | tf_op jit(solution)/shard_map/ppermute | solution.py:51
  142.4 2.0 copy-start
  142.4 31.7 %collective-permute-start.18 = (bf16[11,128,128]{2,1,0:T(8,128)(2,1)S(1)}, bf16[11,128,128]{2,1,0:T(8,128)(2,1)S(1)}, u32[]{:S(2)}, u32[]{:S(2)}) collective-permute-start(bf16[11,128,128]{2,1,0:T(8,128)(2,1)S(1)} %slice.32), channel_id=1, source_target_pairs={{0,32},{32,64},{64,96},{96,128},{128,160},{160,192},{192,224},{224... | collective-permute-start | bytes 1081352 | tf_op jit(solution)/shard_map/ppermute | solution.py:51
  174.1 0.7 copy-start.14
  174.1 0.8 copy-start.15
  184.7 18.1 %all-to-all-start.1 = ((f32[8,8,128]{2,1,0:T(8,128)}), f32[8,8,128]{2,1,0:T(8,128)S(1)}, u32[]{:S(2)}, u32[]{:S(2)}) async-start(f32[8,8,128]{2,1,0:T(8,128)} %get-tuple-element.28), calls=%async_computation.1 | async-start | bytes 65536 | tf_op jit(solution)/shard_map/all_to_all | solution.py:368
  202.8 0.6 copy-start.16

commit v2 on v0

v2 whole, which is shorter than its diff:
```python
import functools

import jax
import jax.numpy as jnp
from jax import lax
from jax.experimental import pallas as pl
from jax.experimental.pallas import tpu as pltpu
from jax.sharding import PartitionSpec as P

BLOCK = 128
XS, YS, CORES = 4, 4, 2
COLS = XS * YS * CORES
ROWS = 8
EPS = 1e-06
F32 = jnp.float32
BF16 = jnp.bfloat16

OFFSETS = (0, -1, 1, 2)
NEAR = ((0, 0), (0, 1), (0, 2), (1, 0), (2, 0))
FAR = tuple((d, e) for d in range(4) for e in range(4) if (d, e) not in NEAR)


def flat(x, y, c):
    return ((x & (XS - 1)) * YS + (y & (YS - 1))) * CORES + c


def place(x, y, c, first, second):
    if isinstance(c, int):
        return flat(x + first, y + second, c) if c == 0 else flat(x + second, y + first, c)
    dx = jnp.where(c == 0, first, second)
    dy = jnp.where(c == 0, second, first)
    return flat(x + dx, y + dy, c)


def shift(value, first, second):
    pairs = []
    for x in range(XS):
        for y in range(YS):
            for c in range(CORES):
                pairs.append((flat(x, y, c), place(x, y, c, first, second)))
    return lax.ppermute(value, "col", pairs)


def swap(value):
    return lax.ppermute(value, "col", [(i, i ^ 1) for i in range(COLS)])


def smem():
    return pl.BlockSpec(memory_space=pltpu.SMEM)


def vmem():
    return pl.BlockSpec(memory_space=pltpu.VMEM)


def any_space():
    return pl.BlockSpec(memory_space=pl.ANY)


def params():
    return pltpu.CompilerParams(vmem_limit_bytes=56 * 1024 * 1024)


def mask_left_kernel(pattern_ref, a_ref, o_ref):
    for i in range(a_ref.shape[0] // BLOCK):
        rows = slice(i * BLOCK, (i + 1) * BLOCK)
        block = a_ref[rows, :]
        o_ref[rows, :] = jnp.where(pattern_ref[i, 0] != 0, block, jnp.zeros_like(block))


def mask_left(a, pattern):
    return pl.pallas_call(
        mask_left_kernel,
        out_shape=jax.ShapeDtypeStruct(a.shape, a.dtype),
        in_specs=[smem(), vmem()],
        out_specs=vmem(),
        compiler_params=params(),
        cost_estimate=pl.CostEstimate(flops=a.size, bytes_accessed=4 * a.size, transcendentals=0),
    )(pattern, a)


def spread_kernel(row_ref, pattern_ref, b_ref, o_ref, held, sems):
    row = row_ref[0]
    count = o_ref.shape[0]

    def copy(j):
        columns = pl.ds(pl.multiple_of((j * ROWS + row) * BLOCK, BLOCK), BLOCK)
        return pltpu.make_async_copy(b_ref.at[:, columns], held.at[j], sems.at[j])

    for j in range(count):
        copy(j).start()
    for j in range(count):
        copy(j).wait()
        block = held[j]
        o_ref[j] = jnp.where(pattern_ref[0, j * ROWS + row] != 0, block, jnp.zeros_like(block))


def spread(b, pattern, row):
    shape = (COLS, b.shape[0], BLOCK)
    return pl.pallas_call(
        spread_kernel,
        out_shape=jax.ShapeDtypeStruct(shape, b.dtype),
        in_specs=[smem(), smem(), any_space()],
        out_specs=vmem(),
        scratch_shapes=[pltpu.VMEM(shape, b.dtype), pltpu.SemaphoreType.DMA((COLS,))],
        compiler_params=params(),
        cost_estimate=pl.CostEstimate(flops=1 << 20, bytes_accessed=1 << 21, transcendentals=0),
    )(row, pattern, b)


def pieces_kernel(where_ref, pattern_ref, b_ref, *rest):
    count = len(NEAR)
    outs, held, sems = rest[:count], rest[count], rest[count + 1]
    width = outs[0].shape[2]
    blocks = width // BLOCK

    def copy(k):
        columns = pl.ds(pl.multiple_of(where_ref[k] * width, width), width)
        return pltpu.make_async_copy(b_ref.at[:, columns], held.at[k], sems.at[k])

    for k in range(2 * count):
        copy(k).start()
    for k in range(2 * count):
        copy(k).wait()
        for i in range(blocks):
            columns = slice(i * BLOCK, (i + 1) * BLOCK)
            block = held[k, :, columns]
            keep = pattern_ref[0, where_ref[k] * blocks + i] != 0
            outs[k // 2][k % 2, :, columns] = jnp.where(keep, block, jnp.zeros_like(block))


def pieces(b, pattern, where):
    width, count = b.shape[1] // COLS, len(NEAR)
    shape = (2, b.shape[0], width)
    return pl.pallas_call(
        pieces_kernel,
        out_shape=[jax.ShapeDtypeStruct(shape, b.dtype)] * count,
        in_specs=[smem(), smem(), any_space()],
        out_specs=[vmem()] * count,
        scratch_shapes=[
            pltpu.VMEM((2 * count, b.shape[0], width), b.dtype),
            pltpu.SemaphoreType.DMA((2 * count,)),
        ],
        compiler_params=params(),
        cost_estimate=pl.CostEstimate(flops=4 << 20, bytes_accessed=8 << 20, transcendentals=0),
    )(where, pattern, b)


def select_kernel(index_ref, r_ref, o_ref):
    for j in range(o_ref.shape[0]):
        o_ref[j] = r_ref[index_ref[j]]


def select(received, index):
    count = index.shape[0]
    return pl.pallas_call(
        select_kernel,
        out_shape=jax.ShapeDtypeStruct((count,) + received.shape[1:], received.dtype),
        in_specs=[smem(), vmem()],
        out_specs=vmem(),
        compiler_params=params(),
        cost_estimate=pl.CostEstimate(flops=0, bytes_accessed=2 << 20, transcendentals=0),
    )(index, pltpu.with_memory_space_constraint(received, pltpu.HBM))


CHUNK, TILE = 384, 512
HALF = 768


def held(value):
    return pltpu.with_memory_space_constraint(value, pltpu.VMEM)


def limit(size):
    return pltpu.CompilerParams(vmem_limit_bytes=size << 20)


def runs(o, d):
    found = []
    for e in range(4):
        if (d, e) in FAR:
            spot = o * len(FAR) + FAR.index((d, e))
        else:
            spot = 2 * len(FAR) + o * len(NEAR) + NEAR.index((d, e))
        if found and found[-1][2] + found[-1][1] == spot:
            found[-1][1] += 1
        else:
            found.append([e, 1, spot])
    return found


def near_kernel(*refs):
    refs = list(refs)
    lefts = [refs.pop(0) for _ in range(10)]
    nears = [refs.pop(0) for _ in range(len(NEAR) + 1)]
    left_out, o_ref, left, piece, near, out, nsem, lsem, osem = refs
    rows, count, depth = o_ref.shape[0], len(NEAR), left_out.shape[1]

    whole = [pltpu.make_async_copy(nears[k].at[0], near.at[k], nsem.at[k]) for k in range(count)]
    whole.append(pltpu.make_async_copy(nears[count], near.at[pl.ds(count, count)], nsem.at[count]))
    parts = []
    for i in range(rows // CHUNK):
        start = i * CHUNK
        part = []
        for k in range(8):
            o, d = k // 4, k % 4
            if d < 3:
                source = lefts[o * 5 + d].at[pl.ds(start, CHUNK), :]
            else:
                source = lefts[o * 5 + 3 + start // HALF].at[pl.ds(start % HALF, CHUNK), :]
            part.append(pltpu.make_async_copy(source, piece.at[i % 2, k], lsem.at[i * 8 + k]))
        parts.append(part)
    for group in (parts[0], whole, parts[1]):
        for copy in group:
            copy.start()
    outs = []
    for i, part in enumerate(parts):
        here, slot = pl.ds(i * CHUNK, CHUNK), i % 2
        for copy in part:
            copy.wait()
        if i >= 2:
            for copy in outs[i - 2]:
                copy.wait()
        for k in range(8):
            for block, width, spot in runs(k // 4, k % 4):
                lanes = slice(block * BLOCK, (block + width) * BLOCK)
                target = slice(spot * BLOCK, (spot + width) * BLOCK)
                left[slot, :, target] = piece[slot, k, :, lanes]
        if i + 2 < len(parts):
            for copy in parts[i + 2]:
                copy.start()
        outs.append([
            pltpu.make_async_copy(left.at[slot, :, pl.ds(0, depth)], left_out.at[here, :], osem.at[2 * i]),
            pltpu.make_async_copy(out.at[slot], o_ref.at[here, :], osem.at[2 * i + 1]),
        ])
        outs[i][0].start()
        if i == 0:
            for copy in whole:
                copy.wait()
        out[slot] = jnp.dot(
            left[slot, :, depth:],
            near[...].reshape(2 * count * BLOCK, ROWS * BLOCK),
            preferred_element_type=F32,
        )
        outs[i][1].start()
    for pair in outs[-2:]:
        for copy in pair:
            copy.wait()


def far_kernel(cpat_ref, left_in, sum_in, fars, o_ref, t_ref, left, partial, far, fsem, lsem):
    rows, sources = o_ref.shape[0], 2 * len(FAR)
    depth = sources * BLOCK
    blocks = [
        pltpu.make_async_copy(
            fars.at[pl.ds(n * sources, sources)],
            far.at[n // 2, :, :, pl.ds(n % 2 * BLOCK, BLOCK)],
            fsem.at[n],
        )
        for n in range(ROWS)
    ]
    parts = []
    for i in range(rows // CHUNK):
        here = pl.ds(i * CHUNK, CHUNK)
        parts.append([
            pltpu.make_async_copy(left_in.at[here, :], left.at[here, :], lsem.at[2 * i]),
            pltpu.make_async_copy(sum_in.at[here, :], partial.at[here, :], lsem.at[2 * i + 1]),
        ])
    for group in (blocks[:2], parts[0], blocks[2:4], *parts[1:], blocks[4:]):
        for copy in group:
            copy.start()
    sums = [jnp.zeros((1, BLOCK), F32) for _ in range(ROWS)]

    def multiply(pair, start, size):
        product = jnp.dot(
            left[start:start + size, :], far[pair].reshape(depth, 2 * BLOCK), preferred_element_type=F32
        )
        for n in range(2):
            lanes = slice(n * BLOCK, (n + 1) * BLOCK)
            column = 2 * pair + n
            target = slice(column * BLOCK, (column + 1) * BLOCK)
            for j in range(size // BLOCK):
                keep = cpat_ref[start // BLOCK + j, column] != 0
                place = slice(start + j * BLOCK, start + (j + 1) * BLOCK)
                block = product[j * BLOCK:(j + 1) * BLOCK, lanes] + partial[place, target]
                block = jnp.where(keep, block * block, jnp.zeros_like(block))
                o_ref[place, target] = block
                sums[column] = sums[column] + jnp.sum(block, axis=0, keepdims=True)

    for copy in blocks[:2]:
        copy.wait()
    for i, part in enumerate(parts):
        for copy in part:
            copy.wait()
        multiply(0, i * CHUNK, CHUNK)
        if i == 0:
            for copy in blocks[2:4]:
                copy.wait()
        multiply(1, i * CHUNK, CHUNK)
    for pair in (2, 3):
        for copy in blocks[2 * pair:2 * pair + 2]:
            copy.wait()
        for start in range(0, rows, TILE):
            multiply(pair, start, TILE)
    for r in range(ROWS):
        for n in range(ROWS):
            t_ref[r, n:n + 1, :] = sums[n]


def cost(rows, sources, data):
    return pl.CostEstimate(
        flops=2 * rows * sources * BLOCK * ROWS * BLOCK, bytes_accessed=data << 20, transcendentals=0
    )


def near_product(lefts, nears):
    rows = 2 * HALF
    return pl.pallas_call(
        near_kernel,
        out_shape=[
            jax.ShapeDtypeStruct((rows, 2 * len(FAR) * BLOCK), BF16),
            jax.ShapeDtypeStruct((rows, ROWS * BLOCK), F32),
        ],
        in_specs=[any_space()] * (len(lefts) + len(nears)),
        out_specs=[any_space()] * 2,
        scratch_shapes=[
            pltpu.VMEM((2, CHUNK, COLS * BLOCK), BF16),
            pltpu.VMEM((2, 8, CHUNK, 512), BF16),
            pltpu.VMEM((2 * len(NEAR), BLOCK, ROWS * BLOCK), BF16),
            pltpu.VMEM((2, CHUNK, ROWS * BLOCK), F32),
            pltpu.SemaphoreType.DMA((len(nears),)),
            pltpu.SemaphoreType.DMA((32,)),
            pltpu.SemaphoreType.DMA((8,)),
        ],
        compiler_params=limit(24),
        cost_estimate=cost(rows, 2 * len(NEAR), 32),
    )(*lefts, *nears)


def far_product(cpat, left, partial, fars):
    rows, depth = left.shape
    left, partial, fars = [
        pltpu.with_memory_space_constraint(array, pltpu.HBM) for array in (left, partial, fars)
    ]
    return pl.pallas_call(
        far_kernel,
        out_shape=[
            pltpu.VMEM((rows, ROWS * BLOCK), F32),
            jax.ShapeDtypeStruct((ROWS, ROWS, BLOCK), F32),
        ],
        in_specs=[smem()] + [any_space()] * 3,
        out_specs=[vmem()] * 2,
        scratch_shapes=[
            pltpu.VMEM((rows, depth), BF16),
            pltpu.VMEM((rows, ROWS * BLOCK), F32),
            pltpu.VMEM((ROWS // 2, 2 * len(FAR), BLOCK, 2 * BLOCK), BF16),
            pltpu.SemaphoreType.DMA((ROWS,)),
            pltpu.SemaphoreType.DMA((8,)),
        ],
        compiler_params=limit(32),
        cost_estimate=cost(rows, 2 * len(FAR), 24),
    )(cpat, left, partial, fars)


def rescale_kernel(count, t_ref, i_ref, o_ref):
    total = t_ref[0]
    for r in range(1, ROWS):
        total = total + t_ref[r]
    scale = count / (total + EPS)
    rows = pl.ds(pl.program_id(0) * o_ref.shape[0], o_ref.shape[0])
    for n in range(ROWS):
        lanes = slice(n * BLOCK, (n + 1) * BLOCK)
        o_ref[:, lanes] = (i_ref[rows, lanes] * scale[n:n + 1, :]).astype(BF16)


def rescale(totals, inflated):
    rows, columns = inflated.shape
    tile = 256
    return pl.pallas_call(
        functools.partial(rescale_kernel, float(rows * ROWS)),
        out_shape=jax.ShapeDtypeStruct((rows, columns), BF16),
        grid=(rows // tile,),
        in_specs=[pl.BlockSpec(totals.shape, lambda i: (0, 0, 0)), vmem()],
        out_specs=pl.BlockSpec((tile, columns), lambda i: (i, 0)),
        compiler_params=limit(16),
        cost_estimate=pl.CostEstimate(flops=rows * 2048, bytes_accessed=4 << 20, transcendentals=0),
    )(totals, held(inflated))


def shards(a_values, b_values, a_pattern, b_pattern, c_pattern):
    col = lax.axis_index("col").astype(jnp.int32)
    row = lax.axis_index("row").astype(jnp.int32)
    x, y, c = col >> 3, (col >> 1) & (YS - 1), col & (CORES - 1)

    sent = spread(b_values, b_pattern, row[None])
    received = lax.all_to_all(sent, "col", split_axis=0, concat_axis=0, tiled=True)

    left = mask_left(a_values, a_pattern)
    where = []
    steps = ((0, 0), (1, 0), (-1, 0), (0, 1), (0, -1))
    for first, second in steps:
        there = place(x, y, c, first, second)
        where += [there, there ^ 1]
    near = pieces(b_values, b_pattern, jnp.stack(where))
    index = []
    for core in (c, 1 - c):
        for d, e in FAR:
            index.append(place(x, y, core, OFFSETS[e], OFFSETS[d]))
    received, left, near = lax.optimization_barrier((received, left, near))
    own = select(received, jnp.stack(index))
    left, near, _ = lax.optimization_barrier((left, near, own))

    fars = lax.all_gather(own, "row", axis=0, tiled=True)

    line = jnp.concatenate([left] + [shift(left, s, 0) for s in (1, -1, 2)], axis=1)
    below, above = shift(line, 0, 1), shift(line, 0, -1)
    lefts = [line, below, above, shift(below[:HALF], 0, 1), shift(above[HALF:], 0, -1)]
    lefts = lefts + [swap(g) for g in lefts]

    nears = [near[0]] + [shift(piece, *step) for piece, step in zip(near[1:], steps[1:])]
    nears.append(swap(jnp.stack([piece[1] for piece in nears])))

    left, partial = near_product(lefts, nears)
    inflated, totals = far_product(c_pattern, left, partial, fars)
    gathered = lax.all_to_all(totals, "row", split_axis=0, concat_axis=0, tiled=True)
    return rescale(gathered, inflated)


def solution(mesh):
    return jax.shard_map(
        shards,
        mesh=mesh,
        in_specs=(
            P("row", "col"),
            P("col", None),
            P("row", "col"),
            P("col", None),
            P("row", "col"),
        ),
        out_specs=P("row", "col"),
        check_vma=False,
    )
```

time: 253 us -> 161 us (0.64)
  waiting for transfers between devices: 131 us -> 47.3 us
  Pallas kernels: 0 us -> 41 us
  local copies, waits for them, and re-layouts: 42.4 us -> 17.6 us
  matrix products: 18.5 us -> 0 us
  other arithmetic: 17.1 us -> 0 us
  starting transfers between devices: 7.69 us -> 22.8 us
  blocking collectives: 22.4 us -> 16.3 us
    all_to_all x1, waiting for transfers between devices: 131 us -> 7.73 us  [shards(): lax.all_to_all(sent, 'col', split_axis=0, concat_axis=0, tiled=True)]
    pallas_call x0 -> x7, Pallas kernels: none -> 41 us  [the longest x1 16.1 us: far_product(): pl.pallas_call(far_kernel, out_shape=[pltpu.VMEM((rows, ROWS * BLOCK), F3...]
    ppermute x0 -> x17, waiting for transfers between devices: none -> 39.6 us  [the longest x11 37 us: shift(): return lax.ppermute(value, 'col', pairs)]
    all_to_all x2 -> x0, local copies, waits for them, and re-layouts: 23.2 us -> none  [shards(): lax.all_to_all(right, 'col', split_axis=1, concat_axis=0, tiled=True)]
    psum x1 -> x0, blocking collectives: 22.4 us -> none  [shards(): column_total = lax.psum(jnp.sum(inflated, axis=0), 'row')]
    dot_general x1 -> x0, matrix products: 18.5 us -> none  [shards(): jnp.dot(lax.all_gather(left, 'col', axis=1, tiled=True), gathered, prefer...]
    all_to_all x0 -> x1, blocking collectives: none -> 16.3 us  [shards(): lax.all_to_all(totals, 'row', split_axis=0, concat_axis=0, tiled=True)]
    ppermute x0 -> x17, starting transfers between devices: none -> 15.2 us  [the longest x11 12.5 us: shift(): return lax.ppermute(value, 'col', pairs)]
  transfers between devices with their start and end apart: 2 -> 19, of which waited for: 1 -> 9; matrix products, arithmetic and copies ran while one was open for 17% -> 3% of each run, Pallas kernels for 0% -> 10%
where the time goes in v2:
time: 161 us; the launch traced here: 159 us
  waiting for transfers between devices  47.3 us (29%)
  Pallas kernels  41 us (25%)
  starting transfers between devices  22.8 us (14%)
  local copies, waits for them, and re-layouts  17.6 us (11%)
  blocking collectives  16.3 us (10%)
  between operations  13.6 us (8%)
    ppermute x11, waiting for transfers between devices, shift(): return lax.ppermute(value, 'col', pairs)  37 us
    all_to_all x1, blocking collectives, shards(): lax.all_to_all(totals, 'row', split_axis=0, concat_axis=0, tiled=True)  16.3 us
    pallas_call x1, Pallas kernels, far_product(): pl.pallas_call(far_kernel, out_shape=[pltpu.VMEM((rows, ROWS * BLOCK), F3...  16.1 us
    unnamed x45, local copies, waits for them, and re-layouts  15.4 us
    ppermute x11, starting transfers between devices, shift(): return lax.ppermute(value, 'col', pairs)  12.5 us
    pallas_call x1, Pallas kernels, near_product(): pl.pallas_call(near_kernel, out_shape=[jax.ShapeDtypeStruct((rows, 2 * le...  10.7 us
    all_to_all x1, waiting for transfers between devices, shards(): lax.all_to_all(sent, 'col', split_axis=0, concat_axis=0, tiled=True)  7.73 us
    all_to_all x1, starting transfers between devices, shards(): lax.all_to_all(sent, 'col', split_axis=0, concat_axis=0, tiled=True)  7.54 us
  transfers between devices with their start and end apart: 19, of which 9 were waited for; matrix products, arithmetic and copies ran while one was open for 3% of the time, Pallas kernels for 10%

profile of v2, /device:TPU:8, one launch (start us, length us, event | category | flops | bytes accessed | tf_op | source)
XLA Modules:
  0.0 158.6 jit_solution(2459567234385153636)
XLA Ops:
  6.5 3.1 %shard_map.55 = bf16[32,128,128]{2,1,0:T(8,128)(2,1)} custom-call(s32[1]{0:T(128)} %bitcast.row_ref, s32[1,256]{1,0:T(1,128)} %pattern_ref.4, bf16[128,32768]{1,0:T(8,128)(2,1)} %b_ref.3), custom_call_target="tpu_custom_call" | custom-call | flops 1048576 | bytes 2097152 | tf_op jit(solution)/shard_map/pallas_call | solution.py:100
  9.7 7.5 %all-to-all-start = ((bf16[32,128,128]{2,1,0:T(8,128)(2,1)}), bf16[32,128,128]{2,1,0:T(8,128)(2,1)S(1)}, u32[]{:S(2)}, u32[]{:S(2)}) async-start(bf16[32,128,128]{2,1,0:T(8,128)(2,1)} %shard_map.55), calls=%async_computation | async-start | bytes 2097152 | tf_op jit(solution)/shard_map/all_to_all | solution.py:396
  17.3 0.7 copy.8.pattern_ref
  18.0 1.8 %shard_map.56 = bf16[1536,128]{1,0:T(8,128)(2,1)} custom-call(s32[12,1]{1,0:T(8,128)} %copy.8.pattern_ref, bf16[1536,128]{1,0:T(8,128)(2,1)} %a_ref.1), custom_call_target="tpu_custom_call" | custom-call | flops 196608 | bytes 786432 | tf_op jit(solution)/shard_map/pallas_call | solution.py:72
  19.9 0.6 stack.115.where_ref
  20.5 0.6 stack.138.index_ref
  21.1 3.9 %shard_map.57 = (bf16[2,128,1024]{2,1,0:T(8,128)(2,1)}, bf16[2,128,1024]{2,1,0:T(8,128)(2,1)}, bf16[2,128,1024]{2,1,0:T(8,128)(2,1)}, bf16[2,128,1024]{2,1,0:T(8,128)(2,1)}, bf16[2,128,1024]{2,1,0:T(8,128)(2,1)}) custom-call(s32[10]{0:T(128)} %stack.115.where_ref, s32[1,256]{1,0:T(1,128)} %pattern_ref.4, bf16[128,32768]{1,0:T(8,128)(2,1)} %b_ref.3), custom_call_target="tpu_custom_call" | custom-call | flops 4194304 | bytes 8388608 | tf_op jit(solution)/shard_map/pallas_call | solution.py:135
  25.1 7.7 %all-to-all-done.r_ref = bf16[32,128,128]{2,1,0:T(8,128)(2,1)S(1)} async-done(((bf16[32,128,128]{2,1,0:T(8,128)(2,1)}), bf16[32,128,128]{2,1,0:T(8,128)(2,1)S(1)}, u32[]{:S(2)}, u32[]{:S(2)}) %all-to-all-start) | async-done | bytes 1048608 | tf_op jit(solution)/shard_map/all_to_all | solution.py:396
  32.8 1.0 copy-done.13
  33.8 2.2 %shard_map.58 = bf16[22,128,128]{2,1,0:T(8,128)(2,1)} custom-call(s32[22]{0:T(128)} %stack.138.index_ref, bf16[32,128,128]{2,1,0:T(8,128)(2,1)} %copy-done.13), custom_call_target="tpu_custom_call" | custom-call | bytes 2097152 | tf_op jit(solution)/shard_map/pallas_call | solution.py:156
  36.1 0.4 collective-permute-start
  36.5 2.9 %collective-permute-start.1 = (bf16[1536,128]{1,0:T(8,128)(2,1)S(1)}, bf16[1536,128]{1,0:T(8,128)(2,1)S(1)}, u32[]{:S(2)}, u32[]{:S(2)}) collective-permute-start(bf16[1536,128]{1,0:T(8,128)(2,1)S(1)} %copy-done.14), channel_id=1, source_target_pairs={{0,24},{1,7},{2,26},{3,1},{4,28},{5,3},{6,30},{7,5},{8,0},{9,15},{... | collective-permute-start | bytes 1179656 | tf_op jit(solution)/shard_map/ppermute | solution.py:41
  39.4 0.9 collective-permute-start.12
  40.2 2.4 %collective-permute-start.13 = (bf16[2,128,1024]{2,1,0:T(8,128)(2,1)}, bf16[2,128,1024]{2,1,0:T(8,128)(2,1)S(1)}, u32[]{:S(2)}, u32[]{:S(2)}) collective-permute-start(bf16[2,128,1024]{2,1,0:T(8,128)(2,1)} %get-tuple-element.42), channel_id=1, source_target_pairs={{0,24},{1,7},{2,26},{3,1},{4,28},{5,3},{6,30},{7,5},{8,0},{9,15},{... | collective-permute-start | bytes 1572872 | tf_op jit(solution)/shard_map/ppermute | solution.py:41
  42.6 0.8 constant_dynamic-update-slice_fusion.3
  43.4 5.2 %collective-permute-done = bf16[1536,128]{1,0:T(8,128)(2,1)S(1)} collective-permute-done((bf16[1536,128]{1,0:T(8,128)(2,1)S(1)}, bf16[1536,128]{1,0:T(8,128)(2,1)S(1)}, u32[]{:S(2)}, u32[]{:S(2)}) %collective-permute-start) | collective-permute-done | bytes 393248 | tf_op jit(solution)/shard_map/ppermute | solution.py:41
  48.6 0.6 collective-permute-start.14
  49.2 0.8 constant_dynamic-update-slice_fusion.2
  50.0 1.6 %collective-permute-start.15 = (bf16[2,128,1024]{2,1,0:T(8,128)(2,1)}, bf16[2,128,1024]{2,1,0:T(8,128)(2,1)S(1)}, u32[]{:S(2)}, u32[]{:S(2)}) collective-permute-start(bf16[2,128,1024]{2,1,0:T(8,128)(2,1)} %get-tuple-element.44), channel_id=1, source_target_pairs={{0,6},{1,25},{2,0},{3,27},{4,2},{5,29},{6,4},{7,31},{8,14},{9,1},{... | collective-permute-start | bytes 1572872 | tf_op jit(solution)/shard_map/ppermute | solution.py:41
  51.6 0.8 constant_dynamic-update-slice_fusion.1
  52.4 0.8 constant_dynamic-update-slice_fusion.refs_0_
  53.2 1.4 collective-permute-start.3
  54.5 6.3 %collective-permute-done.12.refs_11_ = bf16[2,128,1024]{2,1,0:T(8,128)(2,1)S(1)} collective-permute-done((bf16[2,128,1024]{2,1,0:T(8,128)(2,1)S(1)}, bf16[2,128,1024]{2,1,0:T(8,128)(2,1)S(1)}, u32[]{:S(2)}, u32[]{:S(2)}) %collective-permute-start.12) | collective-permute-done | bytes 524320 | tf_op jit(solution)/shard_map/ppermute | solution.py:41
  60.9 0.1 collective-permute-done.13.refs_12_
  61.1 1.0 copy-done.10
  62.1 0.5 collective-permute-start.7
  62.6 12.8 %collective-permute-done.3.refs_1_ = bf16[1536,512]{1,0:T(8,128)(2,1)S(1)} collective-permute-done((bf16[1536,512]{1,0:T(8,128)(2,1)}, bf16[1536,512]{1,0:T(8,128)(2,1)S(1)}, u32[]{:S(2)}, u32[]{:S(2)}) %collective-permute-start.3) | collective-permute-done | bytes 1572896 | tf_op jit(solution)/shard_map/ppermute | solution.py:41
  75.5 1.4 collective-permute-start.5
  76.9 4.6 %collective-permute-done.4.refs_2_ = bf16[1536,512]{1,0:T(8,128)(2,1)S(1)} collective-permute-done((bf16[1536,512]{1,0:T(8,128)(2,1)}, bf16[1536,512]{1,0:T(8,128)(2,1)S(1)}, u32[]{:S(2)}, u32[]{:S(2)}) %collective-permute-start.4) | collective-permute-done | bytes 1572896 | tf_op jit(solution)/shard_map/ppermute | solution.py:41
  81.6 0.9 collective-permute-start.6
  82.4 1.1 copy-done
  83.5 0.5 collective-permute-start.9
  84.0 4.5 %collective-permute-done.5.refs_3_ = bf16[768,512]{1,0:T(8,128)(2,1)} collective-permute-done((bf16[768,512]{1,0:T(8,128)(2,1)S(1)}, bf16[768,512]{1,0:T(8,128)(2,1)}, u32[]{:S(2)}, u32[]{:S(2)}) %collective-permute-start.5) | collective-permute-done | bytes 786464 | tf_op jit(solution)/shard_map/ppermute | solution.py:41
  88.5 1.7 %collective-permute-start.10 = (bf16[768,512]{1,0:T(8,128)(2,1)}, bf16[768,512]{1,0:T(8,128)(2,1)}, u32[]{:S(2)}, u32[]{:S(2)}) collective-permute-start(bf16[768,512]{1,0:T(8,128)(2,1)} %collective-permute-done.5.refs_3_), channel_id=1, source_target_pairs={{0,1},{1,0},{2,3},{3,2},{4,5},{5,4},{6,7},{7,6},{8,9},{9,8},{10,11... | collective-permute-start | bytes 2359304 | tf_op jit(solution)/shard_map/ppermute | solution.py:45
  90.2 3.5 %collective-permute-done.6.refs_4_ = bf16[768,512]{1,0:T(8,128)(2,1)} collective-permute-done((bf16[768,512]{1,0:T(8,128)(2,1)S(1)}, bf16[768,512]{1,0:T(8,128)(2,1)}, u32[]{:S(2)}, u32[]{:S(2)}) %collective-permute-start.6) | collective-permute-done | bytes 786464 | tf_op jit(solution)/shard_map/ppermute | solution.py:41
  93.7 0.1 copy.9.cpat_ref
  93.8 2.5 %collective-permute-done.11.refs_9_ = bf16[768,512]{1,0:T(8,128)(2,1)} collective-permute-done((bf16[768,512]{1,0:T(8,128)(2,1)}, bf16[768,512]{1,0:T(8,128)(2,1)}, u32[]{:S(2)}, u32[]{:S(2)}) %collective-permute-start.11) | collective-permute-done | bytes 786464 | tf_op jit(solution)/shard_map/ppermute | solution.py:45
  96.4 1.3 copy-done.1
  97.7 1.0 copy-done.3
  98.7 1.0 copy-done.5
  99.8 1.0 copy-done.7
  100.8 1.0 copy-done.9
  101.9 1.0 copy-done.11
  102.9 10.7 %shard_map.59 = (bf16[1536,2816]{1,0:T(8,128)(2,1)}, f32[1536,1024]{1,0:T(8,128)S(1)}) custom-call(bf16[1536,512]{1,0:T(8,128)(2,1)} %constant_dynamic-update-slice_fusion.refs_0_, bf16[1536,512]{1,0:T(8,128)(2,1)S(1)} %collective-permute-done.3.refs_1_, bf16[1536,512]{1,0:T(8,128)(2,1)S(1)} %collective-permute-done.4.refs_2_, ...), custom_call_target="tpu_custom_call" | custom-call | flops 4026531840 | bytes 33554432 | tf_op jit(solution)/shard_map/pallas_call | solution.py:318
  113.7 2.7 %copy-done.12 = f32[1536,1024]{1,0:T(8,128)} copy-done((f32[1536,1024]{1,0:T(8,128)}, f32[1536,1024]{1,0:T(8,128)S(1)}, u32[]{:S(2)}) %copy-start.12) | copy-done | bytes 6291480
  116.4 16.1 %shard_map.60 = (f32[1536,1024]{1,0:T(8,128)S(1)}, f32[8,8,128]{2,1,0:T(8,128)S(1)}) custom-call(s32[12,8]{1,0:T(8,128)S(1)} %copy.9.cpat_ref, bf16[1536,2816]{1,0:T(8,128)(2,1)} %get-tuple-element.45.left_in, f32[1536,1024]{1,0:T(8,128)} %copy-done.12, bf16[176,128,128]{2,1,0:T(8,128)(2,1)} %all-gather.2.cloned.1.call-done.fars), custom_call_target="tpu_custom_call" | custom-call | flops 8858370048 | bytes 25165824 | tf_op jit(solution)/shard_map/pallas_call | solution.py:345
  132.4 16.3 %all_to_all.10.t_ref = f32[8,8,128]{2,1,0:T(8,128)S(1)} all-to-all(f32[8,8,128]{2,1,0:T(8,128)S(1)} %get-tuple-element.47), channel_id=1, replica_groups=mesh['row'=8,'col'=32] {'row'}, dimensions={0} | all-to-all | bytes 65536 | tf_op jit(solution)/shard_map/all_to_all | solution.py:425
  148.7 3.0 %shard_map.61 = bf16[1536,1024]{1,0:T(8,128)(2,1)} custom-call(f32[8,8,128]{2,1,0:T(8,128)S(1)} %all_to_all.10.t_ref, f32[1536,1024]{1,0:T(8,128)S(1)} %get-tuple-element.48.i_ref), custom_call_target="tpu_custom_call" | custom-call | flops 3145728 | bytes 4194304 | tf_op jit(solution)/shard_map/pallas_call | solution.py:379
  (50 shorter events, 0.3 us)
Async XLA Ops:
  9.7 7.6 %copy-start.16 = (s32[12,1]{0,1:T(1,128)S(1)}, s32[12,1]{0,1:T(1,128)}, u32[]{:S(2)}) copy-start(s32[12,1]{0,1:T(1,128)} %param.7) | copy-start | bytes 148
  9.7 23.1 %all-to-all-start = ((bf16[32,128,128]{2,1,0:T(8,128)(2,1)}), bf16[32,128,128]{2,1,0:T(8,128)(2,1)S(1)}, u32[]{:S(2)}, u32[]{:S(2)}) async-start(bf16[32,128,128]{2,1,0:T(8,128)(2,1)} %shard_map.55), calls=%async_computation | async-start | bytes 2097152 | tf_op jit(solution)/shard_map/all_to_all | solution.py:396
  17.3 99.1 %all-gather.2.cloned.1.call-start = ((), (), s32[]{:S(2)}) async-start(), calls=%async_computation.2 | async-start | bytes 6488064 | tf_op jit(solution)/shard_map/all_gather | solution.py:413
  25.1 11.0 %copy-start.14 = (bf16[1536,128]{1,0:T(8,128)(2,1)S(1)}, bf16[1536,128]{1,0:T(8,128)(2,1)}, u32[]{:S(2)}) copy-start(bf16[1536,128]{1,0:T(8,128)(2,1)} %shard_map.56) | copy-start | bytes 1179652
  25.1 14.3 %copy-start.17 = (bf16[2,128,1024]{2,1,0:T(8,128)(2,1)S(1)}, bf16[2,128,1024]{2,1,0:T(8,128)(2,1)}, u32[]{:S(2)}) copy-start(bf16[2,128,1024]{2,1,0:T(8,128)(2,1)} %get-tuple-element.41) | copy-start | bytes 1572868
  32.8 1.0 copy-start.13
  33.8 9.6 %copy-start.2 = (bf16[2,128,1024]{2,1,0:T(8,128)(2,1)S(1)}, bf16[2,128,1024]{2,1,0:T(8,128)(2,1)}, u32[]{:S(2)}) copy-start(bf16[2,128,1024]{2,1,0:T(8,128)(2,1)} %get-tuple-element.40.refs_10_) | copy-start | bytes 1572868
  36.1 12.5 %collective-permute-start = (bf16[1536,128]{1,0:T(8,128)(2,1)S(1)}, bf16[1536,128]{1,0:T(8,128)(2,1)S(1)}, u32[]{:S(2)}, u32[]{:S(2)}) collective-permute-start(bf16[1536,128]{1,0:T(8,128)(2,1)S(1)} %copy-done.14), channel_id=1, source_target_pairs={{0,8},{1,3},{2,10},{3,5},{4,12},{5,7},{6,14},{7,1},{8,16},{9,11},{... | collective-permute-start | bytes 1179656 | tf_op jit(solution)/shard_map/ppermute | solution.py:41
  36.5 13.5 %collective-permute-start.1 = (bf16[1536,128]{1,0:T(8,128)(2,1)S(1)}, bf16[1536,128]{1,0:T(8,128)(2,1)S(1)}, u32[]{:S(2)}, u32[]{:S(2)}) collective-permute-start(bf16[1536,128]{1,0:T(8,128)(2,1)S(1)} %copy-done.14), channel_id=1, source_target_pairs={{0,24},{1,7},{2,26},{3,1},{4,28},{5,3},{6,30},{7,5},{8,0},{9,15},{... | collective-permute-start | bytes 1179656 | tf_op jit(solution)/shard_map/ppermute | solution.py:41
  39.4 13.0 %collective-permute-start.2 = (bf16[1536,128]{1,0:T(8,128)(2,1)S(1)}, bf16[1536,128]{1,0:T(8,128)(2,1)S(1)}, u32[]{:S(2)}, u32[]{:S(2)}) collective-permute-start(bf16[1536,128]{1,0:T(8,128)(2,1)S(1)} %copy-done.14), channel_id=1, source_target_pairs={{0,16},{1,5},{2,18},{3,7},{4,20},{5,1},{6,22},{7,3},{8,24},{9,13},... | collective-permute-start | bytes 1179656 | tf_op jit(solution)/shard_map/ppermute | solution.py:41
  39.4 21.5 %collective-permute-start.12 = (bf16[2,128,1024]{2,1,0:T(8,128)(2,1)S(1)}, bf16[2,128,1024]{2,1,0:T(8,128)(2,1)S(1)}, u32[]{:S(2)}, u32[]{:S(2)}) collective-permute-start(bf16[2,128,1024]{2,1,0:T(8,128)(2,1)S(1)} %copy-done.17), channel_id=1, source_target_pairs={{0,8},{1,3},{2,10},{3,5},{4,12},{5,7},{6,14},{7,1},{8,16},{9,11},{... | collective-permute-start | bytes 1572872 | tf_op jit(solution)/shard_map/ppermute | solution.py:41
  40.2 20.8 %collective-permute-start.13 = (bf16[2,128,1024]{2,1,0:T(8,128)(2,1)}, bf16[2,128,1024]{2,1,0:T(8,128)(2,1)S(1)}, u32[]{:S(2)}, u32[]{:S(2)}) collective-permute-start(bf16[2,128,1024]{2,1,0:T(8,128)(2,1)} %get-tuple-element.42), channel_id=1, source_target_pairs={{0,24},{1,7},{2,26},{3,1},{4,28},{5,3},{6,30},{7,5},{8,0},{9,15},{... | collective-permute-start | bytes 1572872 | tf_op jit(solution)/shard_map/ppermute | solution.py:41
  48.6 12.4 %collective-permute-start.14 = (bf16[2,128,1024]{2,1,0:T(8,128)(2,1)}, bf16[2,128,1024]{2,1,0:T(8,128)(2,1)S(1)}, u32[]{:S(2)}, u32[]{:S(2)}) collective-permute-start(bf16[2,128,1024]{2,1,0:T(8,128)(2,1)} %get-tuple-element.43), channel_id=1, source_target_pairs={{0,2},{1,9},{2,4},{3,11},{4,6},{5,13},{6,0},{7,15},{8,10},{9,17},{... | collective-permute-start | bytes 1572872 | tf_op jit(solution)/shard_map/ppermute | solution.py:41
  50.0 11.1 %collective-permute-start.15 = (bf16[2,128,1024]{2,1,0:T(8,128)(2,1)}, bf16[2,128,1024]{2,1,0:T(8,128)(2,1)S(1)}, u32[]{:S(2)}, u32[]{:S(2)}) collective-permute-start(bf16[2,128,1024]{2,1,0:T(8,128)(2,1)} %get-tuple-element.44), channel_id=1, source_target_pairs={{0,6},{1,25},{2,0},{3,27},{4,2},{5,29},{6,4},{7,31},{8,14},{9,1},{... | collective-permute-start | bytes 1572872 | tf_op jit(solution)/shard_map/ppermute | solution.py:41
  53.2 22.3 %collective-permute-start.3 = (bf16[1536,512]{1,0:T(8,128)(2,1)}, bf16[1536,512]{1,0:T(8,128)(2,1)S(1)}, u32[]{:S(2)}, u32[]{:S(2)}) collective-permute-start(bf16[1536,512]{1,0:T(8,128)(2,1)} %constant_dynamic-update-slice_fusion.refs_0_), channel_id=1, source_target_pairs={{0,2},{1,9},{2,4},{3,11},{4,6},{5,13},{6,0},{7,15},{8,10},{9,17},{... | collective-permute-start | bytes 4718600 | tf_op jit(solution)/shard_map/ppermute | solution.py:41
  60.9 1.2 copy-start.4
  60.9 20.6 %collective-permute-start.4 = (bf16[1536,512]{1,0:T(8,128)(2,1)}, bf16[1536,512]{1,0:T(8,128)(2,1)S(1)}, u32[]{:S(2)}, u32[]{:S(2)}) collective-permute-start(bf16[1536,512]{1,0:T(8,128)(2,1)} %constant_dynamic-update-slice_fusion.refs_0_), channel_id=1, source_target_pairs={{0,6},{1,25},{2,0},{3,27},{4,2},{5,29},{6,4},{7,31},{8,14},{9,1},{... | collective-permute-start | bytes 4718600 | tf_op jit(solution)/shard_map/ppermute | solution.py:41
  61.0 1.6 %copy-start.6 = (bf16[2,128,1024]{2,1,0:T(8,128)(2,1)}, bf16[2,128,1024]{2,1,0:T(8,128)(2,1)S(1)}, u32[]{:S(2)}) copy-start(bf16[2,128,1024]{2,1,0:T(8,128)(2,1)S(1)} %collective-permute-done.13.refs_12_) | copy-start | bytes 1572868
  61.0 1.6 copy-start.8
  61.1 1.0 copy-start.10
  62.1 31.7 %copy-start.15 = (s32[12,8]{0,1:T(8,128)S(1)}, s32[12,8]{0,1:T(8,128)}, u32[]{:S(2)}) copy-start(s32[12,8]{0,1:T(8,128)} %param.9) | copy-start | bytes 1156
  62.1 20.4 %collective-permute-start.16 = (bf16[5,128,1024]{2,1,0:T(8,128)(2,1)S(1)}, bf16[5,128,1024]{2,1,0:T(8,128)(2,1)S(1)}, u32[]{:S(2)}, u32[]{:S(2)}) collective-permute-start(bf16[5,128,1024]{2,1,0:T(8,128)(2,1)S(1)} %slice_dynamic-update-slice_fusion), channel_id=1, source_target_pairs={{0,1},{1,0},{2,3},{3,2},{4,5},{5,4},{6,7},{7,6},{8,9},{9,8},{10,11... | collective-permute-start | bytes 3932168 | tf_op jit(solution)/shard_map/ppermute | solution.py:45
  62.1 31.7 %collective-permute-start.7 = (bf16[1536,512]{1,0:T(8,128)(2,1)}, bf16[1536,512]{1,0:T(8,128)(2,1)}, u32[]{:S(2)}, u32[]{:S(2)}) collective-permute-start(bf16[1536,512]{1,0:T(8,128)(2,1)} %constant_dynamic-update-slice_fusion.refs_0_), channel_id=1, source_target_pairs={{0,1},{1,0},{2,3},{3,2},{4,5},{5,4},{6,7},{7,6},{8,9},{9,8},{10,11... | collective-permute-start | bytes 4718600 | tf_op jit(solution)/shard_map/ppermute | solution.py:45
  75.5 13.1 %collective-permute-start.5 = (bf16[768,512]{1,0:T(8,128)(2,1)S(1)}, bf16[768,512]{1,0:T(8,128)(2,1)}, u32[]{:S(2)}, u32[]{:S(2)}) collective-permute-start(bf16[768,512]{1,0:T(8,128)(2,1)S(1)} %slice.28), channel_id=1, source_target_pairs={{0,2},{1,9},{2,4},{3,11},{4,6},{5,13},{6,0},{7,15},{8,10},{9,17},{... | collective-permute-start | bytes 2359304 | tf_op jit(solution)/shard_map/ppermute | solution.py:41
  81.6 12.2 %collective-permute-start.6 = (bf16[768,512]{1,0:T(8,128)(2,1)S(1)}, bf16[768,512]{1,0:T(8,128)(2,1)}, u32[]{:S(2)}, u32[]{:S(2)}) collective-permute-start(bf16[768,512]{1,0:T(8,128)(2,1)S(1)} %slice.29), channel_id=1, source_target_pairs={{0,6},{1,25},{2,0},{3,27},{4,2},{5,29},{6,4},{7,31},{8,14},{9,1},{... | collective-permute-start | bytes 2359304 | tf_op jit(solution)/shard_map/ppermute | solution.py:41
  82.4 13.9 %collective-permute-start.8 = (bf16[1536,512]{1,0:T(8,128)(2,1)S(1)}, bf16[1536,512]{1,0:T(8,128)(2,1)}, u32[]{:S(2)}, u32[]{:S(2)}) collective-permute-start(bf16[1536,512]{1,0:T(8,128)(2,1)S(1)} %collective-permute-done.3.refs_1_), channel_id=1, source_target_pairs={{0,1},{1,0},{2,3},{3,2},{4,5},{5,4},{6,7},{7,6},{8,9},{9,8},{10,11... | collective-permute-start | bytes 4718600 | tf_op jit(solution)/shard_map/ppermute | solution.py:45
  82.4 1.1 copy-start
  83.5 12.9 %collective-permute-start.9 = (bf16[1536,512]{1,0:T(8,128)(2,1)S(1)}, bf16[1536,512]{1,0:T(8,128)(2,1)}, u32[]{:S(2)}, u32[]{:S(2)}) collective-permute-start(bf16[1536,512]{1,0:T(8,128)(2,1)S(1)} %collective-permute-done.4.refs_2_), channel_id=1, source_target_pairs={{0,1},{1,0},{2,3},{3,2},{4,5},{5,4},{6,7},{7,6},{8,9},{9,8},{10,11... | collective-permute-start | bytes 4718600 | tf_op jit(solution)/shard_map/ppermute | solution.py:45
  88.5 5.3 %collective-permute-start.10 = (bf16[768,512]{1,0:T(8,128)(2,1)}, bf16[768,512]{1,0:T(8,128)(2,1)}, u32[]{:S(2)}, u32[]{:S(2)}) collective-permute-start(bf16[768,512]{1,0:T(8,128)(2,1)} %collective-permute-done.5.refs_3_), channel_id=1, source_target_pairs={{0,1},{1,0},{2,3},{3,2},{4,5},{5,4},{6,7},{7,6},{8,9},{9,8},{10,11... | collective-permute-start | bytes 2359304 | tf_op jit(solution)/shard_map/ppermute | solution.py:45
  93.7 2.6 %collective-permute-start.11 = (bf16[768,512]{1,0:T(8,128)(2,1)}, bf16[768,512]{1,0:T(8,128)(2,1)}, u32[]{:S(2)}, u32[]{:S(2)}) collective-permute-start(bf16[768,512]{1,0:T(8,128)(2,1)} %collective-permute-done.6.refs_4_), channel_id=1, source_target_pairs={{0,1},{1,0},{2,3},{3,2},{4,5},{5,4},{6,7},{7,6},{8,9},{9,8},{10,11... | collective-permute-start | bytes 2359304 | tf_op jit(solution)/shard_map/ppermute | solution.py:45
  96.4 1.3 copy-start.1
  97.7 1.0 copy-start.3
  98.7 1.1 copy-start.5
  99.8 1.0 copy-start.7
  100.8 1.0 copy-start.9
  101.9 1.0 copy-start.11
  113.7 2.7 %copy-start.12 = (f32[1536,1024]{1,0:T(8,128)}, f32[1536,1024]{1,0:T(8,128)S(1)}, u32[]{:S(2)}) copy-start(f32[1536,1024]{1,0:T(8,128)S(1)} %get-tuple-element.46.sum_in) | copy-start | bytes 18874372
Sparse Core Ops, SparseCore 0:
  36.2 70.2 all-gather.1

commit v3 on v2

--- a/solution.py
+++ b/solution.py
@@ -59,6 +59,18 @@
 
 def params():
     return pltpu.CompilerParams(vmem_limit_bytes=56 * 1024 * 1024)
+
+
+def held(value):
+    return pltpu.with_memory_space_constraint(value, pltpu.VMEM)
+
+
+def outside(value):
+    return pltpu.with_memory_space_constraint(value, pltpu.HBM)
+
+
+def limit(size):
+    return pltpu.CompilerParams(vmem_limit_bytes=size << 20)
 
 
 def mask_left_kernel(pattern_ref, a_ref, o_ref):
@@ -160,19 +172,11 @@
         out_specs=vmem(),
         compiler_params=params(),
         cost_estimate=pl.CostEstimate(flops=0, bytes_accessed=2 << 20, transcendentals=0),
-    )(index, pltpu.with_memory_space_constraint(received, pltpu.HBM))
-
-
-CHUNK, TILE = 384, 512
+    )(index, held(received))
+
+
+CHUNK = 384
 HALF = 768
-
-
-def held(value):
-    return pltpu.with_memory_space_constraint(value, pltpu.VMEM)
-
-
-def limit(size):
-    return pltpu.CompilerParams(vmem_limit_bytes=size << 20)
 
 
 def runs(o, d):
@@ -189,12 +193,24 @@
     return found
 
 
-def near_kernel(*refs):
+def pairs_of(fars, far, sems):
+    sources = 2 * len(FAR)
+    return [
+        pltpu.make_async_copy(
+            fars.at[pl.ds(n * sources, sources)],
+            far.at[n // 2, :, :, pl.ds(n % 2 * BLOCK, BLOCK)],
+            sems.at[n],
+        )
+        for n in range(ROWS)
+    ]
+
+
+def first_kernel(*refs):
     refs = list(refs)
     lefts = [refs.pop(0) for _ in range(10)]
     nears = [refs.pop(0) for _ in range(len(NEAR) + 1)]
     left_out, o_ref, left, piece, near, out, nsem, lsem, osem = refs
-    rows, count, depth = o_ref.shape[0], len(NEAR), left_out.shape[1]
+    rows, count, depth = o_ref.shape[0], len(NEAR), 2 * len(FAR) * BLOCK
 
     whole = [pltpu.make_async_copy(nears[k].at[0], near.at[k], nsem.at[k]) for k in range(count)]
     whole.append(pltpu.make_async_copy(nears[count], near.at[pl.ds(count, count)], nsem.at[count]))
@@ -248,17 +264,9 @@
             copy.wait()
 
 
-def far_kernel(cpat_ref, left_in, sum_in, fars, o_ref, t_ref, left, partial, far, fsem, lsem):
-    rows, sources = o_ref.shape[0], 2 * len(FAR)
-    depth = sources * BLOCK
-    blocks = [
-        pltpu.make_async_copy(
-            fars.at[pl.ds(n * sources, sources)],
-            far.at[n // 2, :, :, pl.ds(n % 2 * BLOCK, BLOCK)],
-            fsem.at[n],
-        )
-        for n in range(ROWS)
-    ]
+def second_kernel(cpat_ref, left_in, sum_in, fars, o_ref, t_ref, left, partial, far, fsem, lsem):
+    rows, depth = o_ref.shape[0], 2 * len(FAR) * BLOCK
+    blocks = pairs_of(fars, far, fsem)
     parts = []
     for i in range(rows // CHUNK):
         here = pl.ds(i * CHUNK, CHUNK)
@@ -266,42 +274,32 @@
             pltpu.make_async_copy(left_in.at[here, :], left.at[here, :], lsem.at[2 * i]),
             pltpu.make_async_copy(sum_in.at[here, :], partial.at[here, :], lsem.at[2 * i + 1]),
         ])
-    for group in (blocks[:2], parts[0], blocks[2:4], *parts[1:], blocks[4:]):
+    for group in (blocks[:2], parts[0], blocks[2:], *parts[1:]):
         for copy in group:
             copy.start()
     sums = [jnp.zeros((1, BLOCK), F32) for _ in range(ROWS)]
-
-    def multiply(pair, start, size):
-        product = jnp.dot(
-            left[start:start + size, :], far[pair].reshape(depth, 2 * BLOCK), preferred_element_type=F32
-        )
-        for n in range(2):
-            lanes = slice(n * BLOCK, (n + 1) * BLOCK)
-            column = 2 * pair + n
-            target = slice(column * BLOCK, (column + 1) * BLOCK)
-            for j in range(size // BLOCK):
-                keep = cpat_ref[start // BLOCK + j, column] != 0
-                place = slice(start + j * BLOCK, start + (j + 1) * BLOCK)
-                block = product[j * BLOCK:(j + 1) * BLOCK, lanes] + partial[place, target]
-                block = jnp.where(keep, block * block, jnp.zeros_like(block))
-                o_ref[place, target] = block
-                sums[column] = sums[column] + jnp.sum(block, axis=0, keepdims=True)
-
-    for copy in blocks[:2]:
-        copy.wait()
     for i, part in enumerate(parts):
+        start, stop = i * CHUNK, (i + 1) * CHUNK
         for copy in part:
             copy.wait()
-        multiply(0, i * CHUNK, CHUNK)
-        if i == 0:
-            for copy in blocks[2:4]:
-                copy.wait()
-        multiply(1, i * CHUNK, CHUNK)
-    for pair in (2, 3):
-        for copy in blocks[2 * pair:2 * pair + 2]:
-            copy.wait()
-        for start in range(0, rows, TILE):
-            multiply(pair, start, TILE)
+        for pair in range(ROWS // 2):
+            if i == 0:
+                for copy in blocks[2 * pair:2 * pair + 2]:
+                    copy.wait()
+            product = jnp.dot(
+                left[start:stop, :], far[pair].reshape(depth, 2 * BLOCK), preferred_element_type=F32
+            )
+            for n in range(2):
+                lanes = slice(n * BLOCK, (n + 1) * BLOCK)
+                column = 2 * pair + n
+                target = slice(column * BLOCK, (column + 1) * BLOCK)
+                for j in range(CHUNK // BLOCK):
+                    keep = cpat_ref[start // BLOCK + j, column] != 0
+                    place = slice(start + j * BLOCK, start + (j + 1) * BLOCK)
+                    block = product[j * BLOCK:(j + 1) * BLOCK, lanes] + partial[place, target]
+                    block = jnp.where(keep, block * block, jnp.zeros_like(block))
+                    o_ref[place, target] = block
+                    sums[column] = sums[column] + jnp.sum(block, axis=0, keepdims=True)
     for r in range(ROWS):
         for n in range(ROWS):
             t_ref[r, n:n + 1, :] = sums[n]
@@ -313,14 +311,11 @@
     )
 
 
-def near_product(lefts, nears):
-    rows = 2 * HALF
-    return pl.pallas_call(
-        near_kernel,
-        out_shape=[
-            jax.ShapeDtypeStruct((rows, 2 * len(FAR) * BLOCK), BF16),
-            jax.ShapeDtypeStruct((rows, ROWS * BLOCK), F32),
-        ],
+def first_product(lefts, nears):
+    rows, sources = 2 * HALF, 2 * len(FAR)
+    return pl.pallas_call(
+        first_kernel,
+        out_shape=[pltpu.HBM((rows, sources * BLOCK), BF16), pltpu.HBM((rows, ROWS * BLOCK), F32)],
         in_specs=[any_space()] * (len(lefts) + len(nears)),
         out_specs=[any_space()] * 2,
         scratch_shapes=[
@@ -334,16 +329,13 @@
         ],
         compiler_params=limit(24),
         cost_estimate=cost(rows, 2 * len(NEAR), 32),
-    )(*lefts, *nears)
-
-
-def far_product(cpat, left, partial, fars):
+    )(*lefts, *[outside(array) for array in nears])
+
+
+def second_product(cpat, left, partial, fars):
     rows, depth = left.shape
-    left, partial, fars = [
-        pltpu.with_memory_space_constraint(array, pltpu.HBM) for array in (left, partial, fars)
-    ]
-    return pl.pallas_call(
-        far_kernel,
+    return pl.pallas_call(
+        second_kernel,
         out_shape=[
             pltpu.VMEM((rows, ROWS * BLOCK), F32),
             jax.ShapeDtypeStruct((ROWS, ROWS, BLOCK), F32),
@@ -359,7 +351,7 @@
         ],
         compiler_params=limit(32),
         cost_estimate=cost(rows, 2 * len(FAR), 24),
-    )(cpat, left, partial, fars)
+    )(cpat, outside(left), outside(partial), outside(fars))
 
 
 def rescale_kernel(count, t_ref, i_ref, o_ref):
@@ -420,8 +412,8 @@
     nears = [near[0]] + [shift(piece, *step) for piece, step in zip(near[1:], steps[1:])]
     nears.append(swap(jnp.stack([piece[1] for piece in nears])))
 
-    left, partial = near_product(lefts, nears)
-    inflated, totals = far_product(c_pattern, left, partial, fars)
+    left, partial = first_product(lefts, nears)
+    inflated, totals = second_product(c_pattern, left, partial, fars)
     gathered = lax.all_to_all(totals, "row", split_axis=0, concat_axis=0, tiled=True)
     return rescale(gathered, inflated)
 

time: 161 us -> 151 us (0.938)
  local copies, waits for them, and re-layouts: 17.6 us -> 6.29 us
    unnamed x45 -> x29, local copies, waits for them, and re-layouts: 15.4 us -> 4.15 us
  transfers between devices with their start and end apart: 19 -> 19, of which waited for: 9 -> 9; matrix products, arithmetic and copies ran while one was open for 3% -> 4% of each run, Pallas kernels for 10% -> 12%
where the time goes in v3:
time: 151 us; the launch traced here: 148 us
  waiting for transfers between devices  48.3 us (32%)
  Pallas kernels  41.1 us (27%)
  starting transfers between devices  22.9 us (15%)
  blocking collectives  16.2 us (11%)
  between operations  13.6 us (9%)
  local copies, waits for them, and re-layouts  6.29 us (4%)
    ppermute x11, waiting for transfers between devices, shift(): return lax.ppermute(value, 'col', pairs)  38 us
    all_to_all x1, blocking collectives, shards(): lax.all_to_all(totals, 'row', split_axis=0, concat_axis=0, tiled=True)  16.2 us
    pallas_call x1, Pallas kernels, second_product(): pl.pallas_call(second_kernel, out_shape=[pltpu.VMEM((rows, ROWS * BLOCK),...  15.8 us
    ppermute x11, starting transfers between devices, shift(): return lax.ppermute(value, 'col', pairs)  12.5 us
    pallas_call x1, Pallas kernels, first_product(): pl.pallas_call(first_kernel, out_shape=[pltpu.HBM((rows, sources * BLOCK)...  11.6 us
    all_to_all x1, waiting for transfers between devices, shards(): lax.all_to_all(sent, 'col', split_axis=0, concat_axis=0, tiled=True)  7.71 us
    all_to_all x1, starting transfers between devices, shards(): lax.all_to_all(sent, 'col', split_axis=0, concat_axis=0, tiled=True)  7.54 us
    unnamed x29, local copies, waits for them, and re-layouts  4.15 us
  transfers between devices with their start and end apart: 19, of which 9 were waited for; matrix products, arithmetic and copies ran while one was open for 4% of the time, Pallas kernels for 12%

profile of v3, /device:TPU:8, one launch (start us, length us, event | category | flops | bytes accessed | tf_op | source)
XLA Modules:
  0.0 148.4 jit_solution(2088417858395676021)
XLA Ops:
  6.5 3.1 %shard_map.55 = bf16[32,128,128]{2,1,0:T(8,128)(2,1)} custom-call(s32[1]{0:T(128)} %bitcast.row_ref, s32[1,256]{1,0:T(1,128)} %pattern_ref.4, bf16[128,32768]{1,0:T(8,128)(2,1)} %b_ref.3), custom_call_target="tpu_custom_call" | custom-call | flops 1048576 | bytes 2097152 | tf_op jit(solution)/shard_map/pallas_call | solution.py:112
  9.7 0.0 copy-start.8
  9.7 7.5 %all-to-all-start = ((bf16[32,128,128]{2,1,0:T(8,128)(2,1)}), bf16[32,128,128]{2,1,0:T(8,128)(2,1)S(1)}, u32[]{:S(2)}, u32[]{:S(2)}) async-start(bf16[32,128,128]{2,1,0:T(8,128)(2,1)} %shard_map.55), calls=%async_computation | async-start | bytes 2097152 | tf_op jit(solution)/shard_map/all_to_all | solution.py:388
  17.3 0.0 all-gather.2.cloned.1.call-start
  17.3 0.7 copy.8.pattern_ref
  18.0 1.9 %shard_map.56 = bf16[1536,128]{1,0:T(8,128)(2,1)} custom-call(s32[12,1]{1,0:T(8,128)} %copy.8.pattern_ref, bf16[1536,128]{1,0:T(8,128)(2,1)} %a_ref.1), custom_call_target="tpu_custom_call" | custom-call | flops 196608 | bytes 786432 | tf_op jit(solution)/shard_map/pallas_call | solution.py:84
  19.9 0.6 stack.115.where_ref
  20.5 0.6 stack.138.index_ref
  21.1 4.0 %shard_map.57 = (bf16[2,128,1024]{2,1,0:T(8,128)(2,1)}, bf16[2,128,1024]{2,1,0:T(8,128)(2,1)}, bf16[2,128,1024]{2,1,0:T(8,128)(2,1)}, bf16[2,128,1024]{2,1,0:T(8,128)(2,1)}, bf16[2,128,1024]{2,1,0:T(8,128)(2,1)}) custom-call(s32[10]{0:T(128)} %stack.115.where_ref, s32[1,256]{1,0:T(1,128)} %pattern_ref.4, bf16[128,32768]{1,0:T(8,128)(2,1)} %b_ref.3), custom_call_target="tpu_custom_call" | custom-call | flops 4194304 | bytes 8388608 | tf_op jit(solution)/shard_map/pallas_call | solution.py:147
  25.1 7.7 %all-to-all-done.r_ref = bf16[32,128,128]{2,1,0:T(8,128)(2,1)S(1)} async-done(((bf16[32,128,128]{2,1,0:T(8,128)(2,1)}), bf16[32,128,128]{2,1,0:T(8,128)(2,1)S(1)}, u32[]{:S(2)}, u32[]{:S(2)}) %all-to-all-start) | async-done | bytes 1048608 | tf_op jit(solution)/shard_map/all_to_all | solution.py:388
  32.8 1.7 %shard_map.58 = bf16[22,128,128]{2,1,0:T(8,128)(2,1)} custom-call(s32[22]{0:T(128)} %stack.138.index_ref, bf16[32,128,128]{2,1,0:T(8,128)(2,1)S(1)} %all-to-all-done.r_ref), custom_call_target="tpu_custom_call" | custom-call | bytes 2097152 | tf_op jit(solution)/shard_map/pallas_call | solution.py:168
  34.5 0.0 all-gather.2.cloned.1.call-update
  34.6 0.4 collective-permute-start
  35.0 2.9 %collective-permute-start.1 = (bf16[1536,128]{1,0:T(8,128)(2,1)S(1)}, bf16[1536,128]{1,0:T(8,128)(2,1)S(1)}, u32[]{:S(2)}, u32[]{:S(2)}) collective-permute-start(bf16[1536,128]{1,0:T(8,128)(2,1)S(1)} %copy-done), channel_id=1, source_target_pairs={{0,24},{1,7},{2,26},{3,1},{4,28},{5,3},{6,30},{7,5},{8,0},{9,15},{... | collective-permute-start | bytes 1179656 | tf_op jit(solution)/shard_map/ppermute | solution.py:41
  37.9 0.9 collective-permute-start.12
  38.7 2.4 %collective-permute-start.13 = (bf16[2,128,1024]{2,1,0:T(8,128)(2,1)}, bf16[2,128,1024]{2,1,0:T(8,128)(2,1)S(1)}, u32[]{:S(2)}, u32[]{:S(2)}) collective-permute-start(bf16[2,128,1024]{2,1,0:T(8,128)(2,1)} %get-tuple-element.42), channel_id=1, source_target_pairs={{0,24},{1,7},{2,26},{3,1},{4,28},{5,3},{6,30},{7,5},{8,0},{9,15},{... | collective-permute-start | bytes 1572872 | tf_op jit(solution)/shard_map/ppermute | solution.py:41
  41.1 0.8 constant_dynamic-update-slice_fusion.3
  41.9 5.2 %collective-permute-done = bf16[1536,128]{1,0:T(8,128)(2,1)S(1)} collective-permute-done((bf16[1536,128]{1,0:T(8,128)(2,1)S(1)}, bf16[1536,128]{1,0:T(8,128)(2,1)S(1)}, u32[]{:S(2)}, u32[]{:S(2)}) %collective-permute-start) | collective-permute-done | bytes 393248 | tf_op jit(solution)/shard_map/ppermute | solution.py:41
  47.1 0.6 collective-permute-start.14
  47.7 0.8 constant_dynamic-update-slice_fusion.2
  48.5 1.6 %collective-permute-start.15 = (bf16[2,128,1024]{2,1,0:T(8,128)(2,1)}, bf16[2,128,1024]{2,1,0:T(8,128)(2,1)S(1)}, u32[]{:S(2)}, u32[]{:S(2)}) collective-permute-start(bf16[2,128,1024]{2,1,0:T(8,128)(2,1)} %get-tuple-element.44), channel_id=1, source_target_pairs={{0,6},{1,25},{2,0},{3,27},{4,2},{5,29},{6,4},{7,31},{8,14},{9,1},{... | collective-permute-start | bytes 1572872 | tf_op jit(solution)/shard_map/ppermute | solution.py:41
  50.1 0.8 constant_dynamic-update-slice_fusion.1
  50.9 0.8 constant_dynamic-update-slice_fusion.refs_0_
  51.7 1.4 collective-permute-start.3
  53.0 6.3 %collective-permute-done.12.refs_11_ = bf16[2,128,1024]{2,1,0:T(8,128)(2,1)S(1)} collective-permute-done((bf16[2,128,1024]{2,1,0:T(8,128)(2,1)S(1)}, bf16[2,128,1024]{2,1,0:T(8,128)(2,1)S(1)}, u32[]{:S(2)}, u32[]{:S(2)}) %collective-permute-start.12) | collective-permute-done | bytes 524320 | tf_op jit(solution)/shard_map/ppermute | solution.py:41
  59.4 0.1 collective-permute-done.13.refs_12_
  59.6 1.0 copy-done.6
  60.6 0.0 copy-start.7
  60.6 0.1 collective-permute-start.16
  60.7 0.5 collective-permute-start.7
  61.2 12.7 %collective-permute-done.3.refs_1_ = bf16[1536,512]{1,0:T(8,128)(2,1)S(1)} collective-permute-done((bf16[1536,512]{1,0:T(8,128)(2,1)}, bf16[1536,512]{1,0:T(8,128)(2,1)S(1)}, u32[]{:S(2)}, u32[]{:S(2)}) %collective-permute-start.3) | collective-permute-done | bytes 1572896 | tf_op jit(solution)/shard_map/ppermute | solution.py:41
  73.9 0.1 slice.28
  74.0 1.4 collective-permute-start.5
  75.4 4.6 %collective-permute-done.4.refs_2_ = bf16[1536,512]{1,0:T(8,128)(2,1)S(1)} collective-permute-done((bf16[1536,512]{1,0:T(8,128)(2,1)}, bf16[1536,512]{1,0:T(8,128)(2,1)S(1)}, u32[]{:S(2)}, u32[]{:S(2)}) %collective-permute-start.4) | collective-permute-done | bytes 1572896 | tf_op jit(solution)/shard_map/ppermute | solution.py:41
  80.0 0.1 slice.29
  80.1 0.9 collective-permute-start.6
  80.9 0.0 collective-permute-start.8
  80.9 0.5 collective-permute-start.9
  81.4 5.6 %collective-permute-done.5.refs_3_ = bf16[768,512]{1,0:T(8,128)(2,1)} collective-permute-done((bf16[768,512]{1,0:T(8,128)(2,1)S(1)}, bf16[768,512]{1,0:T(8,128)(2,1)}, u32[]{:S(2)}, u32[]{:S(2)}) %collective-permute-start.5) | collective-permute-done | bytes 786464 | tf_op jit(solution)/shard_map/ppermute | solution.py:41
  87.0 1.7 %collective-permute-start.10 = (bf16[768,512]{1,0:T(8,128)(2,1)}, bf16[768,512]{1,0:T(8,128)(2,1)}, u32[]{:S(2)}, u32[]{:S(2)}) collective-permute-start(bf16[768,512]{1,0:T(8,128)(2,1)} %collective-permute-done.5.refs_3_), channel_id=1, source_target_pairs={{0,1},{1,0},{2,3},{3,2},{4,5},{5,4},{6,7},{7,6},{8,9},{9,8},{10,11... | collective-permute-start | bytes 2359304 | tf_op jit(solution)/shard_map/ppermute | solution.py:45
  88.7 3.5 %collective-permute-done.6.refs_4_ = bf16[768,512]{1,0:T(8,128)(2,1)} collective-permute-done((bf16[768,512]{1,0:T(8,128)(2,1)S(1)}, bf16[768,512]{1,0:T(8,128)(2,1)}, u32[]{:S(2)}, u32[]{:S(2)}) %collective-permute-start.6) | collective-permute-done | bytes 786464 | tf_op jit(solution)/shard_map/ppermute | solution.py:41
  92.2 0.1 copy.9.cpat_ref
  92.3 2.5 %collective-permute-done.11.refs_9_ = bf16[768,512]{1,0:T(8,128)(2,1)} collective-permute-done((bf16[768,512]{1,0:T(8,128)(2,1)}, bf16[768,512]{1,0:T(8,128)(2,1)}, u32[]{:S(2)}, u32[]{:S(2)}) %collective-permute-start.11) | collective-permute-done | bytes 786464 | tf_op jit(solution)/shard_map/ppermute | solution.py:45
  94.9 11.6 %shard_map.59 = (bf16[1536,2816]{1,0:T(8,128)(2,1)}, f32[1536,1024]{1,0:T(8,128)}) custom-call(bf16[1536,512]{1,0:T(8,128)(2,1)} %constant_dynamic-update-slice_fusion.refs_0_, bf16[1536,512]{1,0:T(8,128)(2,1)S(1)} %collective-permute-done.3.refs_1_, bf16[1536,512]{1,0:T(8,128)(2,1)S(1)} %collective-permute-done.4.refs_2_, ...), custom_call_target="tpu_custom_call" | custom-call | flops 4026531840 | bytes 33554432 | tf_op jit(solution)/shard_map/pallas_call | solution.py:316
  106.5 0.0 all-gather.2.cloned.1.call-done.fars
  106.5 15.8 %shard_map.60 = (f32[1536,1024]{1,0:T(8,128)S(1)}, f32[8,8,128]{2,1,0:T(8,128)S(1)}) custom-call(s32[12,8]{1,0:T(8,128)S(1)} %copy.9.cpat_ref, bf16[1536,2816]{1,0:T(8,128)(2,1)} %get-tuple-element.45.left_in, f32[1536,1024]{1,0:T(8,128)} %get-tuple-element.46.sum_in, bf16[176,128,128]{2,1,0:T(8,128)(2,1)} %all-gather.2.cloned.1.call-done.fars), custom_call_target="tpu_custom_call" | custom-call | flops 8858370048 | bytes 25165824 | tf_op jit(solution)/shard_map/pallas_call | solution.py:337
  122.3 16.2 %all_to_all.10.t_ref = f32[8,8,128]{2,1,0:T(8,128)S(1)} all-to-all(f32[8,8,128]{2,1,0:T(8,128)S(1)} %get-tuple-element.47), channel_id=1, replica_groups=mesh['row'=8,'col'=32] {'row'}, dimensions={0} | all-to-all | bytes 65536 | tf_op jit(solution)/shard_map/all_to_all | solution.py:417
  138.5 3.0 %shard_map.61 = bf16[1536,1024]{1,0:T(8,128)(2,1)} custom-call(f32[8,8,128]{2,1,0:T(8,128)S(1)} %all_to_all.10.t_ref, f32[1536,1024]{1,0:T(8,128)S(1)} %get-tuple-element.48.i_ref), custom_call_target="tpu_custom_call" | custom-call | flops 3145728 | bytes 4194304 | tf_op jit(solution)/shard_map/pallas_call | solution.py:371
  (34 shorter events, 0.2 us)
Async XLA Ops:
  9.7 7.6 %copy-start.8 = (s32[12,1]{0,1:T(1,128)S(1)}, s32[12,1]{0,1:T(1,128)}, u32[]{:S(2)}) copy-start(s32[12,1]{0,1:T(1,128)} %param.7) | copy-start | bytes 148
  9.7 23.1 %all-to-all-start = ((bf16[32,128,128]{2,1,0:T(8,128)(2,1)}), bf16[32,128,128]{2,1,0:T(8,128)(2,1)S(1)}, u32[]{:S(2)}, u32[]{:S(2)}) async-start(bf16[32,128,128]{2,1,0:T(8,128)(2,1)} %shard_map.55), calls=%async_computation | async-start | bytes 2097152 | tf_op jit(solution)/shard_map/all_to_all | solution.py:388
  17.3 89.3 %all-gather.2.cloned.1.call-start = ((), (), s32[]{:S(2)}) async-start(), calls=%async_computation.2 | async-start | bytes 6488064 | tf_op jit(solution)/shard_map/all_gather | solution.py:405
  25.1 9.5 %copy-start = (bf16[1536,128]{1,0:T(8,128)(2,1)S(1)}, bf16[1536,128]{1,0:T(8,128)(2,1)}, u32[]{:S(2)}) copy-start(bf16[1536,128]{1,0:T(8,128)(2,1)} %shard_map.56) | copy-start | bytes 1179652
  25.1 12.8 %copy-start.9 = (bf16[2,128,1024]{2,1,0:T(8,128)(2,1)S(1)}, bf16[2,128,1024]{2,1,0:T(8,128)(2,1)}, u32[]{:S(2)}) copy-start(bf16[2,128,1024]{2,1,0:T(8,128)(2,1)} %get-tuple-element.41) | copy-start | bytes 1572868
  32.8 9.1 %copy-start.2 = (bf16[2,128,1024]{2,1,0:T(8,128)(2,1)S(1)}, bf16[2,128,1024]{2,1,0:T(8,128)(2,1)}, u32[]{:S(2)}) copy-start(bf16[2,128,1024]{2,1,0:T(8,128)(2,1)} %get-tuple-element.40.refs_10_) | copy-start | bytes 1572868
  34.6 12.5 %collective-permute-start = (bf16[1536,128]{1,0:T(8,128)(2,1)S(1)}, bf16[1536,128]{1,0:T(8,128)(2,1)S(1)}, u32[]{:S(2)}, u32[]{:S(2)}) collective-permute-start(bf16[1536,128]{1,0:T(8,128)(2,1)S(1)} %copy-done), channel_id=1, source_target_pairs={{0,8},{1,3},{2,10},{3,5},{4,12},{5,7},{6,14},{7,1},{8,16},{9,11},{... | collective-permute-start | bytes 1179656 | tf_op jit(solution)/shard_map/ppermute | solution.py:41
  35.0 13.5 %collective-permute-start.1 = (bf16[1536,128]{1,0:T(8,128)(2,1)S(1)}, bf16[1536,128]{1,0:T(8,128)(2,1)S(1)}, u32[]{:S(2)}, u32[]{:S(2)}) collective-permute-start(bf16[1536,128]{1,0:T(8,128)(2,1)S(1)} %copy-done), channel_id=1, source_target_pairs={{0,24},{1,7},{2,26},{3,1},{4,28},{5,3},{6,30},{7,5},{8,0},{9,15},{... | collective-permute-start | bytes 1179656 | tf_op jit(solution)/shard_map/ppermute | solution.py:41
  37.9 13.0 %collective-permute-start.2 = (bf16[1536,128]{1,0:T(8,128)(2,1)S(1)}, bf16[1536,128]{1,0:T(8,128)(2,1)S(1)}, u32[]{:S(2)}, u32[]{:S(2)}) collective-permute-start(bf16[1536,128]{1,0:T(8,128)(2,1)S(1)} %copy-done), channel_id=1, source_target_pairs={{0,16},{1,5},{2,18},{3,7},{4,20},{5,1},{6,22},{7,3},{8,24},{9,13},... | collective-permute-start | bytes 1179656 | tf_op jit(solution)/shard_map/ppermute | solution.py:41
  37.9 21.5 %collective-permute-start.12 = (bf16[2,128,1024]{2,1,0:T(8,128)(2,1)S(1)}, bf16[2,128,1024]{2,1,0:T(8,128)(2,1)S(1)}, u32[]{:S(2)}, u32[]{:S(2)}) collective-permute-start(bf16[2,128,1024]{2,1,0:T(8,128)(2,1)S(1)} %copy-done.9), channel_id=1, source_target_pairs={{0,8},{1,3},{2,10},{3,5},{4,12},{5,7},{6,14},{7,1},{8,16},{9,11},{... | collective-permute-start | bytes 1572872 | tf_op jit(solution)/shard_map/ppermute | solution.py:41
  38.7 20.8 %collective-permute-start.13 = (bf16[2,128,1024]{2,1,0:T(8,128)(2,1)}, bf16[2,128,1024]{2,1,0:T(8,128)(2,1)S(1)}, u32[]{:S(2)}, u32[]{:S(2)}) collective-permute-start(bf16[2,128,1024]{2,1,0:T(8,128)(2,1)} %get-tuple-element.42), channel_id=1, source_target_pairs={{0,24},{1,7},{2,26},{3,1},{4,28},{5,3},{6,30},{7,5},{8,0},{9,15},{... | collective-permute-start | bytes 1572872 | tf_op jit(solution)/shard_map/ppermute | solution.py:41
  47.1 12.4 %collective-permute-start.14 = (bf16[2,128,1024]{2,1,0:T(8,128)(2,1)}, bf16[2,128,1024]{2,1,0:T(8,128)(2,1)S(1)}, u32[]{:S(2)}, u32[]{:S(2)}) collective-permute-start(bf16[2,128,1024]{2,1,0:T(8,128)(2,1)} %get-tuple-element.43), channel_id=1, source_target_pairs={{0,2},{1,9},{2,4},{3,11},{4,6},{5,13},{6,0},{7,15},{8,10},{9,17},{... | collective-permute-start | bytes 1572872 | tf_op jit(solution)/shard_map/ppermute | solution.py:41
  48.5 11.1 %collective-permute-start.15 = (bf16[2,128,1024]{2,1,0:T(8,128)(2,1)}, bf16[2,128,1024]{2,1,0:T(8,128)(2,1)S(1)}, u32[]{:S(2)}, u32[]{:S(2)}) collective-permute-start(bf16[2,128,1024]{2,1,0:T(8,128)(2,1)} %get-tuple-element.44), channel_id=1, source_target_pairs={{0,6},{1,25},{2,0},{3,27},{4,2},{5,29},{6,4},{7,31},{8,14},{9,1},{... | collective-permute-start | bytes 1572872 | tf_op jit(solution)/shard_map/ppermute | solution.py:41
  51.7 22.3 %collective-permute-start.3 = (bf16[1536,512]{1,0:T(8,128)(2,1)}, bf16[1536,512]{1,0:T(8,128)(2,1)S(1)}, u32[]{:S(2)}, u32[]{:S(2)}) collective-permute-start(bf16[1536,512]{1,0:T(8,128)(2,1)} %constant_dynamic-update-slice_fusion.refs_0_), channel_id=1, source_target_pairs={{0,2},{1,9},{2,4},{3,11},{4,6},{5,13},{6,0},{7,15},{8,10},{9,17},{... | collective-permute-start | bytes 4718600 | tf_op jit(solution)/shard_map/ppermute | solution.py:41
  59.4 1.3 copy-start.3
  59.4 20.6 %collective-permute-start.4 = (bf16[1536,512]{1,0:T(8,128)(2,1)}, bf16[1536,512]{1,0:T(8,128)(2,1)S(1)}, u32[]{:S(2)}, u32[]{:S(2)}) collective-permute-start(bf16[1536,512]{1,0:T(8,128)(2,1)} %constant_dynamic-update-slice_fusion.refs_0_), channel_id=1, source_target_pairs={{0,6},{1,25},{2,0},{3,27},{4,2},{5,29},{6,4},{7,31},{8,14},{9,1},{... | collective-permute-start | bytes 4718600 | tf_op jit(solution)/shard_map/ppermute | solution.py:41
  59.5 1.7 %copy-start.4 = (bf16[2,128,1024]{2,1,0:T(8,128)(2,1)}, bf16[2,128,1024]{2,1,0:T(8,128)(2,1)S(1)}, u32[]{:S(2)}) copy-start(bf16[2,128,1024]{2,1,0:T(8,128)(2,1)S(1)} %collective-permute-done.13.refs_12_) | copy-start | bytes 1572868
  59.5 1.7 %copy-start.5 = (bf16[2,128,1024]{2,1,0:T(8,128)(2,1)}, bf16[2,128,1024]{2,1,0:T(8,128)(2,1)S(1)}, u32[]{:S(2)}) copy-start(bf16[2,128,1024]{2,1,0:T(8,128)(2,1)S(1)} %collective-permute-done.14.refs_13_) | copy-start | bytes 1572868
  59.6 1.0 copy-start.6
  60.6 31.7 %copy-start.7 = (s32[12,8]{0,1:T(8,128)S(1)}, s32[12,8]{0,1:T(8,128)}, u32[]{:S(2)}) copy-start(s32[12,8]{0,1:T(8,128)} %param.9) | copy-start | bytes 1156
  60.6 20.4 %collective-permute-start.16 = (bf16[5,128,1024]{2,1,0:T(8,128)(2,1)S(1)}, bf16[5,128,1024]{2,1,0:T(8,128)(2,1)S(1)}, u32[]{:S(2)}, u32[]{:S(2)}) collective-permute-start(bf16[5,128,1024]{2,1,0:T(8,128)(2,1)S(1)} %slice_dynamic-update-slice_fusion), channel_id=1, source_target_pairs={{0,1},{1,0},{2,3},{3,2},{4,5},{5,4},{6,7},{7,6},{8,9},{9,8},{10,11... | collective-permute-start | bytes 3932168 | tf_op jit(solution)/shard_map/ppermute | solution.py:45
  60.7 31.7 %collective-permute-start.7 = (bf16[1536,512]{1,0:T(8,128)(2,1)}, bf16[1536,512]{1,0:T(8,128)(2,1)}, u32[]{:S(2)}, u32[]{:S(2)}) collective-permute-start(bf16[1536,512]{1,0:T(8,128)(2,1)} %constant_dynamic-update-slice_fusion.refs_0_), channel_id=1, source_target_pairs={{0,1},{1,0},{2,3},{3,2},{4,5},{5,4},{6,7},{7,6},{8,9},{9,8},{10,11... | collective-permute-start | bytes 4718600 | tf_op jit(solution)/shard_map/ppermute | solution.py:45
  74.0 13.1 %collective-permute-start.5 = (bf16[768,512]{1,0:T(8,128)(2,1)S(1)}, bf16[768,512]{1,0:T(8,128)(2,1)}, u32[]{:S(2)}, u32[]{:S(2)}) collective-permute-start(bf16[768,512]{1,0:T(8,128)(2,1)S(1)} %slice.28), channel_id=1, source_target_pairs={{0,2},{1,9},{2,4},{3,11},{4,6},{5,13},{6,0},{7,15},{8,10},{9,17},{... | collective-permute-start | bytes 2359304 | tf_op jit(solution)/shard_map/ppermute | solution.py:41
  80.1 12.2 %collective-permute-start.6 = (bf16[768,512]{1,0:T(8,128)(2,1)S(1)}, bf16[768,512]{1,0:T(8,128)(2,1)}, u32[]{:S(2)}, u32[]{:S(2)}) collective-permute-start(bf16[768,512]{1,0:T(8,128)(2,1)S(1)} %slice.29), channel_id=1, source_target_pairs={{0,6},{1,25},{2,0},{3,27},{4,2},{5,29},{6,4},{7,31},{8,14},{9,1},{... | collective-permute-start | bytes 2359304 | tf_op jit(solution)/shard_map/ppermute | solution.py:41
  80.9 13.9 %collective-permute-start.8 = (bf16[1536,512]{1,0:T(8,128)(2,1)S(1)}, bf16[1536,512]{1,0:T(8,128)(2,1)}, u32[]{:S(2)}, u32[]{:S(2)}) collective-permute-start(bf16[1536,512]{1,0:T(8,128)(2,1)S(1)} %collective-permute-done.3.refs_1_), channel_id=1, source_target_pairs={{0,1},{1,0},{2,3},{3,2},{4,5},{5,4},{6,7},{7,6},{8,9},{9,8},{10,11... | collective-permute-start | bytes 4718600 | tf_op jit(solution)/shard_map/ppermute | solution.py:45
  80.9 11.3 %copy-start.1 = (bf16[5,128,1024]{2,1,0:T(8,128)(2,1)}, bf16[5,128,1024]{2,1,0:T(8,128)(2,1)S(1)}, u32[]{:S(2)}) copy-start(bf16[5,128,1024]{2,1,0:T(8,128)(2,1)S(1)} %collective-permute-done.16.refs_15_) | copy-start | bytes 3932164
  80.9 13.9 %collective-permute-start.9 = (bf16[1536,512]{1,0:T(8,128)(2,1)S(1)}, bf16[1536,512]{1,0:T(8,128)(2,1)}, u32[]{:S(2)}, u32[]{:S(2)}) collective-permute-start(bf16[1536,512]{1,0:T(8,128)(2,1)S(1)} %collective-permute-done.4.refs_2_), channel_id=1, source_target_pairs={{0,1},{1,0},{2,3},{3,2},{4,5},{5,4},{6,7},{7,6},{8,9},{9,8},{10,11... | collective-permute-start | bytes 4718600 | tf_op jit(solution)/shard_map/ppermute | solution.py:45
  87.0 5.3 %collective-permute-start.10 = (bf16[768,512]{1,0:T(8,128)(2,1)}, bf16[768,512]{1,0:T(8,128)(2,1)}, u32[]{:S(2)}, u32[]{:S(2)}) collective-permute-start(bf16[768,512]{1,0:T(8,128)(2,1)} %collective-permute-done.5.refs_3_), channel_id=1, source_target_pairs={{0,1},{1,0},{2,3},{3,2},{4,5},{5,4},{6,7},{7,6},{8,9},{9,8},{10,11... | collective-permute-start | bytes 2359304 | tf_op jit(solution)/shard_map/ppermute | solution.py:45
  92.2 2.6 %collective-permute-start.11 = (bf16[768,512]{1,0:T(8,128)(2,1)}, bf16[768,512]{1,0:T(8,128)(2,1)}, u32[]{:S(2)}, u32[]{:S(2)}) collective-permute-start(bf16[768,512]{1,0:T(8,128)(2,1)} %collective-permute-done.6.refs_4_), channel_id=1, source_target_pairs={{0,1},{1,0},{2,3},{3,2},{4,5},{5,4},{6,7},{7,6},{8,9},{9,8},{10,11... | collective-permute-start | bytes 2359304 | tf_op jit(solution)/shard_map/ppermute | solution.py:45
Sparse Core Ops, SparseCore 0:
  34.7 70.2 all-gather.1

commit v4 on v3

--- a/solution.py
+++ b/solution.py
@@ -111,7 +111,7 @@
     shape = (COLS, b.shape[0], BLOCK)
     return pl.pallas_call(
         spread_kernel,
-        out_shape=jax.ShapeDtypeStruct(shape, b.dtype),
+        out_shape=pltpu.VMEM(shape, b.dtype),
         in_specs=[smem(), smem(), any_space()],
         out_specs=vmem(),
         scratch_shapes=[pltpu.VMEM(shape, b.dtype), pltpu.SemaphoreType.DMA((COLS,))],
@@ -176,6 +176,8 @@
 
 
 CHUNK = 384
+CHUNKS = ((0, 768), (768, 768))
+WIDE = 4
 HALF = 768
 
 
@@ -198,7 +200,7 @@
     return [
         pltpu.make_async_copy(
             fars.at[pl.ds(n * sources, sources)],
-            far.at[n // 2, :, :, pl.ds(n % 2 * BLOCK, BLOCK)],
+            far.at[n // WIDE, :, :, pl.ds(n % WIDE * BLOCK, BLOCK)],
             sems.at[n],
         )
         for n in range(ROWS)
@@ -265,35 +267,37 @@
 
 
 def second_kernel(cpat_ref, left_in, sum_in, fars, o_ref, t_ref, left, partial, far, fsem, lsem):
-    rows, depth = o_ref.shape[0], 2 * len(FAR) * BLOCK
+    depth = 2 * len(FAR) * BLOCK
     blocks = pairs_of(fars, far, fsem)
     parts = []
-    for i in range(rows // CHUNK):
-        here = pl.ds(i * CHUNK, CHUNK)
+    for i, (start, size) in enumerate(CHUNKS):
+        here = pl.ds(start, size)
         parts.append([
             pltpu.make_async_copy(left_in.at[here, :], left.at[here, :], lsem.at[2 * i]),
             pltpu.make_async_copy(sum_in.at[here, :], partial.at[here, :], lsem.at[2 * i + 1]),
         ])
-    for group in (blocks[:2], parts[0], blocks[2:], *parts[1:]):
+    for group in (blocks[:WIDE], parts[0], blocks[WIDE:], *parts[1:]):
         for copy in group:
             copy.start()
     sums = [jnp.zeros((1, BLOCK), F32) for _ in range(ROWS)]
     for i, part in enumerate(parts):
-        start, stop = i * CHUNK, (i + 1) * CHUNK
+        start, size = CHUNKS[i]
         for copy in part:
             copy.wait()
-        for pair in range(ROWS // 2):
+        for group in range(ROWS // WIDE):
             if i == 0:
-                for copy in blocks[2 * pair:2 * pair + 2]:
+                for copy in blocks[WIDE * group:WIDE * group + WIDE]:
                     copy.wait()
             product = jnp.dot(
-                left[start:stop, :], far[pair].reshape(depth, 2 * BLOCK), preferred_element_type=F32
+                left[start:start + size, :],
+                far[group].reshape(depth, WIDE * BLOCK),
+                preferred_element_type=F32,
             )
-            for n in range(2):
+            for n in range(WIDE):
                 lanes = slice(n * BLOCK, (n + 1) * BLOCK)
-                column = 2 * pair + n
+                column = WIDE * group + n
                 target = slice(column * BLOCK, (column + 1) * BLOCK)
-                for j in range(CHUNK // BLOCK):
+                for j in range(size // BLOCK):
                     keep = cpat_ref[start // BLOCK + j, column] != 0
                     place = slice(start + j * BLOCK, start + (j + 1) * BLOCK)
                     block = product[j * BLOCK:(j + 1) * BLOCK, lanes] + partial[place, target]
@@ -345,7 +349,7 @@
         scratch_shapes=[
             pltpu.VMEM((rows, depth), BF16),
             pltpu.VMEM((rows, ROWS * BLOCK), F32),
-            pltpu.VMEM((ROWS // 2, 2 * len(FAR), BLOCK, 2 * BLOCK), BF16),
+            pltpu.VMEM((ROWS // WIDE, 2 * len(FAR), BLOCK, WIDE * BLOCK), BF16),
             pltpu.SemaphoreType.DMA((ROWS,)),
             pltpu.SemaphoreType.DMA((8,)),
         ],
@@ -367,7 +371,7 @@
 
 def rescale(totals, inflated):
     rows, columns = inflated.shape
-    tile = 256
+    tile = 512
     return pl.pallas_call(
         functools.partial(rescale_kernel, float(rows * ROWS)),
         out_shape=jax.ShapeDtypeStruct((rows, columns), BF16),

time: 151 us -> 149 us (0.987)
  Pallas kernels: 41.1 us -> 39.4 us
where the time goes in v4:
time: 149 us; the launch traced here: 147 us
  waiting for transfers between devices  48.3 us (32%)
  Pallas kernels  39.4 us (26%)
  starting transfers between devices  22.9 us (15%)
  blocking collectives  16.2 us (11%)
  between operations  13.6 us (9%)
  local copies, waits for them, and re-layouts  6.29 us (4%)
    ppermute x11, waiting for transfers between devices, shift(): return lax.ppermute(value, 'col', pairs)  38 us
    all_to_all x1, blocking collectives, shards(): lax.all_to_all(totals, 'row', split_axis=0, concat_axis=0, tiled=True)  16.2 us
    pallas_call x1, Pallas kernels, second_product(): pl.pallas_call(second_kernel, out_shape=[pltpu.VMEM((rows, ROWS * BLOCK),...  14.6 us
    ppermute x11, starting transfers between devices, shift(): return lax.ppermute(value, 'col', pairs)  12.5 us
    pallas_call x1, Pallas kernels, first_product(): pl.pallas_call(first_kernel, out_shape=[pltpu.HBM((rows, sources * BLOCK)...  11.6 us
    all_to_all x1, waiting for transfers between devices, shards(): lax.all_to_all(sent, 'col', split_axis=0, concat_axis=0, tiled=True)  7.71 us
    all_to_all x1, starting transfers between devices, shards(): lax.all_to_all(sent, 'col', split_axis=0, concat_axis=0, tiled=True)  7.54 us
    unnamed x29, local copies, waits for them, and re-layouts  4.15 us
  transfers between devices with their start and end apart: 19, of which 9 were waited for; matrix products, arithmetic and copies ran while one was open for 4% of the time, Pallas kernels for 12%

profile of v4, /device:TPU:8, one launch (start us, length us, event | category | flops | bytes accessed | tf_op | source)
XLA Modules:
  0.0 146.7 jit_solution(3386942097412583953)
XLA Ops:
  6.5 3.1 %shard_map.55 = bf16[32,128,128]{2,1,0:T(8,128)(2,1)} custom-call(s32[1]{0:T(128)} %bitcast.row_ref, s32[1,256]{1,0:T(1,128)} %pattern_ref.4, bf16[128,32768]{1,0:T(8,128)(2,1)} %b_ref.3), custom_call_target="tpu_custom_call" | custom-call | flops 1048576 | bytes 2097152 | tf_op jit(solution)/shard_map/pallas_call | solution.py:112
  9.7 0.0 copy-start.8
  9.7 7.5 %all-to-all-start = ((bf16[32,128,128]{2,1,0:T(8,128)(2,1)}), bf16[32,128,128]{2,1,0:T(8,128)(2,1)S(1)}, u32[]{:S(2)}, u32[]{:S(2)}) async-start(bf16[32,128,128]{2,1,0:T(8,128)(2,1)} %shard_map.55), calls=%async_computation | async-start | bytes 2097152 | tf_op jit(solution)/shard_map/all_to_all | solution.py:392
  17.3 0.0 all-gather.2.cloned.1.call-start
  17.3 0.7 copy.8.pattern_ref
  18.0 1.9 %shard_map.56 = bf16[1536,128]{1,0:T(8,128)(2,1)} custom-call(s32[12,1]{1,0:T(8,128)} %copy.8.pattern_ref, bf16[1536,128]{1,0:T(8,128)(2,1)} %a_ref.1), custom_call_target="tpu_custom_call" | custom-call | flops 196608 | bytes 786432 | tf_op jit(solution)/shard_map/pallas_call | solution.py:84
  19.9 0.6 stack.115.where_ref
  20.5 0.6 stack.138.index_ref
  21.1 4.0 %shard_map.57 = (bf16[2,128,1024]{2,1,0:T(8,128)(2,1)}, bf16[2,128,1024]{2,1,0:T(8,128)(2,1)}, bf16[2,128,1024]{2,1,0:T(8,128)(2,1)}, bf16[2,128,1024]{2,1,0:T(8,128)(2,1)}, bf16[2,128,1024]{2,1,0:T(8,128)(2,1)}) custom-call(s32[10]{0:T(128)} %stack.115.where_ref, s32[1,256]{1,0:T(1,128)} %pattern_ref.4, bf16[128,32768]{1,0:T(8,128)(2,1)} %b_ref.3), custom_call_target="tpu_custom_call" | custom-call | flops 4194304 | bytes 8388608 | tf_op jit(solution)/shard_map/pallas_call | solution.py:147
  25.1 7.7 %all-to-all-done.r_ref = bf16[32,128,128]{2,1,0:T(8,128)(2,1)S(1)} async-done(((bf16[32,128,128]{2,1,0:T(8,128)(2,1)}), bf16[32,128,128]{2,1,0:T(8,128)(2,1)S(1)}, u32[]{:S(2)}, u32[]{:S(2)}) %all-to-all-start) | async-done | bytes 1048608 | tf_op jit(solution)/shard_map/all_to_all | solution.py:392
  32.8 1.7 %shard_map.58 = bf16[22,128,128]{2,1,0:T(8,128)(2,1)} custom-call(s32[22]{0:T(128)} %stack.138.index_ref, bf16[32,128,128]{2,1,0:T(8,128)(2,1)S(1)} %all-to-all-done.r_ref), custom_call_target="tpu_custom_call" | custom-call | bytes 2097152 | tf_op jit(solution)/shard_map/pallas_call | solution.py:168
  34.5 0.0 all-gather.2.cloned.1.call-update
  34.6 0.4 collective-permute-start
  35.0 2.9 %collective-permute-start.1 = (bf16[1536,128]{1,0:T(8,128)(2,1)S(1)}, bf16[1536,128]{1,0:T(8,128)(2,1)S(1)}, u32[]{:S(2)}, u32[]{:S(2)}) collective-permute-start(bf16[1536,128]{1,0:T(8,128)(2,1)S(1)} %copy-done), channel_id=1, source_target_pairs={{0,24},{1,7},{2,26},{3,1},{4,28},{5,3},{6,30},{7,5},{8,0},{9,15},{... | collective-permute-start | bytes 1179656 | tf_op jit(solution)/shard_map/ppermute | solution.py:41
  37.9 0.9 collective-permute-start.12
  38.7 2.4 %collective-permute-start.13 = (bf16[2,128,1024]{2,1,0:T(8,128)(2,1)}, bf16[2,128,1024]{2,1,0:T(8,128)(2,1)S(1)}, u32[]{:S(2)}, u32[]{:S(2)}) collective-permute-start(bf16[2,128,1024]{2,1,0:T(8,128)(2,1)} %get-tuple-element.42), channel_id=1, source_target_pairs={{0,24},{1,7},{2,26},{3,1},{4,28},{5,3},{6,30},{7,5},{8,0},{9,15},{... | collective-permute-start | bytes 1572872 | tf_op jit(solution)/shard_map/ppermute | solution.py:41
  41.1 0.8 constant_dynamic-update-slice_fusion.3
  41.9 5.2 %collective-permute-done = bf16[1536,128]{1,0:T(8,128)(2,1)S(1)} collective-permute-done((bf16[1536,128]{1,0:T(8,128)(2,1)S(1)}, bf16[1536,128]{1,0:T(8,128)(2,1)S(1)}, u32[]{:S(2)}, u32[]{:S(2)}) %collective-permute-start) | collective-permute-done | bytes 393248 | tf_op jit(solution)/shard_map/ppermute | solution.py:41
  47.1 0.6 collective-permute-start.14
  47.7 0.8 constant_dynamic-update-slice_fusion.2
  48.5 1.6 %collective-permute-start.15 = (bf16[2,128,1024]{2,1,0:T(8,128)(2,1)}, bf16[2,128,1024]{2,1,0:T(8,128)(2,1)S(1)}, u32[]{:S(2)}, u32[]{:S(2)}) collective-permute-start(bf16[2,128,1024]{2,1,0:T(8,128)(2,1)} %get-tuple-element.44), channel_id=1, source_target_pairs={{0,6},{1,25},{2,0},{3,27},{4,2},{5,29},{6,4},{7,31},{8,14},{9,1},{... | collective-permute-start | bytes 1572872 | tf_op jit(solution)/shard_map/ppermute | solution.py:41
  50.1 0.8 constant_dynamic-update-slice_fusion.1
  50.9 0.8 constant_dynamic-update-slice_fusion.refs_0_
  51.7 1.4 collective-permute-start.3
  53.0 6.3 %collective-permute-done.12.refs_11_ = bf16[2,128,1024]{2,1,0:T(8,128)(2,1)S(1)} collective-permute-done((bf16[2,128,1024]{2,1,0:T(8,128)(2,1)S(1)}, bf16[2,128,1024]{2,1,0:T(8,128)(2,1)S(1)}, u32[]{:S(2)}, u32[]{:S(2)}) %collective-permute-start.12) | collective-permute-done | bytes 524320 | tf_op jit(solution)/shard_map/ppermute | solution.py:41
  59.4 0.1 collective-permute-done.13.refs_12_
  59.6 1.0 copy-done.6
  60.6 0.0 copy-start.7
  60.6 0.1 collective-permute-start.16
  60.7 0.5 collective-permute-start.7
  61.2 12.7 %collective-permute-done.3.refs_1_ = bf16[1536,512]{1,0:T(8,128)(2,1)S(1)} collective-permute-done((bf16[1536,512]{1,0:T(8,128)(2,1)}, bf16[1536,512]{1,0:T(8,128)(2,1)S(1)}, u32[]{:S(2)}, u32[]{:S(2)}) %collective-permute-start.3) | collective-permute-done | bytes 1572896 | tf_op jit(solution)/shard_map/ppermute | solution.py:41
  73.9 0.1 slice.28
  74.0 1.4 collective-permute-start.5
  75.4 4.6 %collective-permute-done.4.refs_2_ = bf16[1536,512]{1,0:T(8,128)(2,1)S(1)} collective-permute-done((bf16[1536,512]{1,0:T(8,128)(2,1)}, bf16[1536,512]{1,0:T(8,128)(2,1)S(1)}, u32[]{:S(2)}, u32[]{:S(2)}) %collective-permute-start.4) | collective-permute-done | bytes 1572896 | tf_op jit(solution)/shard_map/ppermute | solution.py:41
  80.0 0.1 slice.29
  80.1 0.9 collective-permute-start.6
  80.9 0.0 collective-permute-start.8
  80.9 0.5 collective-permute-start.9
  81.4 5.6 %collective-permute-done.5.refs_3_ = bf16[768,512]{1,0:T(8,128)(2,1)} collective-permute-done((bf16[768,512]{1,0:T(8,128)(2,1)S(1)}, bf16[768,512]{1,0:T(8,128)(2,1)}, u32[]{:S(2)}, u32[]{:S(2)}) %collective-permute-start.5) | collective-permute-done | bytes 786464 | tf_op jit(solution)/shard_map/ppermute | solution.py:41
  87.0 1.7 %collective-permute-start.10 = (bf16[768,512]{1,0:T(8,128)(2,1)}, bf16[768,512]{1,0:T(8,128)(2,1)}, u32[]{:S(2)}, u32[]{:S(2)}) collective-permute-start(bf16[768,512]{1,0:T(8,128)(2,1)} %collective-permute-done.5.refs_3_), channel_id=1, source_target_pairs={{0,1},{1,0},{2,3},{3,2},{4,5},{5,4},{6,7},{7,6},{8,9},{9,8},{10,11... | collective-permute-start | bytes 2359304 | tf_op jit(solution)/shard_map/ppermute | solution.py:45
  88.7 3.5 %collective-permute-done.6.refs_4_ = bf16[768,512]{1,0:T(8,128)(2,1)} collective-permute-done((bf16[768,512]{1,0:T(8,128)(2,1)S(1)}, bf16[768,512]{1,0:T(8,128)(2,1)}, u32[]{:S(2)}, u32[]{:S(2)}) %collective-permute-start.6) | collective-permute-done | bytes 786464 | tf_op jit(solution)/shard_map/ppermute | solution.py:41
  92.2 0.1 copy.9.cpat_ref
  92.3 2.5 %collective-permute-done.11.refs_9_ = bf16[768,512]{1,0:T(8,128)(2,1)} collective-permute-done((bf16[768,512]{1,0:T(8,128)(2,1)}, bf16[768,512]{1,0:T(8,128)(2,1)}, u32[]{:S(2)}, u32[]{:S(2)}) %collective-permute-start.11) | collective-permute-done | bytes 786464 | tf_op jit(solution)/shard_map/ppermute | solution.py:45
  94.9 11.6 %shard_map.59 = (bf16[1536,2816]{1,0:T(8,128)(2,1)}, f32[1536,1024]{1,0:T(8,128)}) custom-call(bf16[1536,512]{1,0:T(8,128)(2,1)} %constant_dynamic-update-slice_fusion.refs_0_, bf16[1536,512]{1,0:T(8,128)(2,1)S(1)} %collective-permute-done.3.refs_1_, bf16[1536,512]{1,0:T(8,128)(2,1)S(1)} %collective-permute-done.4.refs_2_, ...), custom_call_target="tpu_custom_call" | custom-call | flops 4026531840 | bytes 33554432 | tf_op jit(solution)/shard_map/pallas_call | solution.py:320
  106.5 0.0 all-gather.2.cloned.1.call-done.fars
  106.5 14.6 %shard_map.60 = (f32[1536,1024]{1,0:T(8,128)S(1)}, f32[8,8,128]{2,1,0:T(8,128)S(1)}) custom-call(s32[12,8]{1,0:T(8,128)S(1)} %copy.9.cpat_ref, bf16[1536,2816]{1,0:T(8,128)(2,1)} %get-tuple-element.45.left_in, f32[1536,1024]{1,0:T(8,128)} %get-tuple-element.46.sum_in, bf16[176,128,128]{2,1,0:T(8,128)(2,1)} %all-gather.2.cloned.1.call-done.fars), custom_call_target="tpu_custom_call" | custom-call | flops 8858370048 | bytes 25165824 | tf_op jit(solution)/shard_map/pallas_call | solution.py:341
  121.1 16.2 %all_to_all.10.t_ref = f32[8,8,128]{2,1,0:T(8,128)S(1)} all-to-all(f32[8,8,128]{2,1,0:T(8,128)S(1)} %get-tuple-element.47), channel_id=1, replica_groups=mesh['row'=8,'col'=32] {'row'}, dimensions={0} | all-to-all | bytes 65536 | tf_op jit(solution)/shard_map/all_to_all | solution.py:421
  137.3 2.5 %shard_map.61 = bf16[1536,1024]{1,0:T(8,128)(2,1)} custom-call(f32[8,8,128]{2,1,0:T(8,128)S(1)} %all_to_all.10.t_ref, f32[1536,1024]{1,0:T(8,128)S(1)} %get-tuple-element.48.i_ref), custom_call_target="tpu_custom_call" | custom-call | flops 3145728 | bytes 4194304 | tf_op jit(solution)/shard_map/pallas_call | solution.py:375
  (34 shorter events, 0.2 us)
Async XLA Ops:
  9.7 7.6 %copy-start.8 = (s32[12,1]{0,1:T(1,128)S(1)}, s32[12,1]{0,1:T(1,128)}, u32[]{:S(2)}) copy-start(s32[12,1]{0,1:T(1,128)} %param.7) | copy-start | bytes 148
  9.7 23.1 %all-to-all-start = ((bf16[32,128,128]{2,1,0:T(8,128)(2,1)}), bf16[32,128,128]{2,1,0:T(8,128)(2,1)S(1)}, u32[]{:S(2)}, u32[]{:S(2)}) async-start(bf16[32,128,128]{2,1,0:T(8,128)(2,1)} %shard_map.55), calls=%async_computation | async-start | bytes 2097152 | tf_op jit(solution)/shard_map/all_to_all | solution.py:392
  17.3 89.3 %all-gather.2.cloned.1.call-start = ((), (), s32[]{:S(2)}) async-start(), calls=%async_computation.2 | async-start | bytes 6488064 | tf_op jit(solution)/shard_map/all_gather | solution.py:409
  25.1 9.5 %copy-start = (bf16[1536,128]{1,0:T(8,128)(2,1)S(1)}, bf16[1536,128]{1,0:T(8,128)(2,1)}, u32[]{:S(2)}) copy-start(bf16[1536,128]{1,0:T(8,128)(2,1)} %shard_map.56) | copy-start | bytes 1179652
  25.1 12.8 %copy-start.9 = (bf16[2,128,1024]{2,1,0:T(8,128)(2,1)S(1)}, bf16[2,128,1024]{2,1,0:T(8,128)(2,1)}, u32[]{:S(2)}) copy-start(bf16[2,128,1024]{2,1,0:T(8,128)(2,1)} %get-tuple-element.41) | copy-start | bytes 1572868
  32.8 9.1 %copy-start.2 = (bf16[2,128,1024]{2,1,0:T(8,128)(2,1)S(1)}, bf16[2,128,1024]{2,1,0:T(8,128)(2,1)}, u32[]{:S(2)}) copy-start(bf16[2,128,1024]{2,1,0:T(8,128)(2,1)} %get-tuple-element.40.refs_10_) | copy-start | bytes 1572868
  34.6 12.5 %collective-permute-start = (bf16[1536,128]{1,0:T(8,128)(2,1)S(1)}, bf16[1536,128]{1,0:T(8,128)(2,1)S(1)}, u32[]{:S(2)}, u32[]{:S(2)}) collective-permute-start(bf16[1536,128]{1,0:T(8,128)(2,1)S(1)} %copy-done), channel_id=1, source_target_pairs={{0,8},{1,3},{2,10},{3,5},{4,12},{5,7},{6,14},{7,1},{8,16},{9,11},{... | collective-permute-start | bytes 1179656 | tf_op jit(solution)/shard_map/ppermute | solution.py:41
  35.0 13.5 %collective-permute-start.1 = (bf16[1536,128]{1,0:T(8,128)(2,1)S(1)}, bf16[1536,128]{1,0:T(8,128)(2,1)S(1)}, u32[]{:S(2)}, u32[]{:S(2)}) collective-permute-start(bf16[1536,128]{1,0:T(8,128)(2,1)S(1)} %copy-done), channel_id=1, source_target_pairs={{0,24},{1,7},{2,26},{3,1},{4,28},{5,3},{6,30},{7,5},{8,0},{9,15},{... | collective-permute-start | bytes 1179656 | tf_op jit(solution)/shard_map/ppermute | solution.py:41
  37.9 13.0 %collective-permute-start.2 = (bf16[1536,128]{1,0:T(8,128)(2,1)S(1)}, bf16[1536,128]{1,0:T(8,128)(2,1)S(1)}, u32[]{:S(2)}, u32[]{:S(2)}) collective-permute-start(bf16[1536,128]{1,0:T(8,128)(2,1)S(1)} %copy-done), channel_id=1, source_target_pairs={{0,16},{1,5},{2,18},{3,7},{4,20},{5,1},{6,22},{7,3},{8,24},{9,13},... | collective-permute-start | bytes 1179656 | tf_op jit(solution)/shard_map/ppermute | solution.py:41
  37.9 21.5 %collective-permute-start.12 = (bf16[2,128,1024]{2,1,0:T(8,128)(2,1)S(1)}, bf16[2,128,1024]{2,1,0:T(8,128)(2,1)S(1)}, u32[]{:S(2)}, u32[]{:S(2)}) collective-permute-start(bf16[2,128,1024]{2,1,0:T(8,128)(2,1)S(1)} %copy-done.9), channel_id=1, source_target_pairs={{0,8},{1,3},{2,10},{3,5},{4,12},{5,7},{6,14},{7,1},{8,16},{9,11},{... | collective-permute-start | bytes 1572872 | tf_op jit(solution)/shard_map/ppermute | solution.py:41
  38.7 20.8 %collective-permute-start.13 = (bf16[2,128,1024]{2,1,0:T(8,128)(2,1)}, bf16[2,128,1024]{2,1,0:T(8,128)(2,1)S(1)}, u32[]{:S(2)}, u32[]{:S(2)}) collective-permute-start(bf16[2,128,1024]{2,1,0:T(8,128)(2,1)} %get-tuple-element.42), channel_id=1, source_target_pairs={{0,24},{1,7},{2,26},{3,1},{4,28},{5,3},{6,30},{7,5},{8,0},{9,15},{... | collective-permute-start | bytes 1572872 | tf_op jit(solution)/shard_map/ppermute | solution.py:41
  47.1 12.4 %collective-permute-start.14 = (bf16[2,128,1024]{2,1,0:T(8,128)(2,1)}, bf16[2,128,1024]{2,1,0:T(8,128)(2,1)S(1)}, u32[]{:S(2)}, u32[]{:S(2)}) collective-permute-start(bf16[2,128,1024]{2,1,0:T(8,128)(2,1)} %get-tuple-element.43), channel_id=1, source_target_pairs={{0,2},{1,9},{2,4},{3,11},{4,6},{5,13},{6,0},{7,15},{8,10},{9,17},{... | collective-permute-start | bytes 1572872 | tf_op jit(solution)/shard_map/ppermute | solution.py:41
  48.5 11.1 %collective-permute-start.15 = (bf16[2,128,1024]{2,1,0:T(8,128)(2,1)}, bf16[2,128,1024]{2,1,0:T(8,128)(2,1)S(1)}, u32[]{:S(2)}, u32[]{:S(2)}) collective-permute-start(bf16[2,128,1024]{2,1,0:T(8,128)(2,1)} %get-tuple-element.44), channel_id=1, source_target_pairs={{0,6},{1,25},{2,0},{3,27},{4,2},{5,29},{6,4},{7,31},{8,14},{9,1},{... | collective-permute-start | bytes 1572872 | tf_op jit(solution)/shard_map/ppermute | solution.py:41
  51.7 22.3 %collective-permute-start.3 = (bf16[1536,512]{1,0:T(8,128)(2,1)}, bf16[1536,512]{1,0:T(8,128)(2,1)S(1)}, u32[]{:S(2)}, u32[]{:S(2)}) collective-permute-start(bf16[1536,512]{1,0:T(8,128)(2,1)} %constant_dynamic-update-slice_fusion.refs_0_), channel_id=1, source_target_pairs={{0,2},{1,9},{2,4},{3,11},{4,6},{5,13},{6,0},{7,15},{8,10},{9,17},{... | collective-permute-start | bytes 4718600 | tf_op jit(solution)/shard_map/ppermute | solution.py:41
  59.4 1.3 copy-start.3
  59.4 20.6 %collective-permute-start.4 = (bf16[1536,512]{1,0:T(8,128)(2,1)}, bf16[1536,512]{1,0:T(8,128)(2,1)S(1)}, u32[]{:S(2)}, u32[]{:S(2)}) collective-permute-start(bf16[1536,512]{1,0:T(8,128)(2,1)} %constant_dynamic-update-slice_fusion.refs_0_), channel_id=1, source_target_pairs={{0,6},{1,25},{2,0},{3,27},{4,2},{5,29},{6,4},{7,31},{8,14},{9,1},{... | collective-permute-start | bytes 4718600 | tf_op jit(solution)/shard_map/ppermute | solution.py:41
  59.5 1.7 %copy-start.4 = (bf16[2,128,1024]{2,1,0:T(8,128)(2,1)}, bf16[2,128,1024]{2,1,0:T(8,128)(2,1)S(1)}, u32[]{:S(2)}) copy-start(bf16[2,128,1024]{2,1,0:T(8,128)(2,1)S(1)} %collective-permute-done.13.refs_12_) | copy-start | bytes 1572868
  59.5 1.7 %copy-start.5 = (bf16[2,128,1024]{2,1,0:T(8,128)(2,1)}, bf16[2,128,1024]{2,1,0:T(8,128)(2,1)S(1)}, u32[]{:S(2)}) copy-start(bf16[2,128,1024]{2,1,0:T(8,128)(2,1)S(1)} %collective-permute-done.14.refs_13_) | copy-start | bytes 1572868
  59.6 1.0 copy-start.6
  60.6 31.7 %copy-start.7 = (s32[12,8]{0,1:T(8,128)S(1)}, s32[12,8]{0,1:T(8,128)}, u32[]{:S(2)}) copy-start(s32[12,8]{0,1:T(8,128)} %param.9) | copy-start | bytes 1156
  60.6 20.4 %collective-permute-start.16 = (bf16[5,128,1024]{2,1,0:T(8,128)(2,1)S(1)}, bf16[5,128,1024]{2,1,0:T(8,128)(2,1)S(1)}, u32[]{:S(2)}, u32[]{:S(2)}) collective-permute-start(bf16[5,128,1024]{2,1,0:T(8,128)(2,1)S(1)} %slice_dynamic-update-slice_fusion), channel_id=1, source_target_pairs={{0,1},{1,0},{2,3},{3,2},{4,5},{5,4},{6,7},{7,6},{8,9},{9,8},{10,11... | collective-permute-start | bytes 3932168 | tf_op jit(solution)/shard_map/ppermute | solution.py:45
  60.7 31.7 %collective-permute-start.7 = (bf16[1536,512]{1,0:T(8,128)(2,1)}, bf16[1536,512]{1,0:T(8,128)(2,1)}, u32[]{:S(2)}, u32[]{:S(2)}) collective-permute-start(bf16[1536,512]{1,0:T(8,128)(2,1)} %constant_dynamic-update-slice_fusion.refs_0_), channel_id=1, source_target_pairs={{0,1},{1,0},{2,3},{3,2},{4,5},{5,4},{6,7},{7,6},{8,9},{9,8},{10,11... | collective-permute-start | bytes 4718600 | tf_op jit(solution)/shard_map/ppermute | solution.py:45
  74.0 13.1 %collective-permute-start.5 = (bf16[768,512]{1,0:T(8,128)(2,1)S(1)}, bf16[768,512]{1,0:T(8,128)(2,1)}, u32[]{:S(2)}, u32[]{:S(2)}) collective-permute-start(bf16[768,512]{1,0:T(8,128)(2,1)S(1)} %slice.28), channel_id=1, source_target_pairs={{0,2},{1,9},{2,4},{3,11},{4,6},{5,13},{6,0},{7,15},{8,10},{9,17},{... | collective-permute-start | bytes 2359304 | tf_op jit(solution)/shard_map/ppermute | solution.py:41
  80.1 12.2 %collective-permute-start.6 = (bf16[768,512]{1,0:T(8,128)(2,1)S(1)}, bf16[768,512]{1,0:T(8,128)(2,1)}, u32[]{:S(2)}, u32[]{:S(2)}) collective-permute-start(bf16[768,512]{1,0:T(8,128)(2,1)S(1)} %slice.29), channel_id=1, source_target_pairs={{0,6},{1,25},{2,0},{3,27},{4,2},{5,29},{6,4},{7,31},{8,14},{9,1},{... | collective-permute-start | bytes 2359304 | tf_op jit(solution)/shard_map/ppermute | solution.py:41
  80.9 13.9 %collective-permute-start.8 = (bf16[1536,512]{1,0:T(8,128)(2,1)S(1)}, bf16[1536,512]{1,0:T(8,128)(2,1)}, u32[]{:S(2)}, u32[]{:S(2)}) collective-permute-start(bf16[1536,512]{1,0:T(8,128)(2,1)S(1)} %collective-permute-done.3.refs_1_), channel_id=1, source_target_pairs={{0,1},{1,0},{2,3},{3,2},{4,5},{5,4},{6,7},{7,6},{8,9},{9,8},{10,11... | collective-permute-start | bytes 4718600 | tf_op jit(solution)/shard_map/ppermute | solution.py:45
  80.9 11.3 %copy-start.1 = (bf16[5,128,1024]{2,1,0:T(8,128)(2,1)}, bf16[5,128,1024]{2,1,0:T(8,128)(2,1)S(1)}, u32[]{:S(2)}) copy-start(bf16[5,128,1024]{2,1,0:T(8,128)(2,1)S(1)} %collective-permute-done.16.refs_15_) | copy-start | bytes 3932164
  80.9 13.9 %collective-permute-start.9 = (bf16[1536,512]{1,0:T(8,128)(2,1)S(1)}, bf16[1536,512]{1,0:T(8,128)(2,1)}, u32[]{:S(2)}, u32[]{:S(2)}) collective-permute-start(bf16[1536,512]{1,0:T(8,128)(2,1)S(1)} %collective-permute-done.4.refs_2_), channel_id=1, source_target_pairs={{0,1},{1,0},{2,3},{3,2},{4,5},{5,4},{6,7},{7,6},{8,9},{9,8},{10,11... | collective-permute-start | bytes 4718600 | tf_op jit(solution)/shard_map/ppermute | solution.py:45
  87.0 5.3 %collective-permute-start.10 = (bf16[768,512]{1,0:T(8,128)(2,1)}, bf16[768,512]{1,0:T(8,128)(2,1)}, u32[]{:S(2)}, u32[]{:S(2)}) collective-permute-start(bf16[768,512]{1,0:T(8,128)(2,1)} %collective-permute-done.5.refs_3_), channel_id=1, source_target_pairs={{0,1},{1,0},{2,3},{3,2},{4,5},{5,4},{6,7},{7,6},{8,9},{9,8},{10,11... | collective-permute-start | bytes 2359304 | tf_op jit(solution)/shard_map/ppermute | solution.py:45
  92.2 2.6 %collective-permute-start.11 = (bf16[768,512]{1,0:T(8,128)(2,1)}, bf16[768,512]{1,0:T(8,128)(2,1)}, u32[]{:S(2)}, u32[]{:S(2)}) collective-permute-start(bf16[768,512]{1,0:T(8,128)(2,1)} %collective-permute-done.6.refs_4_), channel_id=1, source_target_pairs={{0,1},{1,0},{2,3},{3,2},{4,5},{5,4},{6,7},{7,6},{8,9},{9,8},{10,11... | collective-permute-start | bytes 2359304 | tf_op jit(solution)/shard_map/ppermute | solution.py:45
Sparse Core Ops, SparseCore 0:
  34.7 70.2 all-gather.1

commit v5 on v4

--- a/solution.py
+++ b/solution.py
@@ -175,10 +175,13 @@
     )(index, held(received))
 
 
+HALF = 768
 CHUNK = 384
-CHUNKS = ((0, 768), (768, 768))
+CHUNKS = ((0, HALF), (HALF, HALF))
 WIDE = 4
-HALF = 768
+
+
+EARLY = len(FAR) - 4
 
 
 def runs(o, d):
@@ -209,10 +212,10 @@
 
 def first_kernel(*refs):
     refs = list(refs)
-    lefts = [refs.pop(0) for _ in range(10)]
+    lefts = [refs.pop(0) for _ in range(6)]
     nears = [refs.pop(0) for _ in range(len(NEAR) + 1)]
     left_out, o_ref, left, piece, near, out, nsem, lsem, osem = refs
-    rows, count, depth = o_ref.shape[0], len(NEAR), 2 * len(FAR) * BLOCK
+    rows, count, depth = o_ref.shape[0], len(NEAR), 2 * EARLY * BLOCK
 
     whole = [pltpu.make_async_copy(nears[k].at[0], near.at[k], nsem.at[k]) for k in range(count)]
     whole.append(pltpu.make_async_copy(nears[count], near.at[pl.ds(count, count)], nsem.at[count]))
@@ -220,13 +223,9 @@
     for i in range(rows // CHUNK):
         start = i * CHUNK
         part = []
-        for k in range(8):
-            o, d = k // 4, k % 4
-            if d < 3:
-                source = lefts[o * 5 + d].at[pl.ds(start, CHUNK), :]
-            else:
-                source = lefts[o * 5 + 3 + start // HALF].at[pl.ds(start % HALF, CHUNK), :]
-            part.append(pltpu.make_async_copy(source, piece.at[i % 2, k], lsem.at[i * 8 + k]))
+        for k in range(6):
+            source = lefts[k].at[pl.ds(start, CHUNK), :]
+            part.append(pltpu.make_async_copy(source, piece.at[i % 2, k], lsem.at[i * 6 + k]))
         parts.append(part)
     for group in (parts[0], whole, parts[1]):
         for copy in group:
@@ -239,8 +238,9 @@
         if i >= 2:
             for copy in outs[i - 2]:
                 copy.wait()
-        for k in range(8):
-            for block, width, spot in runs(k // 4, k % 4):
+        for k in range(6):
+            for block, width, spot in runs(k // 3, k % 3):
+                spot -= 4 * (spot // len(FAR)) if spot < 2 * len(FAR) else 8
                 lanes = slice(block * BLOCK, (block + width) * BLOCK)
                 target = slice(spot * BLOCK, (spot + width) * BLOCK)
                 left[slot, :, target] = piece[slot, k, :, lanes]
@@ -266,16 +266,20 @@
             copy.wait()
 
 
-def second_kernel(cpat_ref, left_in, sum_in, fars, o_ref, t_ref, left, partial, far, fsem, lsem):
+def second_kernel(cpat_ref, left_in, u0, l0, u1, l1, sum_in, fars, o_ref, t_ref, left, partial, far, fsem, lsem):
     depth = 2 * len(FAR) * BLOCK
     blocks = pairs_of(fars, far, fsem)
     parts = []
     for i, (start, size) in enumerate(CHUNKS):
         here = pl.ds(start, size)
-        parts.append([
-            pltpu.make_async_copy(left_in.at[here, :], left.at[here, :], lsem.at[2 * i]),
-            pltpu.make_async_copy(sum_in.at[here, :], partial.at[here, :], lsem.at[2 * i + 1]),
-        ])
+        part = [pltpu.make_async_copy(sum_in.at[here, :], partial.at[here, :], lsem.at[5 * i])]
+        for o, opposite in enumerate(((u0, l0), (u1, l1))):
+            wide, place = EARLY * BLOCK, o * len(FAR) * BLOCK
+            early = left_in.at[here, pl.ds(o * wide, wide)]
+            part.append(pltpu.make_async_copy(early, left.at[here, pl.ds(place, wide)], lsem.at[5 * i + 1 + o]))
+            target = left.at[here, pl.ds(place + wide, 4 * BLOCK)]
+            part.append(pltpu.make_async_copy(opposite[i], target, lsem.at[5 * i + 3 + o]))
+        parts.append(part)
     for group in (blocks[:WIDE], parts[0], blocks[WIDE:], *parts[1:]):
         for copy in group:
             copy.start()
@@ -316,15 +320,15 @@
 
 
 def first_product(lefts, nears):
-    rows, sources = 2 * HALF, 2 * len(FAR)
+    rows, sources = 2 * HALF, 2 * EARLY
     return pl.pallas_call(
         first_kernel,
         out_shape=[pltpu.HBM((rows, sources * BLOCK), BF16), pltpu.HBM((rows, ROWS * BLOCK), F32)],
         in_specs=[any_space()] * (len(lefts) + len(nears)),
         out_specs=[any_space()] * 2,
         scratch_shapes=[
-            pltpu.VMEM((2, CHUNK, COLS * BLOCK), BF16),
-            pltpu.VMEM((2, 8, CHUNK, 512), BF16),
+            pltpu.VMEM((2, CHUNK, (COLS - 8) * BLOCK), BF16),
+            pltpu.VMEM((2, 6, CHUNK, 512), BF16),
             pltpu.VMEM((2 * len(NEAR), BLOCK, ROWS * BLOCK), BF16),
             pltpu.VMEM((2, CHUNK, ROWS * BLOCK), F32),
             pltpu.SemaphoreType.DMA((len(nears),)),
@@ -336,26 +340,26 @@
     )(*lefts, *[outside(array) for array in nears])
 
 
-def second_product(cpat, left, partial, fars):
-    rows, depth = left.shape
+def second_product(cpat, left, opposite, partial, fars):
+    rows, depth = 2 * HALF, 2 * len(FAR) * BLOCK
     return pl.pallas_call(
         second_kernel,
         out_shape=[
             pltpu.VMEM((rows, ROWS * BLOCK), F32),
             jax.ShapeDtypeStruct((ROWS, ROWS, BLOCK), F32),
         ],
-        in_specs=[smem()] + [any_space()] * 3,
+        in_specs=[smem()] + [any_space()] * 7,
         out_specs=[vmem()] * 2,
         scratch_shapes=[
             pltpu.VMEM((rows, depth), BF16),
             pltpu.VMEM((rows, ROWS * BLOCK), F32),
             pltpu.VMEM((ROWS // WIDE, 2 * len(FAR), BLOCK, WIDE * BLOCK), BF16),
             pltpu.SemaphoreType.DMA((ROWS,)),
-            pltpu.SemaphoreType.DMA((8,)),
+            pltpu.SemaphoreType.DMA((10,)),
         ],
         compiler_params=limit(32),
         cost_estimate=cost(rows, 2 * len(FAR), 24),
-    )(cpat, outside(left), outside(partial), outside(fars))
+    )(cpat, outside(left), *opposite, outside(partial), outside(fars))
 
 
 def rescale_kernel(count, t_ref, i_ref, o_ref):
@@ -410,14 +414,17 @@
 
     line = jnp.concatenate([left] + [shift(left, s, 0) for s in (1, -1, 2)], axis=1)
     below, above = shift(line, 0, 1), shift(line, 0, -1)
-    lefts = [line, below, above, shift(below[:HALF], 0, 1), shift(above[HALF:], 0, -1)]
+    opposite = [shift(below[:HALF], 0, 1), shift(above[HALF:], 0, -1)]
+    lefts = [line, below, above]
     lefts = lefts + [swap(g) for g in lefts]
 
     nears = [near[0]] + [shift(piece, *step) for piece, step in zip(near[1:], steps[1:])]
     nears.append(swap(jnp.stack([piece[1] for piece in nears])))
 
     left, partial = first_product(lefts, nears)
-    inflated, totals = second_product(c_pattern, left, partial, fars)
+    opposite, partial = lax.optimization_barrier((opposite, partial))
+    opposite = opposite + [swap(g) for g in opposite]
+    inflated, totals = second_product(c_pattern, left, opposite, partial, fars)
     gathered = lax.all_to_all(totals, "row", split_axis=0, concat_axis=0, tiled=True)
     return rescale(gathered, inflated)
 

time: 149 us -> 148 us (level)
  local copies, waits for them, and re-layouts: 6.29 us -> 2.7 us
  waiting for transfers between devices: 48.3 us -> 50.5 us
    ppermute x6, waiting for transfers between devices: 2.54 us -> 8.93 us  [swap(): return lax.ppermute(value, 'col', [(i, i ^ 1) for i in range(COLS)])]
    ppermute x11, waiting for transfers between devices: 38 us -> 33.8 us  [shift(): return lax.ppermute(value, 'col', pairs)]
    unnamed x29 -> x35, local copies, waits for them, and re-layouts: 4.15 us -> 1.15 us
    ppermute x11, starting transfers between devices: 12.5 us -> 14.7 us  [shift(): return lax.ppermute(value, 'col', pairs)]
  transfers between devices with their start and end apart: 19 -> 19, of which waited for: 9 -> 12; matrix products, arithmetic and copies ran while one was open for 4% -> 2% of each run, Pallas kernels for 12% -> 12%
where the time goes in v5:
time: 148 us; the launch traced here: 146 us
  waiting for transfers between devices  50.5 us (34%)
  Pallas kernels  39.2 us (26%)
  starting transfers between devices  24 us (16%)
  blocking collectives  16.3 us (11%)
  between operations  13.7 us (9%)
  local copies, waits for them, and re-layouts  2.7 us (2%)
    ppermute x11, waiting for transfers between devices, shift(): return lax.ppermute(value, 'col', pairs)  33.8 us
    all_to_all x1, blocking collectives, shards(): lax.all_to_all(totals, 'row', split_axis=0, concat_axis=0, tiled=True)  16.3 us
    ppermute x11, starting transfers between devices, shift(): return lax.ppermute(value, 'col', pairs)  14.7 us
    pallas_call x1, Pallas kernels, second_product(): pl.pallas_call(second_kernel, out_shape=[pltpu.VMEM((rows, ROWS * BLOCK),...  13.9 us
    pallas_call x1, Pallas kernels, first_product(): pl.pallas_call(first_kernel, out_shape=[pltpu.HBM((rows, sources * BLOCK)...  12.2 us
    ppermute x6, waiting for transfers between devices, swap(): return lax.ppermute(value, 'col', [(i, i ^ 1) for i in range(COLS)])  8.93 us
    all_to_all x1, waiting for transfers between devices, shards(): lax.all_to_all(sent, 'col', split_axis=0, concat_axis=0, tiled=True)  7.68 us
    all_to_all x1, starting transfers between devices, shards(): lax.all_to_all(sent, 'col', split_axis=0, concat_axis=0, tiled=True)  7.54 us
  transfers between devices with their start and end apart: 19, of which 12 were waited for; matrix products, arithmetic and copies ran while one was open for 2% of the time, Pallas kernels for 12%

profile of v5, /device:TPU:8, one launch (start us, length us, event | category | flops | bytes accessed | tf_op | source)
XLA Modules:
  0.0 146.3 jit_solution(5826434556247176900)
XLA Ops:
  6.5 3.1 %shard_map.55 = bf16[32,128,128]{2,1,0:T(8,128)(2,1)} custom-call(s32[1]{0:T(128)} %bitcast.row_ref, s32[1,256]{1,0:T(1,128)} %pattern_ref.4, bf16[128,32768]{1,0:T(8,128)(2,1)} %b_ref.3), custom_call_target="tpu_custom_call" | custom-call | flops 1048576 | bytes 2097152 | tf_op jit(solution)/shard_map/pallas_call | solution.py:112
  9.7 7.5 %all-to-all-start = ((bf16[32,128,128]{2,1,0:T(8,128)(2,1)}), bf16[32,128,128]{2,1,0:T(8,128)(2,1)S(1)}, u32[]{:S(2)}, u32[]{:S(2)}) async-start(bf16[32,128,128]{2,1,0:T(8,128)(2,1)} %shard_map.55), calls=%async_computation | async-start | bytes 2097152 | tf_op jit(solution)/shard_map/all_to_all | solution.py:396
  17.3 0.0 all-gather.2.cloned.1.call-start
  17.3 0.7 copy.8.pattern_ref
  18.0 1.9 %shard_map.56 = bf16[1536,128]{1,0:T(8,128)(2,1)} custom-call(s32[12,1]{1,0:T(8,128)} %copy.8.pattern_ref, bf16[1536,128]{1,0:T(8,128)(2,1)} %a_ref.1), custom_call_target="tpu_custom_call" | custom-call | flops 196608 | bytes 786432 | tf_op jit(solution)/shard_map/pallas_call | solution.py:84
  19.8 0.7 stack.115.where_ref
  20.5 0.6 stack.138.index_ref
  21.2 3.9 %shard_map.57 = (bf16[2,128,1024]{2,1,0:T(8,128)(2,1)}, bf16[2,128,1024]{2,1,0:T(8,128)(2,1)}, bf16[2,128,1024]{2,1,0:T(8,128)(2,1)}, bf16[2,128,1024]{2,1,0:T(8,128)(2,1)}, bf16[2,128,1024]{2,1,0:T(8,128)(2,1)}) custom-call(s32[10]{0:T(128)} %stack.115.where_ref, s32[1,256]{1,0:T(1,128)} %pattern_ref.4, bf16[128,32768]{1,0:T(8,128)(2,1)} %b_ref.3), custom_call_target="tpu_custom_call" | custom-call | flops 4194304 | bytes 8388608 | tf_op jit(solution)/shard_map/pallas_call | solution.py:147
  25.1 7.7 %all-to-all-done.r_ref = bf16[32,128,128]{2,1,0:T(8,128)(2,1)S(1)} async-done(((bf16[32,128,128]{2,1,0:T(8,128)(2,1)}), bf16[32,128,128]{2,1,0:T(8,128)(2,1)S(1)}, u32[]{:S(2)}, u32[]{:S(2)}) %all-to-all-start) | async-done | bytes 1048608 | tf_op jit(solution)/shard_map/all_to_all | solution.py:396
  32.8 1.6 %shard_map.58 = bf16[22,128,128]{2,1,0:T(8,128)(2,1)} custom-call(s32[22]{0:T(128)} %stack.138.index_ref, bf16[32,128,128]{2,1,0:T(8,128)(2,1)S(1)} %all-to-all-done.r_ref), custom_call_target="tpu_custom_call" | custom-call | bytes 2097152 | tf_op jit(solution)/shard_map/pallas_call | solution.py:168
  34.5 0.4 collective-permute-start
  34.9 2.9 %collective-permute-start.1 = (bf16[1536,128]{1,0:T(8,128)(2,1)S(1)}, bf16[1536,128]{1,0:T(8,128)(2,1)S(1)}, u32[]{:S(2)}, u32[]{:S(2)}) collective-permute-start(bf16[1536,128]{1,0:T(8,128)(2,1)S(1)} %copy-done), channel_id=1, source_target_pairs={{0,24},{1,7},{2,26},{3,1},{4,28},{5,3},{6,30},{7,5},{8,0},{9,15},{... | collective-permute-start | bytes 1179656 | tf_op jit(solution)/shard_map/ppermute | solution.py:41
  37.8 0.9 collective-permute-start.8
  38.7 0.1 constant_dynamic-update-slice_fusion.3
  38.7 9.0 %collective-permute-done = bf16[1536,128]{1,0:T(8,128)(2,1)S(1)} collective-permute-done((bf16[1536,128]{1,0:T(8,128)(2,1)S(1)}, bf16[1536,128]{1,0:T(8,128)(2,1)S(1)}, u32[]{:S(2)}, u32[]{:S(2)}) %collective-permute-start) | collective-permute-done | bytes 393248 | tf_op jit(solution)/shard_map/ppermute | solution.py:41
  47.8 0.1 constant_dynamic-update-slice_fusion.2
  47.9 0.1 constant_dynamic-update-slice_fusion.1
  48.0 0.1 constant_dynamic-update-slice_fusion.refs_0_
  48.1 1.3 collective-permute-start.3
  49.4 0.8 collective-permute-start.4
  50.2 3.1 %collective-permute-start.9 = (bf16[2,128,1024]{2,1,0:T(8,128)(2,1)S(1)}, bf16[2,128,1024]{2,1,0:T(8,128)(2,1)S(1)}, u32[]{:S(2)}, u32[]{:S(2)}) collective-permute-start(bf16[2,128,1024]{2,1,0:T(8,128)(2,1)S(1)} %copy-done.11), channel_id=1, source_target_pairs={{0,24},{1,7},{2,26},{3,1},{4,28},{5,3},{6,30},{7,5},{8,0},{9,15},{... | collective-permute-start | bytes 1572872 | tf_op jit(solution)/shard_map/ppermute | solution.py:41
  53.3 1.2 collective-permute-start.10
  54.6 0.5 collective-permute-done.8.refs_7_
  55.1 1.6 %collective-permute-start.11 = (bf16[2,128,1024]{2,1,0:T(8,128)(2,1)S(1)}, bf16[2,128,1024]{2,1,0:T(8,128)(2,1)S(1)}, u32[]{:S(2)}, u32[]{:S(2)}) collective-permute-start(bf16[2,128,1024]{2,1,0:T(8,128)(2,1)S(1)} %copy-done.9), channel_id=1, source_target_pairs={{0,6},{1,25},{2,0},{3,27},{4,2},{5,29},{6,4},{7,31},{8,14},{9,1},{... | collective-permute-start | bytes 1572872 | tf_op jit(solution)/shard_map/ppermute | solution.py:41
  56.7 9.0 %collective-permute-done.9.refs_8_ = bf16[2,128,1024]{2,1,0:T(8,128)(2,1)S(1)} collective-permute-done((bf16[2,128,1024]{2,1,0:T(8,128)(2,1)S(1)}, bf16[2,128,1024]{2,1,0:T(8,128)(2,1)S(1)}, u32[]{:S(2)}, u32[]{:S(2)}) %collective-permute-start.9) | collective-permute-done | bytes 524320 | tf_op jit(solution)/shard_map/ppermute | solution.py:41
  65.7 8.5 %collective-permute-done.10.refs_9_ = bf16[2,128,1024]{2,1,0:T(8,128)(2,1)S(1)} collective-permute-done((bf16[2,128,1024]{2,1,0:T(8,128)(2,1)S(1)}, bf16[2,128,1024]{2,1,0:T(8,128)(2,1)S(1)}, u32[]{:S(2)}, u32[]{:S(2)}) %collective-permute-start.10) | collective-permute-done | bytes 524320 | tf_op jit(solution)/shard_map/ppermute | solution.py:41
  74.2 6.8 %collective-permute-done.11.refs_10_ = bf16[2,128,1024]{2,1,0:T(8,128)(2,1)S(1)} collective-permute-done((bf16[2,128,1024]{2,1,0:T(8,128)(2,1)S(1)}, bf16[2,128,1024]{2,1,0:T(8,128)(2,1)S(1)}, u32[]{:S(2)}, u32[]{:S(2)}) %collective-permute-start.11) | collective-permute-done | bytes 524320 | tf_op jit(solution)/shard_map/ppermute | solution.py:41
  81.1 0.1 collective-permute-start.12
  81.2 0.5 collective-permute-start.5
  81.7 0.1 collective-permute-start.6
  81.8 0.4 collective-permute-start.7
  82.2 0.1 slice.32
  82.2 1.4 collective-permute-start.13
  83.7 0.1 slice.33
  83.8 0.4 collective-permute-done.12.refs_11_
  84.2 1.0 collective-permute-start.14
  85.2 1.2 collective-permute-done.5.refs_3_
  86.4 2.2 %collective-permute-done.6.refs_4_ = bf16[1536,512]{1,0:T(8,128)(2,1)S(1)} collective-permute-done((bf16[1536,512]{1,0:T(8,128)(2,1)S(1)}, bf16[1536,512]{1,0:T(8,128)(2,1)S(1)}, u32[]{:S(2)}, u32[]{:S(2)}) %collective-permute-start.6) | collective-permute-done | bytes 1572896 | tf_op jit(solution)/shard_map/ppermute | solution.py:45
  88.7 2.2 %collective-permute-done.7.refs_5_ = bf16[1536,512]{1,0:T(8,128)(2,1)S(1)} collective-permute-done((bf16[1536,512]{1,0:T(8,128)(2,1)S(1)}, bf16[1536,512]{1,0:T(8,128)(2,1)S(1)}, u32[]{:S(2)}, u32[]{:S(2)}) %collective-permute-start.7) | collective-permute-done | bytes 1572896 | tf_op jit(solution)/shard_map/ppermute | solution.py:45
  90.9 12.2 %shard_map.59 = (bf16[1536,1792]{1,0:T(8,128)(2,1)}, f32[1536,1024]{1,0:T(8,128)}) custom-call(bf16[1536,512]{1,0:T(8,128)(2,1)S(1)} %constant_dynamic-update-slice_fusion.refs_0_, bf16[1536,512]{1,0:T(8,128)(2,1)S(1)} %collective-permute-done.3.refs_1_, bf16[1536,512]{1,0:T(8,128)(2,1)S(1)} %collective-permute-done.4.refs_2_, ...), custom_call_target="tpu_custom_call" | custom-call | flops 4026531840 | bytes 33554432 | tf_op jit(solution)/shard_map/pallas_call | solution.py:324
  103.2 0.2 collective-permute-start.15
  103.4 0.4 collective-permute-start.16
  103.8 0.1 copy.9.cpat_ref
  103.9 1.7 %collective-permute-done.15.u1 = bf16[768,512]{1,0:T(8,128)(2,1)S(1)} collective-permute-done((bf16[768,512]{1,0:T(8,128)(2,1)S(1)}, bf16[768,512]{1,0:T(8,128)(2,1)S(1)}, u32[]{:S(2)}, u32[]{:S(2)}) %collective-permute-start.15) | collective-permute-done | bytes 786464 | tf_op jit(solution)/shard_map/ppermute | solution.py:45
  105.6 1.1 collective-permute-done.16.l1
  106.7 13.9 %shard_map.60 = (f32[1536,1024]{1,0:T(8,128)S(1)}, f32[8,8,128]{2,1,0:T(8,128)S(1)}) custom-call(s32[12,8]{1,0:T(8,128)S(1)} %copy.9.cpat_ref, bf16[1536,1792]{1,0:T(8,128)(2,1)} %get-tuple-element.48.left_in, bf16[768,512]{1,0:T(8,128)(2,1)S(1)} %collective-permute-done.13.u0, bf16[768,512]{1,0:T(8,128)(2,1)S(1)} %collective-permute-done.14.l0, ...), custom_call_target="tpu_custom_call" | custom-call | flops 8858370048 | bytes 25165824 | tf_op jit(solution)/shard_map/pallas_call | solution.py:345
  120.6 16.3 %all_to_all.10.t_ref = f32[8,8,128]{2,1,0:T(8,128)S(1)} all-to-all(f32[8,8,128]{2,1,0:T(8,128)S(1)} %get-tuple-element.53), channel_id=1, replica_groups=mesh['row'=8,'col'=32] {'row'}, dimensions={0} | all-to-all | bytes 65536 | tf_op jit(solution)/shard_map/all_to_all | solution.py:428
  136.9 2.5 %shard_map.61 = bf16[1536,1024]{1,0:T(8,128)(2,1)} custom-call(f32[8,8,128]{2,1,0:T(8,128)S(1)} %all_to_all.10.t_ref, f32[1536,1024]{1,0:T(8,128)S(1)} %get-tuple-element.54.i_ref), custom_call_target="tpu_custom_call" | custom-call | flops 3145728 | bytes 4194304 | tf_op jit(solution)/shard_map/pallas_call | solution.py:379
  (40 shorter events, 0.2 us)
Async XLA Ops:
  9.7 7.6 %copy-start.7 = (s32[12,1]{0,1:T(1,128)S(1)}, s32[12,1]{0,1:T(1,128)}, u32[]{:S(2)}) copy-start(s32[12,1]{0,1:T(1,128)} %param.7) | copy-start | bytes 148
  9.7 23.1 %all-to-all-start = ((bf16[32,128,128]{2,1,0:T(8,128)(2,1)}), bf16[32,128,128]{2,1,0:T(8,128)(2,1)S(1)}, u32[]{:S(2)}, u32[]{:S(2)}) async-start(bf16[32,128,128]{2,1,0:T(8,128)(2,1)} %shard_map.55), calls=%async_computation | async-start | bytes 2097152 | tf_op jit(solution)/shard_map/all_to_all | solution.py:396
  17.3 89.4 %all-gather.2.cloned.1.call-start = ((), (), s32[]{:S(2)}) async-start(), calls=%async_computation.2 | async-start | bytes 6488064 | tf_op jit(solution)/shard_map/all_gather | solution.py:413
  25.1 9.3 %copy-start = (bf16[1536,128]{1,0:T(8,128)(2,1)S(1)}, bf16[1536,128]{1,0:T(8,128)(2,1)}, u32[]{:S(2)}) copy-start(bf16[1536,128]{1,0:T(8,128)(2,1)} %shard_map.56) | copy-start | bytes 1179652
  25.1 12.7 %copy-start.12 = (bf16[2,128,1024]{2,1,0:T(8,128)(2,1)S(1)}, bf16[2,128,1024]{2,1,0:T(8,128)(2,1)}, u32[]{:S(2)}) copy-start(bf16[2,128,1024]{2,1,0:T(8,128)(2,1)} %get-tuple-element.44) | copy-start | bytes 1572868
  34.4 15.7 %copy-start.11 = (bf16[2,128,1024]{2,1,0:T(8,128)(2,1)S(1)}, bf16[2,128,1024]{2,1,0:T(8,128)(2,1)}, u32[]{:S(2)}) copy-start(bf16[2,128,1024]{2,1,0:T(8,128)(2,1)} %get-tuple-element.45) | copy-start | bytes 1572868
  34.5 18.9 %copy-start.10 = (bf16[2,128,1024]{2,1,0:T(8,128)(2,1)S(1)}, bf16[2,128,1024]{2,1,0:T(8,128)(2,1)}, u32[]{:S(2)}) copy-start(bf16[2,128,1024]{2,1,0:T(8,128)(2,1)} %get-tuple-element.46) | copy-start | bytes 1572868
  34.5 20.1 %copy-start.1 = (bf16[2,128,1024]{2,1,0:T(8,128)(2,1)S(1)}, bf16[2,128,1024]{2,1,0:T(8,128)(2,1)}, u32[]{:S(2)}) copy-start(bf16[2,128,1024]{2,1,0:T(8,128)(2,1)} %get-tuple-element.43.refs_6_) | copy-start | bytes 1572868
  34.5 13.3 %collective-permute-start = (bf16[1536,128]{1,0:T(8,128)(2,1)S(1)}, bf16[1536,128]{1,0:T(8,128)(2,1)S(1)}, u32[]{:S(2)}, u32[]{:S(2)}) collective-permute-start(bf16[1536,128]{1,0:T(8,128)(2,1)S(1)} %copy-done), channel_id=1, source_target_pairs={{0,8},{1,3},{2,10},{3,5},{4,12},{5,7},{6,14},{7,1},{8,16},{9,11},{... | collective-permute-start | bytes 1179656 | tf_op jit(solution)/shard_map/ppermute | solution.py:41
  34.9 12.9 %collective-permute-start.1 = (bf16[1536,128]{1,0:T(8,128)(2,1)S(1)}, bf16[1536,128]{1,0:T(8,128)(2,1)S(1)}, u32[]{:S(2)}, u32[]{:S(2)}) collective-permute-start(bf16[1536,128]{1,0:T(8,128)(2,1)S(1)} %copy-done), channel_id=1, source_target_pairs={{0,24},{1,7},{2,26},{3,1},{4,28},{5,3},{6,30},{7,5},{8,0},{9,15},{... | collective-permute-start | bytes 1179656 | tf_op jit(solution)/shard_map/ppermute | solution.py:41
  37.8 10.2 %collective-permute-start.2 = (bf16[1536,128]{1,0:T(8,128)(2,1)S(1)}, bf16[1536,128]{1,0:T(8,128)(2,1)S(1)}, u32[]{:S(2)}, u32[]{:S(2)}) collective-permute-start(bf16[1536,128]{1,0:T(8,128)(2,1)S(1)} %copy-done), channel_id=1, source_target_pairs={{0,16},{1,5},{2,18},{3,7},{4,20},{5,1},{6,22},{7,3},{8,24},{9,13},... | collective-permute-start | bytes 1179656 | tf_op jit(solution)/shard_map/ppermute | solution.py:41
  37.8 17.3 %collective-permute-start.8 = (bf16[2,128,1024]{2,1,0:T(8,128)(2,1)S(1)}, bf16[2,128,1024]{2,1,0:T(8,128)(2,1)S(1)}, u32[]{:S(2)}, u32[]{:S(2)}) collective-permute-start(bf16[2,128,1024]{2,1,0:T(8,128)(2,1)S(1)} %copy-done.12), channel_id=1, source_target_pairs={{0,8},{1,3},{2,10},{3,5},{4,12},{5,7},{6,14},{7,1},{8,16},{9,11},{... | collective-permute-start | bytes 1572872 | tf_op jit(solution)/shard_map/ppermute | solution.py:41
  38.7 16.4 %copy-start.9 = (bf16[2,128,1024]{2,1,0:T(8,128)(2,1)S(1)}, bf16[2,128,1024]{2,1,0:T(8,128)(2,1)}, u32[]{:S(2)}) copy-start(bf16[2,128,1024]{2,1,0:T(8,128)(2,1)} %get-tuple-element.47) | copy-start | bytes 1572868
  48.1 33.6 %collective-permute-start.3 = (bf16[1536,512]{1,0:T(8,128)(2,1)S(1)}, bf16[1536,512]{1,0:T(8,128)(2,1)S(1)}, u32[]{:S(2)}, u32[]{:S(2)}) collective-permute-start(bf16[1536,512]{1,0:T(8,128)(2,1)S(1)} %constant_dynamic-update-slice_fusion.refs_0_), channel_id=1, source_target_pairs={{0,2},{1,9},{2,4},{3,11},{4,6},{5,13},{6,0},{7,15},{8,10},{9,17},{... | collective-permute-start | bytes 4718600 | tf_op jit(solution)/shard_map/ppermute | solution.py:41
  49.4 32.4 %collective-permute-start.4 = (bf16[1536,512]{1,0:T(8,128)(2,1)S(1)}, bf16[1536,512]{1,0:T(8,128)(2,1)S(1)}, u32[]{:S(2)}, u32[]{:S(2)}) collective-permute-start(bf16[1536,512]{1,0:T(8,128)(2,1)S(1)} %constant_dynamic-update-slice_fusion.refs_0_), channel_id=1, source_target_pairs={{0,6},{1,25},{2,0},{3,27},{4,2},{5,29},{6,4},{7,31},{8,14},{9,1},{... | collective-permute-start | bytes 4718600 | tf_op jit(solution)/shard_map/ppermute | solution.py:41
  50.2 15.5 %collective-permute-start.9 = (bf16[2,128,1024]{2,1,0:T(8,128)(2,1)S(1)}, bf16[2,128,1024]{2,1,0:T(8,128)(2,1)S(1)}, u32[]{:S(2)}, u32[]{:S(2)}) collective-permute-start(bf16[2,128,1024]{2,1,0:T(8,128)(2,1)S(1)} %copy-done.11), channel_id=1, source_target_pairs={{0,24},{1,7},{2,26},{3,1},{4,28},{5,3},{6,30},{7,5},{8,0},{9,15},{... | collective-permute-start | bytes 1572872 | tf_op jit(solution)/shard_map/ppermute | solution.py:41
  53.3 20.9 %collective-permute-start.10 = (bf16[2,128,1024]{2,1,0:T(8,128)(2,1)S(1)}, bf16[2,128,1024]{2,1,0:T(8,128)(2,1)S(1)}, u32[]{:S(2)}, u32[]{:S(2)}) collective-permute-start(bf16[2,128,1024]{2,1,0:T(8,128)(2,1)S(1)} %copy-done.10), channel_id=1, source_target_pairs={{0,2},{1,9},{2,4},{3,11},{4,6},{5,13},{6,0},{7,15},{8,10},{9,17},{... | collective-permute-start | bytes 1572872 | tf_op jit(solution)/shard_map/ppermute | solution.py:41
  55.1 27.1 %copy-start.2 = (bf16[2,128,1024]{2,1,0:T(8,128)(2,1)}, bf16[2,128,1024]{2,1,0:T(8,128)(2,1)S(1)}, u32[]{:S(2)}) copy-start(bf16[2,128,1024]{2,1,0:T(8,128)(2,1)S(1)} %collective-permute-done.8.refs_7_) | copy-start | bytes 1572868
  55.1 25.9 %collective-permute-start.11 = (bf16[2,128,1024]{2,1,0:T(8,128)(2,1)S(1)}, bf16[2,128,1024]{2,1,0:T(8,128)(2,1)S(1)}, u32[]{:S(2)}, u32[]{:S(2)}) collective-permute-start(bf16[2,128,1024]{2,1,0:T(8,128)(2,1)S(1)} %copy-done.9), channel_id=1, source_target_pairs={{0,6},{1,25},{2,0},{3,27},{4,2},{5,29},{6,4},{7,31},{8,14},{9,1},{... | collective-permute-start | bytes 1572872 | tf_op jit(solution)/shard_map/ppermute | solution.py:41
  65.7 16.5 %copy-start.3 = (bf16[2,128,1024]{2,1,0:T(8,128)(2,1)}, bf16[2,128,1024]{2,1,0:T(8,128)(2,1)S(1)}, u32[]{:S(2)}) copy-start(bf16[2,128,1024]{2,1,0:T(8,128)(2,1)S(1)} %collective-permute-done.9.refs_8_) | copy-start | bytes 1572868
  74.2 9.6 %copy-start.4 = (bf16[2,128,1024]{2,1,0:T(8,128)(2,1)}, bf16[2,128,1024]{2,1,0:T(8,128)(2,1)S(1)}, u32[]{:S(2)}) copy-start(bf16[2,128,1024]{2,1,0:T(8,128)(2,1)S(1)} %collective-permute-done.10.refs_9_) | copy-start | bytes 1572868
  81.0 2.7 %copy-start.5 = (bf16[2,128,1024]{2,1,0:T(8,128)(2,1)}, bf16[2,128,1024]{2,1,0:T(8,128)(2,1)S(1)}, u32[]{:S(2)}) copy-start(bf16[2,128,1024]{2,1,0:T(8,128)(2,1)S(1)} %collective-permute-done.11.refs_10_) | copy-start | bytes 1572868
  81.1 3.1 %collective-permute-start.12 = (bf16[5,128,1024]{2,1,0:T(8,128)(2,1)S(1)}, bf16[5,128,1024]{2,1,0:T(8,128)(2,1)S(1)}, u32[]{:S(2)}, u32[]{:S(2)}) collective-permute-start(bf16[5,128,1024]{2,1,0:T(8,128)(2,1)S(1)} %slice_dynamic-update-slice_fusion), channel_id=1, source_target_pairs={{0,1},{1,0},{2,3},{3,2},{4,5},{5,4},{6,7},{7,6},{8,9},{9,8},{10,11... | collective-permute-start | bytes 3932168 | tf_op jit(solution)/shard_map/ppermute | solution.py:45
  81.2 5.3 %collective-permute-start.5 = (bf16[1536,512]{1,0:T(8,128)(2,1)S(1)}, bf16[1536,512]{1,0:T(8,128)(2,1)S(1)}, u32[]{:S(2)}, u32[]{:S(2)}) collective-permute-start(bf16[1536,512]{1,0:T(8,128)(2,1)S(1)} %constant_dynamic-update-slice_fusion.refs_0_), channel_id=1, source_target_pairs={{0,1},{1,0},{2,3},{3,2},{4,5},{5,4},{6,7},{7,6},{8,9},{9,8},{10,11... | collective-permute-start | bytes 4718600 | tf_op jit(solution)/shard_map/ppermute | solution.py:45
  81.7 7.0 %collective-permute-start.6 = (bf16[1536,512]{1,0:T(8,128)(2,1)S(1)}, bf16[1536,512]{1,0:T(8,128)(2,1)S(1)}, u32[]{:S(2)}, u32[]{:S(2)}) collective-permute-start(bf16[1536,512]{1,0:T(8,128)(2,1)S(1)} %collective-permute-done.3.refs_1_), channel_id=1, source_target_pairs={{0,1},{1,0},{2,3},{3,2},{4,5},{5,4},{6,7},{7,6},{8,9},{9,8},{10,11... | collective-permute-start | bytes 4718600 | tf_op jit(solution)/shard_map/ppermute | solution.py:45
  81.8 9.2 %collective-permute-start.7 = (bf16[1536,512]{1,0:T(8,128)(2,1)S(1)}, bf16[1536,512]{1,0:T(8,128)(2,1)S(1)}, u32[]{:S(2)}, u32[]{:S(2)}) collective-permute-start(bf16[1536,512]{1,0:T(8,128)(2,1)S(1)} %collective-permute-done.4.refs_2_), channel_id=1, source_target_pairs={{0,1},{1,0},{2,3},{3,2},{4,5},{5,4},{6,7},{7,6},{8,9},{9,8},{10,11... | collective-permute-start | bytes 4718600 | tf_op jit(solution)/shard_map/ppermute | solution.py:45
  82.2 20.9 %collective-permute-start.13 = (bf16[768,512]{1,0:T(8,128)(2,1)S(1)}, bf16[768,512]{1,0:T(8,128)(2,1)S(1)}, u32[]{:S(2)}, u32[]{:S(2)}) collective-permute-start(bf16[768,512]{1,0:T(8,128)(2,1)S(1)} %slice.32), channel_id=1, source_target_pairs={{0,2},{1,9},{2,4},{3,11},{4,6},{5,13},{6,0},{7,15},{8,10},{9,17},{... | collective-permute-start | bytes 2359304 | tf_op jit(solution)/shard_map/ppermute | solution.py:41
  83.8 20.0 %copy-start.6 = (s32[12,8]{0,1:T(8,128)S(1)}, s32[12,8]{0,1:T(8,128)}, u32[]{:S(2)}) copy-start(s32[12,8]{0,1:T(8,128)} %param.9) | copy-start | bytes 1156
  84.2 6.8 %copy-start.8 = (bf16[5,128,1024]{2,1,0:T(8,128)(2,1)}, bf16[5,128,1024]{2,1,0:T(8,128)(2,1)S(1)}, u32[]{:S(2)}) copy-start(bf16[5,128,1024]{2,1,0:T(8,128)(2,1)S(1)} %collective-permute-done.12.refs_11_) | copy-start | bytes 3932164
  84.2 19.0 %collective-permute-start.14 = (bf16[768,512]{1,0:T(8,128)(2,1)S(1)}, bf16[768,512]{1,0:T(8,128)(2,1)S(1)}, u32[]{:S(2)}, u32[]{:S(2)}) collective-permute-start(bf16[768,512]{1,0:T(8,128)(2,1)S(1)} %slice.33), channel_id=1, source_target_pairs={{0,6},{1,25},{2,0},{3,27},{4,2},{5,29},{6,4},{7,31},{8,14},{9,1},{... | collective-permute-start | bytes 2359304 | tf_op jit(solution)/shard_map/ppermute | solution.py:41
  103.2 2.4 %collective-permute-start.15 = (bf16[768,512]{1,0:T(8,128)(2,1)S(1)}, bf16[768,512]{1,0:T(8,128)(2,1)S(1)}, u32[]{:S(2)}, u32[]{:S(2)}) collective-permute-start(bf16[768,512]{1,0:T(8,128)(2,1)S(1)} %collective-permute-done.13.u0), channel_id=1, source_target_pairs={{0,1},{1,0},{2,3},{3,2},{4,5},{5,4},{6,7},{7,6},{8,9},{9,8},{10,11... | collective-permute-start | bytes 2359304 | tf_op jit(solution)/shard_map/ppermute | solution.py:45
  103.4 3.3 %collective-permute-start.16 = (bf16[768,512]{1,0:T(8,128)(2,1)S(1)}, bf16[768,512]{1,0:T(8,128)(2,1)S(1)}, u32[]{:S(2)}, u32[]{:S(2)}) collective-permute-start(bf16[768,512]{1,0:T(8,128)(2,1)S(1)} %collective-permute-done.14.l0), channel_id=1, source_target_pairs={{0,1},{1,0},{2,3},{3,2},{4,5},{5,4},{6,7},{7,6},{8,9},{9,8},{10,11... | collective-permute-start | bytes 2359304 | tf_op jit(solution)/shard_map/ppermute | solution.py:45
Sparse Core Ops, SparseCore 0:
  34.6 70.2 all-gather.1

commit v6 on v5

--- a/solution.py
+++ b/solution.py
@@ -176,7 +176,7 @@
 
 
 HALF = 768
-CHUNK = 384
+CHUNK = 256
 CHUNKS = ((0, HALF), (HALF, HALF))
 WIDE = 4
 
@@ -332,8 +332,8 @@
             pltpu.VMEM((2 * len(NEAR), BLOCK, ROWS * BLOCK), BF16),
             pltpu.VMEM((2, CHUNK, ROWS * BLOCK), F32),
             pltpu.SemaphoreType.DMA((len(nears),)),
-            pltpu.SemaphoreType.DMA((32,)),
-            pltpu.SemaphoreType.DMA((8,)),
+            pltpu.SemaphoreType.DMA((36,)),
+            pltpu.SemaphoreType.DMA((12,)),
         ],
         compiler_params=limit(24),
         cost_estimate=cost(rows, 2 * len(NEAR), 32),

time: 148 us -> 146 us (0.986)
  Pallas kernels: 39.2 us -> 37.1 us
    pallas_call x1, Pallas kernels: 12.2 us -> 10.1 us  [first_product(): pl.pallas_call(first_kernel, out_shape=[pltpu.HBM((rows, sources * BLOCK)...]
  transfers between devices with their start and end apart: 19 -> 19, of which waited for: 12 -> 13; matrix products, arithmetic and copies ran while one was open for 2% -> 2% of each run, Pallas kernels for 12% -> 11%
where the time goes in v6:
time: 146 us; the launch traced here: 144 us
  waiting for transfers between devices  50.7 us (35%)
  Pallas kernels  37.1 us (25%)
  starting transfers between devices  24 us (16%)
  blocking collectives  16.1 us (11%)
  between operations  13.7 us (9%)
  local copies, waits for them, and re-layouts  2.7 us (2%)
    ppermute x11, waiting for transfers between devices, shift(): return lax.ppermute(value, 'col', pairs)  33.8 us
    all_to_all x1, blocking collectives, shards(): lax.all_to_all(totals, 'row', split_axis=0, concat_axis=0, tiled=True)  16.1 us
    ppermute x11, starting transfers between devices, shift(): return lax.ppermute(value, 'col', pairs)  14.7 us
    pallas_call x1, Pallas kernels, second_product(): pl.pallas_call(second_kernel, out_shape=[pltpu.VMEM((rows, ROWS * BLOCK),...  13.9 us
    pallas_call x1, Pallas kernels, first_product(): pl.pallas_call(first_kernel, out_shape=[pltpu.HBM((rows, sources * BLOCK)...  10.1 us
    ppermute x6, waiting for transfers between devices, swap(): return lax.ppermute(value, 'col', [(i, i ^ 1) for i in range(COLS)])  8.93 us
    all_to_all x1, waiting for transfers between devices, shards(): lax.all_to_all(sent, 'col', split_axis=0, concat_axis=0, tiled=True)  7.68 us
    all_to_all x1, starting transfers between devices, shards(): lax.all_to_all(sent, 'col', split_axis=0, concat_axis=0, tiled=True)  7.54 us
  transfers between devices with their start and end apart: 19, of which 13 were waited for; matrix products, arithmetic and copies ran while one was open for 2% of the time, Pallas kernels for 11%

profile of v6, /device:TPU:8, one launch (start us, length us, event | category | flops | bytes accessed | tf_op | source)
XLA Modules:
  0.0 144.2 jit_solution(705812962640491897)
XLA Ops:
  6.5 3.1 %shard_map.55 = bf16[32,128,128]{2,1,0:T(8,128)(2,1)} custom-call(s32[1]{0:T(128)} %bitcast.row_ref, s32[1,256]{1,0:T(1,128)} %pattern_ref.4, bf16[128,32768]{1,0:T(8,128)(2,1)} %b_ref.3), custom_call_target="tpu_custom_call" | custom-call | flops 1048576 | bytes 2097152 | tf_op jit(solution)/shard_map/pallas_call | solution.py:112
  9.7 7.5 %all-to-all-start = ((bf16[32,128,128]{2,1,0:T(8,128)(2,1)}), bf16[32,128,128]{2,1,0:T(8,128)(2,1)S(1)}, u32[]{:S(2)}, u32[]{:S(2)}) async-start(bf16[32,128,128]{2,1,0:T(8,128)(2,1)} %shard_map.55), calls=%async_computation | async-start | bytes 2097152 | tf_op jit(solution)/shard_map/all_to_all | solution.py:396
  17.3 0.7 copy.8.pattern_ref
  18.0 1.9 %shard_map.56 = bf16[1536,128]{1,0:T(8,128)(2,1)} custom-call(s32[12,1]{1,0:T(8,128)} %copy.8.pattern_ref, bf16[1536,128]{1,0:T(8,128)(2,1)} %a_ref.1), custom_call_target="tpu_custom_call" | custom-call | flops 196608 | bytes 786432 | tf_op jit(solution)/shard_map/pallas_call | solution.py:84
  19.8 0.7 stack.115.where_ref
  20.5 0.6 stack.138.index_ref
  21.2 3.9 %shard_map.57 = (bf16[2,128,1024]{2,1,0:T(8,128)(2,1)}, bf16[2,128,1024]{2,1,0:T(8,128)(2,1)}, bf16[2,128,1024]{2,1,0:T(8,128)(2,1)}, bf16[2,128,1024]{2,1,0:T(8,128)(2,1)}, bf16[2,128,1024]{2,1,0:T(8,128)(2,1)}) custom-call(s32[10]{0:T(128)} %stack.115.where_ref, s32[1,256]{1,0:T(1,128)} %pattern_ref.4, bf16[128,32768]{1,0:T(8,128)(2,1)} %b_ref.3), custom_call_target="tpu_custom_call" | custom-call | flops 4194304 | bytes 8388608 | tf_op jit(solution)/shard_map/pallas_call | solution.py:147
  25.1 7.7 %all-to-all-done.r_ref = bf16[32,128,128]{2,1,0:T(8,128)(2,1)S(1)} async-done(((bf16[32,128,128]{2,1,0:T(8,128)(2,1)}), bf16[32,128,128]{2,1,0:T(8,128)(2,1)S(1)}, u32[]{:S(2)}, u32[]{:S(2)}) %all-to-all-start) | async-done | bytes 1048608 | tf_op jit(solution)/shard_map/all_to_all | solution.py:396
  32.8 1.6 %shard_map.58 = bf16[22,128,128]{2,1,0:T(8,128)(2,1)} custom-call(s32[22]{0:T(128)} %stack.138.index_ref, bf16[32,128,128]{2,1,0:T(8,128)(2,1)S(1)} %all-to-all-done.r_ref), custom_call_target="tpu_custom_call" | custom-call | bytes 2097152 | tf_op jit(solution)/shard_map/pallas_call | solution.py:168
  34.5 0.4 collective-permute-start
  34.9 2.9 %collective-permute-start.1 = (bf16[1536,128]{1,0:T(8,128)(2,1)S(1)}, bf16[1536,128]{1,0:T(8,128)(2,1)S(1)}, u32[]{:S(2)}, u32[]{:S(2)}) collective-permute-start(bf16[1536,128]{1,0:T(8,128)(2,1)S(1)} %copy-done), channel_id=1, source_target_pairs={{0,24},{1,7},{2,26},{3,1},{4,28},{5,3},{6,30},{7,5},{8,0},{9,15},{... | collective-permute-start | bytes 1179656 | tf_op jit(solution)/shard_map/ppermute | solution.py:41
  37.8 0.9 collective-permute-start.8
  38.7 0.1 constant_dynamic-update-slice_fusion.3
  38.7 9.0 %collective-permute-done = bf16[1536,128]{1,0:T(8,128)(2,1)S(1)} collective-permute-done((bf16[1536,128]{1,0:T(8,128)(2,1)S(1)}, bf16[1536,128]{1,0:T(8,128)(2,1)S(1)}, u32[]{:S(2)}, u32[]{:S(2)}) %collective-permute-start) | collective-permute-done | bytes 393248 | tf_op jit(solution)/shard_map/ppermute | solution.py:41
  47.8 0.1 constant_dynamic-update-slice_fusion.2
  47.9 0.1 constant_dynamic-update-slice_fusion.1
  48.0 0.1 constant_dynamic-update-slice_fusion.refs_0_
  48.1 1.3 collective-permute-start.3
  49.4 0.8 collective-permute-start.4
  50.2 3.1 %collective-permute-start.9 = (bf16[2,128,1024]{2,1,0:T(8,128)(2,1)S(1)}, bf16[2,128,1024]{2,1,0:T(8,128)(2,1)S(1)}, u32[]{:S(2)}, u32[]{:S(2)}) collective-permute-start(bf16[2,128,1024]{2,1,0:T(8,128)(2,1)S(1)} %copy-done.11), channel_id=1, source_target_pairs={{0,24},{1,7},{2,26},{3,1},{4,28},{5,3},{6,30},{7,5},{8,0},{9,15},{... | collective-permute-start | bytes 1572872 | tf_op jit(solution)/shard_map/ppermute | solution.py:41
  53.3 1.2 collective-permute-start.10
  54.6 0.5 collective-permute-done.8.refs_7_
  55.1 1.6 %collective-permute-start.11 = (bf16[2,128,1024]{2,1,0:T(8,128)(2,1)S(1)}, bf16[2,128,1024]{2,1,0:T(8,128)(2,1)S(1)}, u32[]{:S(2)}, u32[]{:S(2)}) collective-permute-start(bf16[2,128,1024]{2,1,0:T(8,128)(2,1)S(1)} %copy-done.9), channel_id=1, source_target_pairs={{0,6},{1,25},{2,0},{3,27},{4,2},{5,29},{6,4},{7,31},{8,14},{9,1},{... | collective-permute-start | bytes 1572872 | tf_op jit(solution)/shard_map/ppermute | solution.py:41
  56.7 9.0 %collective-permute-done.9.refs_8_ = bf16[2,128,1024]{2,1,0:T(8,128)(2,1)S(1)} collective-permute-done((bf16[2,128,1024]{2,1,0:T(8,128)(2,1)S(1)}, bf16[2,128,1024]{2,1,0:T(8,128)(2,1)S(1)}, u32[]{:S(2)}, u32[]{:S(2)}) %collective-permute-start.9) | collective-permute-done | bytes 524320 | tf_op jit(solution)/shard_map/ppermute | solution.py:41
  65.7 8.5 %collective-permute-done.10.refs_9_ = bf16[2,128,1024]{2,1,0:T(8,128)(2,1)S(1)} collective-permute-done((bf16[2,128,1024]{2,1,0:T(8,128)(2,1)S(1)}, bf16[2,128,1024]{2,1,0:T(8,128)(2,1)S(1)}, u32[]{:S(2)}, u32[]{:S(2)}) %collective-permute-start.10) | collective-permute-done | bytes 524320 | tf_op jit(solution)/shard_map/ppermute | solution.py:41
  74.2 6.8 %collective-permute-done.11.refs_10_ = bf16[2,128,1024]{2,1,0:T(8,128)(2,1)S(1)} collective-permute-done((bf16[2,128,1024]{2,1,0:T(8,128)(2,1)S(1)}, bf16[2,128,1024]{2,1,0:T(8,128)(2,1)S(1)}, u32[]{:S(2)}, u32[]{:S(2)}) %collective-permute-start.11) | collective-permute-done | bytes 524320 | tf_op jit(solution)/shard_map/ppermute | solution.py:41
  81.1 0.1 collective-permute-start.12
  81.2 0.5 collective-permute-start.5
  81.7 0.1 collective-permute-start.6
  81.8 0.4 collective-permute-start.7
  82.2 0.1 slice.32
  82.2 1.4 collective-permute-start.13
  83.7 0.1 slice.33
  83.8 0.4 collective-permute-done.12.refs_11_
  84.2 1.0 collective-permute-start.14
  85.2 1.2 collective-permute-done.5.refs_3_
  86.4 2.2 %collective-permute-done.6.refs_4_ = bf16[1536,512]{1,0:T(8,128)(2,1)S(1)} collective-permute-done((bf16[1536,512]{1,0:T(8,128)(2,1)S(1)}, bf16[1536,512]{1,0:T(8,128)(2,1)S(1)}, u32[]{:S(2)}, u32[]{:S(2)}) %collective-permute-start.6) | collective-permute-done | bytes 1572896 | tf_op jit(solution)/shard_map/ppermute | solution.py:45
  88.7 2.2 %collective-permute-done.7.refs_5_ = bf16[1536,512]{1,0:T(8,128)(2,1)S(1)} collective-permute-done((bf16[1536,512]{1,0:T(8,128)(2,1)S(1)}, bf16[1536,512]{1,0:T(8,128)(2,1)S(1)}, u32[]{:S(2)}, u32[]{:S(2)}) %collective-permute-start.7) | collective-permute-done | bytes 1572896 | tf_op jit(solution)/shard_map/ppermute | solution.py:45
  90.9 10.1 %shard_map.59 = (bf16[1536,1792]{1,0:T(8,128)(2,1)}, f32[1536,1024]{1,0:T(8,128)}) custom-call(bf16[1536,512]{1,0:T(8,128)(2,1)S(1)} %constant_dynamic-update-slice_fusion.refs_0_, bf16[1536,512]{1,0:T(8,128)(2,1)S(1)} %collective-permute-done.3.refs_1_, bf16[1536,512]{1,0:T(8,128)(2,1)S(1)} %collective-permute-done.4.refs_2_, ...), custom_call_target="tpu_custom_call" | custom-call | flops 4026531840 | bytes 33554432 | tf_op jit(solution)/shard_map/pallas_call | solution.py:324
  101.1 0.2 collective-permute-start.15
  101.3 0.4 collective-permute-start.16
  101.7 0.1 copy.9.cpat_ref
  101.8 1.7 %collective-permute-done.15.u1 = bf16[768,512]{1,0:T(8,128)(2,1)S(1)} collective-permute-done((bf16[768,512]{1,0:T(8,128)(2,1)S(1)}, bf16[768,512]{1,0:T(8,128)(2,1)S(1)}, u32[]{:S(2)}, u32[]{:S(2)}) %collective-permute-start.15) | collective-permute-done | bytes 786464 | tf_op jit(solution)/shard_map/ppermute | solution.py:45
  103.5 1.1 collective-permute-done.16.l1
  104.6 0.2 all-gather.2.cloned.1.call-done.fars
  104.8 13.9 %shard_map.60 = (f32[1536,1024]{1,0:T(8,128)S(1)}, f32[8,8,128]{2,1,0:T(8,128)S(1)}) custom-call(s32[12,8]{1,0:T(8,128)S(1)} %copy.9.cpat_ref, bf16[1536,1792]{1,0:T(8,128)(2,1)} %get-tuple-element.48.left_in, bf16[768,512]{1,0:T(8,128)(2,1)S(1)} %collective-permute-done.13.u0, bf16[768,512]{1,0:T(8,128)(2,1)S(1)} %collective-permute-done.14.l0, ...), custom_call_target="tpu_custom_call" | custom-call | flops 8858370048 | bytes 25165824 | tf_op jit(solution)/shard_map/pallas_call | solution.py:345
  118.7 16.1 %all_to_all.10.t_ref = f32[8,8,128]{2,1,0:T(8,128)S(1)} all-to-all(f32[8,8,128]{2,1,0:T(8,128)S(1)} %get-tuple-element.53), channel_id=1, replica_groups=mesh['row'=8,'col'=32] {'row'}, dimensions={0} | all-to-all | bytes 65536 | tf_op jit(solution)/shard_map/all_to_all | solution.py:428
  134.8 2.5 %shard_map.61 = bf16[1536,1024]{1,0:T(8,128)(2,1)} custom-call(f32[8,8,128]{2,1,0:T(8,128)S(1)} %all_to_all.10.t_ref, f32[1536,1024]{1,0:T(8,128)S(1)} %get-tuple-element.54.i_ref), custom_call_target="tpu_custom_call" | custom-call | flops 3145728 | bytes 4194304 | tf_op jit(solution)/shard_map/pallas_call | solution.py:379
  (40 shorter events, 0.2 us)
Async XLA Ops:
  9.7 7.6 %copy-start.7 = (s32[12,1]{0,1:T(1,128)S(1)}, s32[12,1]{0,1:T(1,128)}, u32[]{:S(2)}) copy-start(s32[12,1]{0,1:T(1,128)} %param.7) | copy-start | bytes 148
  9.7 23.1 %all-to-all-start = ((bf16[32,128,128]{2,1,0:T(8,128)(2,1)}), bf16[32,128,128]{2,1,0:T(8,128)(2,1)S(1)}, u32[]{:S(2)}, u32[]{:S(2)}) async-start(bf16[32,128,128]{2,1,0:T(8,128)(2,1)} %shard_map.55), calls=%async_computation | async-start | bytes 2097152 | tf_op jit(solution)/shard_map/all_to_all | solution.py:396
  17.3 87.6 %all-gather.2.cloned.1.call-start = ((), (), s32[]{:S(2)}) async-start(), calls=%async_computation.2 | async-start | bytes 6488064 | tf_op jit(solution)/shard_map/all_gather | solution.py:413
  25.1 9.3 %copy-start = (bf16[1536,128]{1,0:T(8,128)(2,1)S(1)}, bf16[1536,128]{1,0:T(8,128)(2,1)}, u32[]{:S(2)}) copy-start(bf16[1536,128]{1,0:T(8,128)(2,1)} %shard_map.56) | copy-start | bytes 1179652
  25.1 12.7 %copy-start.12 = (bf16[2,128,1024]{2,1,0:T(8,128)(2,1)S(1)}, bf16[2,128,1024]{2,1,0:T(8,128)(2,1)}, u32[]{:S(2)}) copy-start(bf16[2,128,1024]{2,1,0:T(8,128)(2,1)} %get-tuple-element.44) | copy-start | bytes 1572868
  34.4 15.7 %copy-start.11 = (bf16[2,128,1024]{2,1,0:T(8,128)(2,1)S(1)}, bf16[2,128,1024]{2,1,0:T(8,128)(2,1)}, u32[]{:S(2)}) copy-start(bf16[2,128,1024]{2,1,0:T(8,128)(2,1)} %get-tuple-element.45) | copy-start | bytes 1572868
  34.5 18.9 %copy-start.10 = (bf16[2,128,1024]{2,1,0:T(8,128)(2,1)S(1)}, bf16[2,128,1024]{2,1,0:T(8,128)(2,1)}, u32[]{:S(2)}) copy-start(bf16[2,128,1024]{2,1,0:T(8,128)(2,1)} %get-tuple-element.46) | copy-start | bytes 1572868
  34.5 20.1 %copy-start.1 = (bf16[2,128,1024]{2,1,0:T(8,128)(2,1)S(1)}, bf16[2,128,1024]{2,1,0:T(8,128)(2,1)}, u32[]{:S(2)}) copy-start(bf16[2,128,1024]{2,1,0:T(8,128)(2,1)} %get-tuple-element.43.refs_6_) | copy-start | bytes 1572868
  34.5 13.3 %collective-permute-start = (bf16[1536,128]{1,0:T(8,128)(2,1)S(1)}, bf16[1536,128]{1,0:T(8,128)(2,1)S(1)}, u32[]{:S(2)}, u32[]{:S(2)}) collective-permute-start(bf16[1536,128]{1,0:T(8,128)(2,1)S(1)} %copy-done), channel_id=1, source_target_pairs={{0,8},{1,3},{2,10},{3,5},{4,12},{5,7},{6,14},{7,1},{8,16},{9,11},{... | collective-permute-start | bytes 1179656 | tf_op jit(solution)/shard_map/ppermute | solution.py:41
  34.9 12.9 %collective-permute-start.1 = (bf16[1536,128]{1,0:T(8,128)(2,1)S(1)}, bf16[1536,128]{1,0:T(8,128)(2,1)S(1)}, u32[]{:S(2)}, u32[]{:S(2)}) collective-permute-start(bf16[1536,128]{1,0:T(8,128)(2,1)S(1)} %copy-done), channel_id=1, source_target_pairs={{0,24},{1,7},{2,26},{3,1},{4,28},{5,3},{6,30},{7,5},{8,0},{9,15},{... | collective-permute-start | bytes 1179656 | tf_op jit(solution)/shard_map/ppermute | solution.py:41
  37.8 10.2 %collective-permute-start.2 = (bf16[1536,128]{1,0:T(8,128)(2,1)S(1)}, bf16[1536,128]{1,0:T(8,128)(2,1)S(1)}, u32[]{:S(2)}, u32[]{:S(2)}) collective-permute-start(bf16[1536,128]{1,0:T(8,128)(2,1)S(1)} %copy-done), channel_id=1, source_target_pairs={{0,16},{1,5},{2,18},{3,7},{4,20},{5,1},{6,22},{7,3},{8,24},{9,13},... | collective-permute-start | bytes 1179656 | tf_op jit(solution)/shard_map/ppermute | solution.py:41
  37.8 17.3 %collective-permute-start.8 = (bf16[2,128,1024]{2,1,0:T(8,128)(2,1)S(1)}, bf16[2,128,1024]{2,1,0:T(8,128)(2,1)S(1)}, u32[]{:S(2)}, u32[]{:S(2)}) collective-permute-start(bf16[2,128,1024]{2,1,0:T(8,128)(2,1)S(1)} %copy-done.12), channel_id=1, source_target_pairs={{0,8},{1,3},{2,10},{3,5},{4,12},{5,7},{6,14},{7,1},{8,16},{9,11},{... | collective-permute-start | bytes 1572872 | tf_op jit(solution)/shard_map/ppermute | solution.py:41
  38.7 16.4 %copy-start.9 = (bf16[2,128,1024]{2,1,0:T(8,128)(2,1)S(1)}, bf16[2,128,1024]{2,1,0:T(8,128)(2,1)}, u32[]{:S(2)}) copy-start(bf16[2,128,1024]{2,1,0:T(8,128)(2,1)} %get-tuple-element.47) | copy-start | bytes 1572868
  48.1 33.6 %collective-permute-start.3 = (bf16[1536,512]{1,0:T(8,128)(2,1)S(1)}, bf16[1536,512]{1,0:T(8,128)(2,1)S(1)}, u32[]{:S(2)}, u32[]{:S(2)}) collective-permute-start(bf16[1536,512]{1,0:T(8,128)(2,1)S(1)} %constant_dynamic-update-slice_fusion.refs_0_), channel_id=1, source_target_pairs={{0,2},{1,9},{2,4},{3,11},{4,6},{5,13},{6,0},{7,15},{8,10},{9,17},{... | collective-permute-start | bytes 4718600 | tf_op jit(solution)/shard_map/ppermute | solution.py:41
  49.4 32.4 %collective-permute-start.4 = (bf16[1536,512]{1,0:T(8,128)(2,1)S(1)}, bf16[1536,512]{1,0:T(8,128)(2,1)S(1)}, u32[]{:S(2)}, u32[]{:S(2)}) collective-permute-start(bf16[1536,512]{1,0:T(8,128)(2,1)S(1)} %constant_dynamic-update-slice_fusion.refs_0_), channel_id=1, source_target_pairs={{0,6},{1,25},{2,0},{3,27},{4,2},{5,29},{6,4},{7,31},{8,14},{9,1},{... | collective-permute-start | bytes 4718600 | tf_op jit(solution)/shard_map/ppermute | solution.py:41
  50.2 15.5 %collective-permute-start.9 = (bf16[2,128,1024]{2,1,0:T(8,128)(2,1)S(1)}, bf16[2,128,1024]{2,1,0:T(8,128)(2,1)S(1)}, u32[]{:S(2)}, u32[]{:S(2)}) collective-permute-start(bf16[2,128,1024]{2,1,0:T(8,128)(2,1)S(1)} %copy-done.11), channel_id=1, source_target_pairs={{0,24},{1,7},{2,26},{3,1},{4,28},{5,3},{6,30},{7,5},{8,0},{9,15},{... | collective-permute-start | bytes 1572872 | tf_op jit(solution)/shard_map/ppermute | solution.py:41
  53.3 20.9 %collective-permute-start.10 = (bf16[2,128,1024]{2,1,0:T(8,128)(2,1)S(1)}, bf16[2,128,1024]{2,1,0:T(8,128)(2,1)S(1)}, u32[]{:S(2)}, u32[]{:S(2)}) collective-permute-start(bf16[2,128,1024]{2,1,0:T(8,128)(2,1)S(1)} %copy-done.10), channel_id=1, source_target_pairs={{0,2},{1,9},{2,4},{3,11},{4,6},{5,13},{6,0},{7,15},{8,10},{9,17},{... | collective-permute-start | bytes 1572872 | tf_op jit(solution)/shard_map/ppermute | solution.py:41
  55.1 27.1 %copy-start.2 = (bf16[2,128,1024]{2,1,0:T(8,128)(2,1)}, bf16[2,128,1024]{2,1,0:T(8,128)(2,1)S(1)}, u32[]{:S(2)}) copy-start(bf16[2,128,1024]{2,1,0:T(8,128)(2,1)S(1)} %collective-permute-done.8.refs_7_) | copy-start | bytes 1572868
  55.1 25.9 %collective-permute-start.11 = (bf16[2,128,1024]{2,1,0:T(8,128)(2,1)S(1)}, bf16[2,128,1024]{2,1,0:T(8,128)(2,1)S(1)}, u32[]{:S(2)}, u32[]{:S(2)}) collective-permute-start(bf16[2,128,1024]{2,1,0:T(8,128)(2,1)S(1)} %copy-done.9), channel_id=1, source_target_pairs={{0,6},{1,25},{2,0},{3,27},{4,2},{5,29},{6,4},{7,31},{8,14},{9,1},{... | collective-permute-start | bytes 1572872 | tf_op jit(solution)/shard_map/ppermute | solution.py:41
  65.7 16.5 %copy-start.3 = (bf16[2,128,1024]{2,1,0:T(8,128)(2,1)}, bf16[2,128,1024]{2,1,0:T(8,128)(2,1)S(1)}, u32[]{:S(2)}) copy-start(bf16[2,128,1024]{2,1,0:T(8,128)(2,1)S(1)} %collective-permute-done.9.refs_8_) | copy-start | bytes 1572868
  74.2 9.6 %copy-start.4 = (bf16[2,128,1024]{2,1,0:T(8,128)(2,1)}, bf16[2,128,1024]{2,1,0:T(8,128)(2,1)S(1)}, u32[]{:S(2)}) copy-start(bf16[2,128,1024]{2,1,0:T(8,128)(2,1)S(1)} %collective-permute-done.10.refs_9_) | copy-start | bytes 1572868
  81.0 2.7 %copy-start.5 = (bf16[2,128,1024]{2,1,0:T(8,128)(2,1)}, bf16[2,128,1024]{2,1,0:T(8,128)(2,1)S(1)}, u32[]{:S(2)}) copy-start(bf16[2,128,1024]{2,1,0:T(8,128)(2,1)S(1)} %collective-permute-done.11.refs_10_) | copy-start | bytes 1572868
  81.1 3.1 %collective-permute-start.12 = (bf16[5,128,1024]{2,1,0:T(8,128)(2,1)S(1)}, bf16[5,128,1024]{2,1,0:T(8,128)(2,1)S(1)}, u32[]{:S(2)}, u32[]{:S(2)}) collective-permute-start(bf16[5,128,1024]{2,1,0:T(8,128)(2,1)S(1)} %slice_dynamic-update-slice_fusion), channel_id=1, source_target_pairs={{0,1},{1,0},{2,3},{3,2},{4,5},{5,4},{6,7},{7,6},{8,9},{9,8},{10,11... | collective-permute-start | bytes 3932168 | tf_op jit(solution)/shard_map/ppermute | solution.py:45
  81.2 5.3 %collective-permute-start.5 = (bf16[1536,512]{1,0:T(8,128)(2,1)S(1)}, bf16[1536,512]{1,0:T(8,128)(2,1)S(1)}, u32[]{:S(2)}, u32[]{:S(2)}) collective-permute-start(bf16[1536,512]{1,0:T(8,128)(2,1)S(1)} %constant_dynamic-update-slice_fusion.refs_0_), channel_id=1, source_target_pairs={{0,1},{1,0},{2,3},{3,2},{4,5},{5,4},{6,7},{7,6},{8,9},{9,8},{10,11... | collective-permute-start | bytes 4718600 | tf_op jit(solution)/shard_map/ppermute | solution.py:45
  81.7 7.0 %collective-permute-start.6 = (bf16[1536,512]{1,0:T(8,128)(2,1)S(1)}, bf16[1536,512]{1,0:T(8,128)(2,1)S(1)}, u32[]{:S(2)}, u32[]{:S(2)}) collective-permute-start(bf16[1536,512]{1,0:T(8,128)(2,1)S(1)} %collective-permute-done.3.refs_1_), channel_id=1, source_target_pairs={{0,1},{1,0},{2,3},{3,2},{4,5},{5,4},{6,7},{7,6},{8,9},{9,8},{10,11... | collective-permute-start | bytes 4718600 | tf_op jit(solution)/shard_map/ppermute | solution.py:45
  81.8 9.2 %collective-permute-start.7 = (bf16[1536,512]{1,0:T(8,128)(2,1)S(1)}, bf16[1536,512]{1,0:T(8,128)(2,1)S(1)}, u32[]{:S(2)}, u32[]{:S(2)}) collective-permute-start(bf16[1536,512]{1,0:T(8,128)(2,1)S(1)} %collective-permute-done.4.refs_2_), channel_id=1, source_target_pairs={{0,1},{1,0},{2,3},{3,2},{4,5},{5,4},{6,7},{7,6},{8,9},{9,8},{10,11... | collective-permute-start | bytes 4718600 | tf_op jit(solution)/shard_map/ppermute | solution.py:45
  82.2 18.8 %collective-permute-start.13 = (bf16[768,512]{1,0:T(8,128)(2,1)S(1)}, bf16[768,512]{1,0:T(8,128)(2,1)S(1)}, u32[]{:S(2)}, u32[]{:S(2)}) collective-permute-start(bf16[768,512]{1,0:T(8,128)(2,1)S(1)} %slice.32), channel_id=1, source_target_pairs={{0,2},{1,9},{2,4},{3,11},{4,6},{5,13},{6,0},{7,15},{8,10},{9,17},{... | collective-permute-start | bytes 2359304 | tf_op jit(solution)/shard_map/ppermute | solution.py:41
  83.8 17.9 %copy-start.6 = (s32[12,8]{0,1:T(8,128)S(1)}, s32[12,8]{0,1:T(8,128)}, u32[]{:S(2)}) copy-start(s32[12,8]{0,1:T(8,128)} %param.9) | copy-start | bytes 1156
  84.2 6.8 %copy-start.8 = (bf16[5,128,1024]{2,1,0:T(8,128)(2,1)}, bf16[5,128,1024]{2,1,0:T(8,128)(2,1)S(1)}, u32[]{:S(2)}) copy-start(bf16[5,128,1024]{2,1,0:T(8,128)(2,1)S(1)} %collective-permute-done.12.refs_11_) | copy-start | bytes 3932164
  84.2 16.9 %collective-permute-start.14 = (bf16[768,512]{1,0:T(8,128)(2,1)S(1)}, bf16[768,512]{1,0:T(8,128)(2,1)S(1)}, u32[]{:S(2)}, u32[]{:S(2)}) collective-permute-start(bf16[768,512]{1,0:T(8,128)(2,1)S(1)} %slice.33), channel_id=1, source_target_pairs={{0,6},{1,25},{2,0},{3,27},{4,2},{5,29},{6,4},{7,31},{8,14},{9,1},{... | collective-permute-start | bytes 2359304 | tf_op jit(solution)/shard_map/ppermute | solution.py:41
  101.1 2.4 %collective-permute-start.15 = (bf16[768,512]{1,0:T(8,128)(2,1)S(1)}, bf16[768,512]{1,0:T(8,128)(2,1)S(1)}, u32[]{:S(2)}, u32[]{:S(2)}) collective-permute-start(bf16[768,512]{1,0:T(8,128)(2,1)S(1)} %collective-permute-done.13.u0), channel_id=1, source_target_pairs={{0,1},{1,0},{2,3},{3,2},{4,5},{5,4},{6,7},{7,6},{8,9},{9,8},{10,11... | collective-permute-start | bytes 2359304 | tf_op jit(solution)/shard_map/ppermute | solution.py:45
  101.3 3.3 %collective-permute-start.16 = (bf16[768,512]{1,0:T(8,128)(2,1)S(1)}, bf16[768,512]{1,0:T(8,128)(2,1)S(1)}, u32[]{:S(2)}, u32[]{:S(2)}) collective-permute-start(bf16[768,512]{1,0:T(8,128)(2,1)S(1)} %collective-permute-done.14.l0), channel_id=1, source_target_pairs={{0,1},{1,0},{2,3},{3,2},{4,5},{5,4},{6,7},{7,6},{8,9},{9,8},{10,11... | collective-permute-start | bytes 2359304 | tf_op jit(solution)/shard_map/ppermute | solution.py:45
Sparse Core Ops, SparseCore 0:
  34.6 70.2 all-gather.1
